TPU v7x, 32 devices: a whole 2x2x4 slice. The times are simulated.
32 devices in a mesh: clip: 8 (over z, x), seq: 4 (over y, core).
Axes of the slice: x: 2, y: 2, z: 4, core: 2. Of those that a mesh axis runs over, the one named last changes fastest.
Arguments:
- tokens: bfloat16 [8, 2048, 768], P('clip', 'seq'), may hold values from -6 to 6
- out_grad: bfloat16 [8, 2048, 768], P('clip', 'seq'), may hold values from -6144 to 6144
- saved_logits: bfloat16 [8, 2048, 128], P('clip', 'seq'), may hold values from -14 to 400
- slot_params: bfloat16 [768, 128], P(None, 'seq'), may hold values from -0.21875 to 0.21875
- slot_inputs: bfloat16 [8, 128, 768], P(None, ('clip', 'seq')), may hold values from -6 to 6
- slot_outputs: bfloat16 [8, 128, 768], P('clip', 'seq'), may hold values from -0.119628906 to 0.119628906
- expert_in: bfloat16 [32, 768, 3072], P(('clip', 'seq')), may hold values from -0.21875 to 0.21875
- expert_out: bfloat16 [32, 3072, 768], P(('clip', 'seq')), may hold values from -0.109375 to 0.109375
Outputs:
- token_grad: bfloat16 [8, 2048, 768], P('clip', 'seq')
All inputs are finite; a program needn't handle non-finite values.
Results may differ from a plain program's by a relative error of at most 0.023.
Values may be sent and summed in bfloat16 or wider, within the bound.
No kernel may reach another device: no remote copies, remote signals or barrier semaphores. Data moves between devices by JAX's collectives and lax.ppermute only.
A program may use at most 64 MiB of HBM per device.

v0:
```python
import jax
import jax.numpy as jnp
from jax import lax
from jax.sharding import PartitionSpec as P


def combined_all(value, axis, join):
    pieces = jax.tree.map(lambda part: lax.all_gather(part, axis), value)
    head = jax.tree.map(lambda part: part[0], pieces)
    tail = jax.tree.map(lambda part: part[1:], pieces)
    total, _ = lax.scan(lambda total, piece: (join(total, piece), None), head, tail)
    return total


def merge_stats(first, second):
    highest = jnp.maximum(first[0], second[0])
    total = first[1] * jnp.exp(first[0] - highest) + second[1] * jnp.exp(second[0] - highest)
    return (highest, total)


def on_device(
    tokens, out_grad, saved_logits, slot_params, slot_inputs, slot_outputs, expert_in, expert_out
):
    clip_count = lax.axis_size("clip")
    seq_count = lax.axis_size("seq")
    tok_feats = tokens[0]
    out_cot = out_grad[0]
    scores = saved_logits[0].astype(jnp.float32)
    width = tok_feats.shape[1]
    slot_total = scores.shape[1]
    clip_total = slot_inputs.shape[0]
    local_slots = slot_inputs.shape[1]
    expert_block = expert_in.shape[0]
    slot_each = local_slots // expert_block
    param_all, outputs_all = (
        lax.all_gather(slot_params, "seq", axis=1, tiled=True),
        lax.all_gather(slot_outputs, "seq", axis=1, tiled=True),
    )
    slot_out = outputs_all[0]
    combine = jax.nn.softmax(scores, axis=1)
    local_max = jnp.max(scores, axis=0)
    local_sum = jnp.sum(jnp.exp(scores - local_max), axis=0)
    col_max, col_sum = combined_all((local_max, local_sum), "seq", merge_stats)
    dispatch = jnp.exp(scores - col_max) / col_sum
    comb_cot = jnp.einsum("td,sd->ts", out_cot, slot_out, preferred_element_type=jnp.float32)
    comb_logit = combine * (comb_cot - jnp.sum(combine * comb_cot, axis=1, keepdims=True))
    partial_cot = jnp.einsum(
        "ts,td->sd", combine.astype(jnp.bfloat16), out_cot, preferred_element_type=jnp.float32
    )
    blocks = partial_cot.reshape(clip_count, seq_count, local_slots, width)
    shares = lax.psum_scatter(
        blocks.astype(jnp.bfloat16), "seq", scatter_dimension=1, tiled=True
    ).astype(jnp.float32)
    received = lax.all_to_all(
        shares[:, 0].astype(jnp.bfloat16), "clip", split_axis=0, concat_axis=0, tiled=True
    )
    expert_cot = received.reshape(clip_total, expert_block, slot_each, width)
    expert_feed = slot_inputs.reshape(clip_total, expert_block, slot_each, width)
    hidden = jnp.einsum(
        "cejd,edh->cejh", expert_feed, expert_in, preferred_element_type=jnp.float32
    )
    act_cot = jnp.einsum(
        "cejd,ehd->cejh", expert_cot, expert_out, preferred_element_type=jnp.float32
    )
    unused, pull_back = jax.vjp(jax.nn.gelu, hidden)
    hidden_cot = pull_back(act_cot)[0].astype(jnp.bfloat16)
    local_grad = jnp.einsum(
        "cejh,edh->cejd", hidden_cot, expert_in, preferred_element_type=jnp.float32
    )
    local_grad = local_grad.astype(jnp.bfloat16)
    returned = lax.all_to_all(local_grad, "clip", split_axis=0, concat_axis=0, tiled=True)
    collected = lax.all_gather(returned, "seq", axis=1, tiled=True)
    slot_grad = collected.reshape(slot_total, width)
    dispatch_b = dispatch.astype(jnp.bfloat16)
    direct = jnp.dot(dispatch_b, slot_grad, preferred_element_type=jnp.float32)
    disp_cot = jnp.einsum("td,sd->ts", tok_feats, slot_grad, preferred_element_type=jnp.float32)
    slot_dots = lax.psum(jnp.sum(dispatch * disp_cot, axis=0), "seq")
    disp_logit = dispatch * (disp_cot - slot_dots)
    logit_grad = (comb_logit + disp_logit).astype(jnp.bfloat16)
    through = jnp.einsum("ts,ds->td", logit_grad, param_all, preferred_element_type=jnp.float32)
    return (direct + through).astype(jnp.bfloat16)[None]


def solution(mesh):
    placed = (
        P("clip", "seq", None),
        P("clip", "seq", None),
        P("clip", "seq", None),
        P(None, "seq"),
        P(None, ("clip", "seq"), None),
        P("clip", "seq", None),
        P(("clip", "seq"), None, None),
        P(("clip", "seq"), None, None),
    )
    return jax.shard_map(
        on_device, mesh=mesh, in_specs=placed, out_specs=P("clip", "seq", None), check_vma=False
    )
```

profile of v0, /device:TPU:0, one launch (start us, length us, event | category | flops | bytes accessed | tf_op | source)
XLA Modules:
  0.0 90.9 jit_solution(15180465009968826205)
XLA Ops:
  6.5 0.0 copy-start
  6.5 1.1 %fusion.85 = (bf16[128]{0:T(256)(128)(2,1)S(1)}, bf16[512]{0:T(512)(128)(2,1)S(1)}) fusion(bf16[1,512,128]{2,1,0:T(8,128)(2,1)} %param.12), kind=kLoop, calls=%fused_computation.85 | loop fusion | flops 130432 | bytes 132352 | tf_op jit(solution)/shard_map/reduce_max | solution.py:41
  7.6 1.0 %copy.16 = bf16[1,512,128]{1,2,0:T(8,128)(2,1)S(1)} copy(bf16[1,512,128]{2,1,0:T(8,128)(2,1)} %param.12) | data formatting | bytes 262144 | tf_op args[2]
  8.7 0.2 fusion.49
  8.9 0.1 convert_bitcast_fusion.1
  9.0 1.0 %convolution_convert_fusion = bf16[8,4,4,768]{3,0,2,1:T(8,128)(2,1)} fusion(bf16[1,512,768]{2,1,0:T(8,128)(2,1)S(1)} %copy-done, bf16[8,4,4,512]{3,2,1,0:T(4,128)(2,1)S(1)} %dot_general.37), kind=kOutput, calls=%fused_computation.17 | convolution fusion | flops 100761600 | bytes 1114112 | tf_op jit(solution)/shard_map/ts,td->sd/dot_general | solution.py:47
  10.0 0.0 reduce-scatter.2.cloned.1.call-update
  10.0 6.0 %all-gather.2 = f32[4,1,128]{2,1,0:T(1,128)S(1)} all-gather(f32[1,1,128]{2,1,0:T(1,128)S(1)} %get-tuple-element.53), channel_id=2, replica_groups=mesh['clip'=8,'seq'=4] {'seq'}, dimensions={0}, use_global_device_ids=true | all-gather | bytes 2560 | tf_op jit(solution)/shard_map/all_gather | solution.py:8
  16.0 5.3 %all-gather.3 = f32[4,1,128]{2,1,0:T(1,128)S(1)} all-gather(f32[1,1,128]{2,1,0:T(1,128)S(1)} %bitcast.147), channel_id=3, replica_groups=mesh['clip'=8,'seq'=4] {'seq'}, dimensions={0}, use_global_device_ids=true | all-gather | bytes 2560 | tf_op jit(solution)/shard_map/all_gather | solution.py:8
  21.3 0.1 while.12
  21.4 11.2 %reduce-scatter.2.cloned.1.call-done = bf16[8,1,4,768]{3,0,2,1:T(8,128)(2,1)} async-done(((bf16[8,4,4,768]{3,0,2,1:T(8,128)(2,1)}), bf16[8,1,4,768]{3,0,2,1:T(8,128)(2,1)}) %reduce-scatter.2.cloned.1.call-update) | async-done | bytes 49168 | tf_op jit(solution)/shard_map/reduce_scatter | solution.py:51
  32.6 1.4 %copy.18 = bf16[8,4,768]{2,1,0:T(4,128)(2,1)} copy(bf16[8,4,768]{2,0,1:T(8,128)(2,1)} %bitcast.144) | data formatting | bytes 98304 | tf_op jit(solution)/shard_map/convert_element_type | solution.py:55
  34.0 5.5 %all-to-all-start = ((bf16[8,4,768]{2,1,0:T(4,128)(2,1)}), bf16[8,4,768]{2,1,0:T(4,128)(2,1)S(1)}, u32[]{:S(2)}, u32[]{:S(2)}) async-start(bf16[8,4,768]{2,1,0:T(4,128)(2,1)} %copy.18), calls=%async_computation.1 | async-start | bytes 98304 | tf_op jit(solution)/shard_map/all_to_all | solution.py:54
  39.5 3.2 %fusion.14 = f32[8,1,4,3072]{3,0,2,1:T(8,128)S(1)} fusion(bf16[1,768,3072]{2,1,0:T(8,128)(2,1)} %param.16, bf16[8,4,768]{2,1,0:T(4,128)(2,1)} %param.14), kind=kOutput, calls=%fused_computation.14 | convolution fusion | flops 150994944 | bytes 5160960 | tf_op jit(solution)/shard_map/cejd,edh->cejh/dot_general | solution.py:59
  42.8 0.0 copy-start.2
  42.8 0.0 copy-start.3
  42.8 0.0 copy-start.1
  42.8 3.5 %all-to-all-done = bf16[8,4,768]{2,1,0:T(4,128)(2,1)S(1)} async-done(((bf16[8,4,768]{2,1,0:T(4,128)(2,1)}), bf16[8,4,768]{2,1,0:T(4,128)(2,1)S(1)}, u32[]{:S(2)}, u32[]{:S(2)}) %all-to-all-start) | async-done | bytes 49184 | tf_op jit(solution)/shard_map/all_to_all | solution.py:54
  46.3 6.6 %fusion.21 = bf16[8,1,4,768]{3,0,2,1:T(8,128)(2,1)S(1)} fusion(bf16[1,768,3072]{2,1,0:T(8,128)(2,1)} %param.16, f32[8,1,4,3072]{3,0,2,1:T(8,128)S(1)} %fusion.14, bf16[1,3072,768]{2,1,0:T(8,128)(2,1)} %param.17, bf16[8,4,768]{2,1,0:T(4,128)(2,1)S(1)} %all-to-all-done), kind=kOutput, calls=%fused_computation.20 | convolution fusion | flops 303980544 | bytes 9928704 | tf_op jit(solution)/shard_map/cejh,edh->cejd/dot_general | solution.py:67
  52.9 0.6 copy.21
  53.5 3.3 %all-to-all-start.1 = ((bf16[8,1,4,768]{3,2,1,0:T(4,128)(2,1)}), bf16[8,1,4,768]{3,2,1,0:T(4,128)(2,1)S(1)}, u32[]{:S(2)}, u32[]{:S(2)}) async-start(bf16[8,1,4,768]{3,2,1,0:T(4,128)(2,1)} %copy.21), calls=%async_computation.2 | async-start | bytes 98304 | tf_op jit(solution)/shard_map/all_to_all | solution.py:71
  56.9 5.6 %all_gather.24 = bf16[768,128]{0,1:T(8,128)(2,1)S(1)} all-gather(bf16[768,32]{0,1:T(8,128)(2,1)S(1)} %copy-done.2), channel_id=1, replica_groups=mesh['clip'=8,'seq'=4] {'seq'}, dimensions={1}, use_global_device_ids=true | all-gather | bytes 245760 | tf_op jit(solution)/shard_map/all_gather | solution.py:36
  62.5 6.0 %all_gather.23 = bf16[1,128,768]{2,1,0:T(8,128)(2,1)} all-gather(bf16[1,32,768]{2,1,0:T(8,128)(2,1)S(1)} %copy-done.3), channel_id=1, replica_groups=mesh['clip'=8,'seq'=4] {'seq'}, dimensions={1}, use_global_device_ids=true | all-gather | bytes 245760 | tf_op jit(solution)/shard_map/all_gather | solution.py:37
  68.6 0.0 all-to-all-done.1
  68.6 5.6 %all_gather.22 = bf16[8,4,4,768]{3,0,2,1:T(8,128)(2,1)S(1)} all-gather(bf16[8,1,4,768]{3,0,2,1:T(8,128)(2,1)S(1)} %copy.22), channel_id=1, replica_groups=mesh['clip'=8,'seq'=4] {'seq'}, dimensions={1}, use_global_device_ids=true | all-gather | bytes 245760 | tf_op jit(solution)/shard_map/all_gather | solution.py:72
  74.2 0.1 copy.23
  74.3 0.1 reshape.61
  74.3 0.4 convolution_bitcast_fusion
  74.7 0.5 fusion.66
  75.2 1.3 %multiply_reduce_fusion.1 = (f32[512]{0:T(512)S(1)}, f32[128]{0:T(128)S(1)}, f32[512,128]{0,1:T(8,128)S(1)}) fusion(f32[512]{0:T(512)S(1)} %get-tuple-element.38, f32[512]{0:T(512)S(1)} %reduce_max.37, bf16[1,512,128]{1,2,0:T(8,128)(2,1)S(1)} %copy.16, f32[512,128]{0,1:T(8,128)S(1)} %convolution_bitcast_fusion, f32[128]{0:T(128)S(1)} %get-tuple-element.34, ...), kind=kOutput, calls=%fused_computation.54 | convolution fusion | flops 101252480 | bytes 1646080 | tf_op jit(solution)/shard_map/td,sd->ts/dot_general | solution.py:45
  76.6 6.1 %psum.7 = f32[128]{0:T(128)S(1)} all-reduce(f32[128]{0:T(128)S(1)} %get-tuple-element.36), channel_id=1, replica_groups=mesh['clip'=8,'seq'=4] {'seq'}, use_global_device_ids=true, to_apply=%region_9.10 | all-reduce | flops 128 | bytes 1024 | tf_op jit(solution)/shard_map/psum | solution.py:77
  82.7 1.4 %fusion.17 = bf16[1,512,768]{2,1,0:T(8,128)(2,1)} fusion(f32[512,768]{1,0:T(8,128)S(1)} %fusion.66, bf16[768,128]{0,1:T(8,128)(2,1)S(1)} %all_gather.24, f32[512,128]{0,1:T(8,128)S(1)} %convolution_bitcast_fusion, f32[512,128]{0,1:T(8,128)S(1)} %get-tuple-element.55, bf16[1,512,128]{1,2,0:T(8,128)(2,1)S(1)} %copy.16, f32[128]{0:T(128)S(1)} %psum.7, ...), kind=kOutput, calls=%fused_computation.16 | convolution fusion | flops 102170624 | bytes 3218944 | tf_op jit(solution)/shard_map/ts,ds->td/dot_general | solution.py:80
  (18 shorter events, 0.2 us)
Async XLA Ops:
  6.5 2.4 %copy-start = (bf16[1,512,768]{2,1,0:T(8,128)(2,1)S(1)}, bf16[1,512,768]{2,1,0:T(8,128)(2,1)}, u32[]{:S(2)}) copy-start(bf16[1,512,768]{2,1,0:T(8,128)(2,1)} %param.11) | copy-start | bytes 2359300
  6.5 26.0 %reduce-scatter.2.cloned.1.call-start = ((), (), s32[]{:S(2)}) async-start(), calls=%async_computation.3 | async-start | bytes 245760 | tf_op jit(solution)/shard_map/reduce_scatter | solution.py:51
  34.0 12.3 %all-to-all-start = ((bf16[8,4,768]{2,1,0:T(4,128)(2,1)}), bf16[8,4,768]{2,1,0:T(4,128)(2,1)S(1)}, u32[]{:S(2)}, u32[]{:S(2)}) async-start(bf16[8,4,768]{2,1,0:T(4,128)(2,1)} %copy.18), calls=%async_computation.1 | async-start | bytes 98304 | tf_op jit(solution)/shard_map/all_to_all | solution.py:54
  42.8 14.1 %copy-start.2 = (bf16[768,32]{0,1:T(8,128)(2,1)S(1)}, bf16[768,32]{0,1:T(8,128)(2,1)}, u32[]{:S(2)}) copy-start(bf16[768,32]{0,1:T(8,128)(2,1)} %param.13) | copy-start | bytes 147460
  42.8 19.8 %copy-start.3 = (bf16[1,32,768]{2,1,0:T(8,128)(2,1)S(1)}, bf16[1,32,768]{2,1,0:T(8,128)(2,1)}, u32[]{:S(2)}) copy-start(bf16[1,32,768]{2,1,0:T(8,128)(2,1)} %param.15) | copy-start | bytes 147460
  42.8 31.5 %copy-start.1 = (bf16[1,512,768]{2,1,0:T(8,128)(2,1)S(1)}, bf16[1,512,768]{2,1,0:T(8,128)(2,1)}, u32[]{:S(2)}) copy-start(bf16[1,512,768]{2,1,0:T(8,128)(2,1)} %param.10) | copy-start | bytes 2359300
  53.5 15.0 %all-to-all-start.1 = ((bf16[8,1,4,768]{3,2,1,0:T(4,128)(2,1)}), bf16[8,1,4,768]{3,2,1,0:T(4,128)(2,1)S(1)}, u32[]{:S(2)}, u32[]{:S(2)}) async-start(bf16[8,1,4,768]{3,2,1,0:T(4,128)(2,1)} %copy.21), calls=%async_computation.2 | async-start | bytes 98304 | tf_op jit(solution)/shard_map/all_to_all | solution.py:71
Sparse Core Ops, SparseCore 0:
  10.1 22.4 reduce-scatter.1
where the time goes:
time: 91.4 us; the launch traced here: 90.9 us
  blocking collectives  34.7 us (38%)
  waiting for transfers between devices  14.7 us (16%)
  matrix products  14.4 us (16%)
  between operations  13.5 us (15%)
  starting transfers between devices  8.86 us (10%)
  local copies, waits for them, and re-layouts  3.3 us (4%)
  other arithmetic  1.43 us (2%)
    all_gather x2, blocking collectives, combined_all(): pieces = jax.tree.map(lambda part: lax.all_gather(part, axis), value)  11.3 us
    reduce_scatter x1, waiting for transfers between devices, on_device(): lax.psum_scatter(blocks.astype(jnp.bfloat16), 'seq', scatter_dimension=1,...  11.2 us
    dot_general x1, matrix products, on_device(): jnp.einsum('cejh,edh->cejd', hidden_cot, expert_in, preferred_element_typ...  6.57 us
    psum x1, blocking collectives, on_device(): slot_dots = lax.psum(jnp.sum(dispatch * disp_cot, axis=0), 'seq')  6.14 us
    all_gather x1, blocking collectives, on_device(): lax.all_gather(slot_outputs, 'seq', axis=1, tiled=True)  6.04 us
    all_gather x1, blocking collectives, on_device(): lax.all_gather(slot_params, 'seq', axis=1, tiled=True)  5.61 us
    all_gather x1, blocking collectives, on_device(): collected = lax.all_gather(returned, 'seq', axis=1, tiled=True)  5.61 us
    all_to_all x1, starting transfers between devices, on_device(): lax.all_to_all(shares[:, 0].astype(jnp.bfloat16), 'clip', split_axis=0, c...  5.52 us
  transfers between devices with their start and end apart: 3, of which 2 were waited for; matrix products, arithmetic and copies ran while one was open for 4% of the time, Pallas kernels for 0%

commit v1 on v0

v1 whole, which is shorter than its diff:
```python
import jax
import jax.numpy as jnp
from jax import lax
from jax.sharding import PartitionSpec as P

BOTH = ("clip", "seq")


def on_device(
    tokens, out_grad, saved_logits, slot_params, slot_inputs, slot_outputs, expert_in, expert_out
):
    clip_count = lax.axis_size("clip")
    seq_count = lax.axis_size("seq")
    tok_feats = tokens[0]
    out_cot = out_grad[0]
    scores = saved_logits[0].astype(jnp.float32)
    width = tok_feats.shape[1]
    slot_total = scores.shape[1]
    clip_total = slot_inputs.shape[0]
    local_slots = slot_inputs.shape[1]
    expert_block = expert_in.shape[0]
    slot_each = local_slots // expert_block
    combine = jax.nn.softmax(scores, axis=1)
    partial_cot = jnp.einsum(
        "ts,td->sd", combine.astype(jnp.bfloat16), out_cot, preferred_element_type=jnp.float32
    )
    blocks = partial_cot.astype(jnp.bfloat16).reshape(
        clip_count * seq_count, local_slots, width
    )
    received = lax.all_to_all(blocks, BOTH, split_axis=0, concat_axis=0, tiled=True)
    seq_slots = slot_params.shape[1]
    packed = jnp.concatenate([slot_params.T, slot_outputs[0]], axis=0)
    packed_all = lax.all_gather(packed, "seq", axis=0)
    param_all = packed_all[:, :seq_slots].reshape(slot_total, width)
    slot_out = packed_all[:, seq_slots:].reshape(slot_total, width)
    local_max = jnp.max(scores, axis=0)
    local_sum = jnp.sum(jnp.exp(scores - local_max), axis=0)
    stats = lax.all_gather(jnp.stack([local_max, local_sum]), "seq")
    col_max = jnp.max(stats[:, 0], axis=0)
    col_sum = jnp.sum(stats[:, 1] * jnp.exp(stats[:, 0] - col_max), axis=0)
    dispatch = jnp.exp(scores - col_max) / col_sum
    comb_cot = jnp.einsum("td,sd->ts", out_cot, slot_out, preferred_element_type=jnp.float32)
    comb_logit = combine * (comb_cot - jnp.sum(combine * comb_cot, axis=1, keepdims=True))
    expert_feed = slot_inputs.reshape(clip_total, expert_block, slot_each, width)
    hidden = jnp.einsum(
        "cejd,edh->cejh", expert_feed, expert_in, preferred_element_type=jnp.float32
    )
    expert_cot = received.reshape(clip_count, seq_count, expert_block, slot_each, width)
    expert_cot = jnp.sum(expert_cot.astype(jnp.float32), axis=1).astype(jnp.bfloat16)
    act_cot = jnp.einsum(
        "cejd,ehd->cejh", expert_cot, expert_out, preferred_element_type=jnp.float32
    )
    unused, pull_back = jax.vjp(jax.nn.gelu, hidden)
    hidden_cot = pull_back(act_cot)[0].astype(jnp.bfloat16)
    local_grad = jnp.einsum(
        "cejh,edh->cejd", hidden_cot, expert_in, preferred_element_type=jnp.float32
    ).astype(jnp.bfloat16)
    local_grad = local_grad.reshape(clip_count, 1, local_slots, width)
    copies = jnp.broadcast_to(local_grad, (clip_count, seq_count, local_slots, width))
    slot_grad = lax.all_to_all(
        copies.reshape(clip_count * seq_count, local_slots, width),
        BOTH,
        split_axis=0,
        concat_axis=0,
        tiled=True,
    ).reshape(slot_total, width)
    dispatch_b = dispatch.astype(jnp.bfloat16)
    direct = jnp.dot(dispatch_b, slot_grad, preferred_element_type=jnp.float32)
    disp_cot = jnp.einsum("td,sd->ts", tok_feats, slot_grad, preferred_element_type=jnp.float32)
    slot_dots = lax.psum(jnp.sum(dispatch * disp_cot, axis=0), "seq")
    disp_logit = dispatch * (disp_cot - slot_dots)
    logit_grad = (comb_logit + disp_logit).astype(jnp.bfloat16)
    through = jnp.einsum("ts,sd->td", logit_grad, param_all, preferred_element_type=jnp.float32)
    return (direct + through).astype(jnp.bfloat16)[None]


def solution(mesh):
    placed = (
        P("clip", "seq", None),
        P("clip", "seq", None),
        P("clip", "seq", None),
        P(None, "seq"),
        P(None, BOTH, None),
        P("clip", "seq", None),
        P(BOTH, None, None),
        P(BOTH, None, None),
    )
    return jax.shard_map(
        on_device, mesh=mesh, in_specs=placed, out_specs=P("clip", "seq", None), check_vma=False
    )
```

time: 91.4 us -> 52.8 us (0.58)
  blocking collectives: 34.7 us -> 19.9 us
  waiting for transfers between devices: 14.7 us -> 0.07 us
  between operations: 13.5 us -> 0.12 us
  starting transfers between devices: 8.86 us -> 13.1 us
    all_gather x5 -> x2, blocking collectives: 28.5 us -> 13.2 us  [the longest x1 8.12 us: on_device(): packed_all = lax.all_gather(packed, 'seq', axis=0)]
    reduce_scatter x1 -> x0, waiting for transfers between devices: 11.2 us -> none  [on_device(): lax.psum_scatter(blocks.astype(jnp.bfloat16), 'seq', scatter_dimension=1,...]
    all_to_all x2, starting transfers between devices: 8.86 us -> 13.1 us  [the longest x1 7.3 us: on_device(): lax.all_to_all(blocks, BOTH, split_axis=0, concat_axis=0, tiled=True)]
    all_to_all x2, waiting for transfers between devices: 3.54 us -> 0.07 us  [the longest x1 0.07 us: on_device(): lax.all_to_all(copies.reshape(clip_count * seq_count, local_slots, width)...]
    convert_element_type x2 -> x1, local copies, waits for them, and re-layouts: 2.09 us -> 0.03 us  [on_device(): local_grad = jnp.einsum('cejh,edh->cejd', hidden_cot, expert_in, preferre...]
  transfers between devices with their start and end apart: 3 -> 2, of which waited for: 2 -> 1; matrix products, arithmetic and copies ran while one was open for 4% -> 9% of each run, Pallas kernels for 0% -> 0%
where the time goes in v1:
time: 52.8 us; the launch traced here: 52.4 us
  blocking collectives  19.9 us (38%)
  matrix products  13.7 us (26%)
  starting transfers between devices  13.1 us (25%)
  local copies, waits for them, and re-layouts  3.25 us (6%)
  other arithmetic  2.28 us (4%)
    all_gather x1, blocking collectives, on_device(): packed_all = lax.all_gather(packed, 'seq', axis=0)  8.12 us
    all_to_all x1, starting transfers between devices, on_device(): lax.all_to_all(blocks, BOTH, split_axis=0, concat_axis=0, tiled=True)  7.3 us
    psum x1, blocking collectives, on_device(): slot_dots = lax.psum(jnp.sum(dispatch * disp_cot, axis=0), 'seq')  6.63 us
    dot_general x1, matrix products, on_device(): jnp.einsum('cejh,edh->cejd', hidden_cot, expert_in, preferred_element_typ...  6.63 us
    all_to_all x1, starting transfers between devices, on_device(): lax.all_to_all(copies.reshape(clip_count * seq_count, local_slots, width)...  5.8 us
    all_gather x1, blocking collectives, on_device(): stats = lax.all_gather(jnp.stack([local_max, local_sum]), 'seq')  5.1 us
    dot_general x1, matrix products, on_device(): jnp.einsum('cejd,edh->cejh', expert_feed, expert_in, preferred_element_ty...  3.22 us
    dot_general x1, matrix products, on_device(): jnp.einsum('ts,sd->td', logit_grad, param_all, preferred_element_type=jnp...  1.4 us
  transfers between devices with their start and end apart: 2, of which 1 were waited for; matrix products, arithmetic and copies ran while one was open for 9% of the time, Pallas kernels for 0%

profile of v1, /device:TPU:0, one launch (start us, length us, event | category | flops | bytes accessed | tf_op | source)
XLA Modules:
  0.0 52.4 jit_solution(12210913490706278211)
XLA Ops:
  0.0 0.0 copy-start
  0.0 1.1 %fusion.82 = (bf16[128]{0:T(256)(128)(2,1)S(1)}, bf16[512]{0:T(512)(128)(2,1)S(1)}) fusion(bf16[1,512,128]{2,1,0:T(8,128)(2,1)} %param.10), kind=kLoop, calls=%fused_computation.84 | loop fusion | flops 130432 | bytes 132352 | tf_op jit(solution)/shard_map/reduce_max | solution.py:36
  1.1 1.0 %copy.13 = bf16[1,512,128]{1,2,0:T(8,128)(2,1)S(1)} copy(bf16[1,512,128]{2,1,0:T(8,128)(2,1)} %param.10) | data formatting | bytes 262144 | tf_op args[2]
  2.1 0.2 fusion.40
  2.3 0.0 copy-done
  2.3 0.3 convolution_convert_fusion
  2.6 0.7 %reshape.83 = bf16[32,4,768]{2,1,0:T(4,128)(2,1)} reshape(bf16[128,768]{1,0:T(8,128)(2,1)S(1)} %convolution_convert_fusion) | data formatting | bytes 393216 | tf_op jit(solution)/shard_map/reshape | solution.py:27
  3.4 7.3 %all-to-all-start = ((bf16[32,4,768]{2,1,0:T(4,128)(2,1)}), bf16[32,4,768]{2,1,0:T(4,128)(2,1)S(1)}, u32[]{:S(2)}, u32[]{:S(2)}) async-start(bf16[32,4,768]{2,1,0:T(4,128)(2,1)} %reshape.83), calls=%async_computation | async-start | bytes 393216 | tf_op jit(solution)/shard_map/all_to_all | solution.py:30
  10.7 5.1 %all-gather.2 = f32[4,2,128]{2,1,0:T(2,128)S(1)} all-gather(f32[1,2,128]{2,1,0:T(2,128)S(1)} %maximum_bitcast_fusion), channel_id=2, replica_groups=mesh['clip'=8,'seq'=4] {'seq'}, dimensions={0}, use_global_device_ids=true | all-gather | bytes 5120 | tf_op jit(solution)/shard_map/all_gather | solution.py:38
  15.8 0.8 %pad_maximum_fusion = bf16[64,768]{1,0:T(8,128)(2,1)S(1)} fusion(bf16[32,768]{1,0:T(8,128)(2,1)} %bitcast.119, bf16[32,768]{1,0:T(8,128)(2,1)} %bitcast.120), kind=kLoop, calls=%fused_computation.71 | loop fusion | flops 196608 | bytes 196608 | tf_op jit(solution)/shard_map/concatenate | solution.py:32
  16.7 3.2 %fusion.9 = f32[8,1,4,3072]{3,0,2,1:T(8,128)S(1)} fusion(bf16[1,768,3072]{2,1,0:T(8,128)(2,1)} %param.14, bf16[8,4,768]{2,1,0:T(4,128)(2,1)} %param.12), kind=kOutput, calls=%fused_computation.7 | convolution fusion | flops 150994944 | bytes 5160960 | tf_op jit(solution)/shard_map/cejd,edh->cejh/dot_general | solution.py:45
  19.9 0.0 all-to-all-done
  19.9 0.1 bitcast_reduce_fusion
  20.0 0.0 copy-start.1
  20.0 6.6 %fusion.13 = bf16[8,4,768]{2,0,1:T(8,128)(2,1)S(1)} fusion(bf16[1,768,3072]{2,1,0:T(8,128)(2,1)} %param.14, f32[8,1,4,3072]{3,0,2,1:T(8,128)S(1)} %fusion.9, bf16[1,3072,768]{2,1,0:T(8,128)(2,1)} %param.15, bf16[8,4,768]{2,1,0:T(4,128)(2,1)S(1)} %bitcast_reduce_fusion), kind=kOutput, calls=%fused_computation.13 | convolution fusion | flops 303980544 | bytes 9928704 | tf_op jit(solution)/shard_map/cejh,edh->cejd/dot_general | solution.py:55
  26.7 0.7 %broadcast_in_dim.4 = bf16[8,4,4,768]{3,2,1,0:T(4,128)(2,1)} broadcast(bf16[8,4,768]{2,1,0:T(4,128)(2,1)S(1)} %copy.17), dimensions={0,2,3} | broadcast | bytes 245760 | tf_op jit(solution)/shard_map/broadcast_in_dim | solution.py:59
  27.4 5.8 %all-to-all-start.1 = ((bf16[32,4,768]{2,1,0:T(4,128)(2,1)}), bf16[32,4,768]{2,1,0:T(4,128)(2,1)S(1)}, u32[]{:S(2)}, u32[]{:S(2)}) async-start(bf16[32,4,768]{2,1,0:T(4,128)(2,1)} %bitcast.23), calls=%async_computation.1 | async-start | bytes 393216 | tf_op jit(solution)/shard_map/all_to_all | solution.py:60
  33.2 8.1 %all-gather.1 = bf16[256,768]{1,0:T(8,128)(2,1)S(1)} all-gather(bf16[64,768]{1,0:T(8,128)(2,1)S(1)} %pad_maximum_fusion), channel_id=3, replica_groups=mesh['clip'=8,'seq'=4] {'seq'}, dimensions={0}, use_global_device_ids=true | all-gather | bytes 491520 | tf_op jit(solution)/shard_map/all_gather | solution.py:33
  41.3 0.7 %fusion.83 = (bf16[4,32,768]{2,1,0:T(8,128)(2,1)}, bf16[4,32,768]{2,1,0:T(8,128)(2,1)S(1)}) fusion(bf16[4,64,768]{2,1,0:T(8,128)(2,1)S(1)} %bitcast.116), kind=kLoop, calls=%fused_computation.85 | loop fusion | bytes 786432 | tf_op jit(solution)/shard_map/slice | solution.py:35
  42.0 0.1 all-to-all-done.1
  42.1 0.1 reshape.89
  42.1 0.0 copy-done.1
  42.2 0.4 convolution_bitcast_fusion
  42.5 0.5 fusion.61
  43.0 1.3 %multiply_reduce_fusion.1 = (f32[512]{0:T(512)S(1)}, f32[128]{0:T(128)S(1)}, f32[512,128]{0,1:T(8,128)S(1)}) fusion(bf16[1,512,128]{1,2,0:T(8,128)(2,1)S(1)} %copy.13, f32[512]{0:T(512)S(1)} %get-tuple-element.8, f32[512]{0:T(512)S(1)} %reduce_max.47, f32[512,128]{0,1:T(8,128)S(1)} %convolution_bitcast_fusion, f32[128]{0:T(128)S(1)} %multiply_reduce_fusion.2, ...), kind=kOutput, calls=%fused_computation.50 | convolution fusion | flops 101252480 | bytes 1646080 | tf_op jit(solution)/shard_map/td,sd->ts/dot_general | solution.py:42
  44.4 6.6 %psum.7 = f32[128]{0:T(128)S(1)} all-reduce(f32[128]{0:T(128)S(1)} %get-tuple-element.6), channel_id=1, replica_groups=mesh['clip'=8,'seq'=4] {'seq'}, use_global_device_ids=true, to_apply=%region_9.0 | all-reduce | flops 128 | bytes 1024 | tf_op jit(solution)/shard_map/psum | solution.py:70
  51.0 1.4 %fusion.12 = bf16[1,512,768]{2,1,0:T(8,128)(2,1)} fusion(f32[512,768]{1,0:T(8,128)S(1)} %fusion.61, bf16[128,768]{1,0:T(8,128)(2,1)S(1)} %bitcast.117, f32[512,128]{0,1:T(8,128)S(1)} %convolution_bitcast_fusion, f32[512,128]{0,1:T(8,128)S(1)} %get-tuple-element.18, bf16[1,512,128]{1,2,0:T(8,128)(2,1)S(1)} %copy.13, f32[128]{0:T(128)S(1)} %psum.7, ...), kind=kOutput, calls=%fused_computation.9 | convolution fusion | flops 102170624 | bytes 3218944 | tf_op jit(solution)/shard_map/ts,sd->td/dot_general | solution.py:73
  (6 shorter events, 0.1 us)
Async XLA Ops:
  0.0 2.3 %copy-start = (bf16[1,512,768]{2,1,0:T(8,128)(2,1)S(1)}, bf16[1,512,768]{2,1,0:T(8,128)(2,1)}, u32[]{:S(2)}) copy-start(bf16[1,512,768]{2,1,0:T(8,128)(2,1)} %param.9) | copy-start | bytes 2359300
  3.4 16.5 %all-to-all-start = ((bf16[32,4,768]{2,1,0:T(4,128)(2,1)}), bf16[32,4,768]{2,1,0:T(4,128)(2,1)S(1)}, u32[]{:S(2)}, u32[]{:S(2)}) async-start(bf16[32,4,768]{2,1,0:T(4,128)(2,1)} %reshape.83), calls=%async_computation | async-start | bytes 393216 | tf_op jit(solution)/shard_map/all_to_all | solution.py:30
  20.0 22.2 %copy-start.1 = (bf16[1,512,768]{2,1,0:T(8,128)(2,1)S(1)}, bf16[1,512,768]{2,1,0:T(8,128)(2,1)}, u32[]{:S(2)}) copy-start(bf16[1,512,768]{2,1,0:T(8,128)(2,1)} %param.8) | copy-start | bytes 2359300
  27.4 14.7 %all-to-all-start.1 = ((bf16[32,4,768]{2,1,0:T(4,128)(2,1)}), bf16[32,4,768]{2,1,0:T(4,128)(2,1)S(1)}, u32[]{:S(2)}, u32[]{:S(2)}) async-start(bf16[32,4,768]{2,1,0:T(4,128)(2,1)} %bitcast.23), calls=%async_computation.1 | async-start | bytes 393216 | tf_op jit(solution)/shard_map/all_to_all | solution.py:60

commit v2 on v1

--- a/solution.py
+++ b/solution.py
@@ -4,6 +4,84 @@
 from jax.sharding import PartitionSpec as P
 
 BOTH = ("clip", "seq")
+
+
+def swap(value, bit):
+    count = lax.axis_size("seq")
+    return lax.ppermute(value, "seq", [(i, i ^ bit) for i in range(count)])
+
+
+def pack_stats(highest, total, width):
+    part0 = lax.reduce_precision(total, 8, 7)
+    part1 = lax.reduce_precision(total - part0, 8, 7)
+    part2 = total - part0 - part1
+    flat = jnp.concatenate([highest, part0, part1, part2]).astype(jnp.bfloat16)
+    rows = -(-flat.size // (8 * width)) * 8
+    return jnp.pad(flat, (0, rows * width - flat.size)).reshape(rows, width)
+
+
+def unpack_stats(rows, slot_total):
+    parts = rows.reshape(-1)[: 4 * slot_total].astype(jnp.float32).reshape(4, slot_total)
+    return parts[0], parts[1] + parts[2] + parts[3]
+
+
+def merge(mine, theirs):
+    highest = jnp.maximum(mine[0], theirs[0])
+    scale_a, scale_b = jnp.exp(mine[0] - highest), jnp.exp(theirs[0] - highest)
+    return highest, mine[1] * scale_a + theirs[1] * scale_b, scale_a, scale_b
+
+
+def seq_exchange(highest, total, sums, static_rows):
+    width = sums.shape[1]
+    slot_total = sums.shape[0]
+    count = lax.axis_size("seq")
+    me = lax.axis_index("seq")
+    bits = []
+    while (1 << len(bits)) < count:
+        bits.append(1 << len(bits))
+    held = sums
+    start = 0
+    gathered = static_rows[None]
+    for bit in bits:
+        last = bit == bits[-1]
+        up = (me & bit) != 0
+        half = held.shape[0] // 2
+        stat_rows = pack_stats(highest, total, width)
+        if last:
+            keep, give = held, held
+        else:
+            low, high = held[:half], held[half:]
+            keep = jnp.where(up, high, low)
+            give = jnp.where(up, low, high)
+            start = start + jnp.where(up, half, 0)
+        pieces = [give.astype(jnp.bfloat16), stat_rows] + ([static_rows] if last else [])
+        got = swap(jnp.concatenate(pieces, axis=0), bit)
+        rows = give.shape[0]
+        theirs = unpack_stats(got[rows : rows + stat_rows.shape[0]], slot_total)
+        highest, total, scale_a, scale_b = merge((highest, total), theirs)
+        mine_a = lax.dynamic_slice_in_dim(scale_a, start, rows)[:, None]
+        mine_b = lax.dynamic_slice_in_dim(scale_b, start, rows)[:, None]
+        held = keep.astype(jnp.float32) * mine_a + got[:rows].astype(jnp.float32) * mine_b
+        if last:
+            other = got[rows + stat_rows.shape[0] :]
+            gathered = jnp.stack(
+                [jnp.where(up, other, static_rows), jnp.where(up, static_rows, other)]
+            )
+    held = held.astype(jnp.bfloat16)
+    for bit in bits[-2::-1]:
+        up = (me & bit) != 0
+        rows = held.shape[0]
+        got = swap(
+            jnp.concatenate([held, gathered.reshape(-1, width)], axis=0), bit
+        )
+        held = jnp.concatenate(
+            [jnp.where(up, got[:rows], held), jnp.where(up, held, got[:rows])], axis=0
+        )
+        other = got[rows:].reshape(gathered.shape)
+        gathered = jnp.stack(
+            [jnp.where(up, other, gathered), jnp.where(up, gathered, other)], axis=1
+        ).reshape((-1,) + static_rows.shape)
+    return highest, total, held, gathered
 
 
 def on_device(
@@ -28,17 +106,20 @@
         clip_count * seq_count, local_slots, width
     )
     received = lax.all_to_all(blocks, BOTH, split_axis=0, concat_axis=0, tiled=True)
+    local_max = jnp.max(scores, axis=0)
+    raised = jnp.exp(scores - local_max)
+    local_sum = jnp.sum(raised, axis=0)
+    local_tok = jnp.einsum(
+        "ts,td->sd", raised.astype(jnp.bfloat16), tok_feats, preferred_element_type=jnp.float32
+    )
     seq_slots = slot_params.shape[1]
-    packed = jnp.concatenate([slot_params.T, slot_outputs[0]], axis=0)
-    packed_all = lax.all_gather(packed, "seq", axis=0)
+    static_rows = jnp.concatenate([slot_params.T, slot_outputs[0]], axis=0)
+    col_max, col_sum, slot_tok, packed_all = seq_exchange(
+        local_max, local_sum, local_tok, static_rows
+    )
     param_all = packed_all[:, :seq_slots].reshape(slot_total, width)
     slot_out = packed_all[:, seq_slots:].reshape(slot_total, width)
-    local_max = jnp.max(scores, axis=0)
-    local_sum = jnp.sum(jnp.exp(scores - local_max), axis=0)
-    stats = lax.all_gather(jnp.stack([local_max, local_sum]), "seq")
-    col_max = jnp.max(stats[:, 0], axis=0)
-    col_sum = jnp.sum(stats[:, 1] * jnp.exp(stats[:, 0] - col_max), axis=0)
-    dispatch = jnp.exp(scores - col_max) / col_sum
+    dispatch = raised * (jnp.exp(local_max - col_max) / col_sum)
     comb_cot = jnp.einsum("td,sd->ts", out_cot, slot_out, preferred_element_type=jnp.float32)
     comb_logit = combine * (comb_cot - jnp.sum(combine * comb_cot, axis=1, keepdims=True))
     expert_feed = slot_inputs.reshape(clip_total, expert_block, slot_each, width)
@@ -65,13 +146,15 @@
         tiled=True,
     ).reshape(slot_total, width)
     dispatch_b = dispatch.astype(jnp.bfloat16)
-    direct = jnp.dot(dispatch_b, slot_grad, preferred_element_type=jnp.float32)
     disp_cot = jnp.einsum("td,sd->ts", tok_feats, slot_grad, preferred_element_type=jnp.float32)
-    slot_dots = lax.psum(jnp.sum(dispatch * disp_cot, axis=0), "seq")
+    slot_dots = jnp.sum(slot_grad.astype(jnp.float32) * slot_tok.astype(jnp.float32), axis=1)
+    slot_dots = slot_dots / col_sum
     disp_logit = dispatch * (disp_cot - slot_dots)
     logit_grad = (comb_logit + disp_logit).astype(jnp.bfloat16)
-    through = jnp.einsum("ts,sd->td", logit_grad, param_all, preferred_element_type=jnp.float32)
-    return (direct + through).astype(jnp.bfloat16)[None]
+    both_weights = jnp.concatenate([dispatch_b, logit_grad], axis=1)
+    both_rows = jnp.concatenate([slot_grad, param_all], axis=0)
+    token_grad = jnp.dot(both_weights, both_rows, preferred_element_type=jnp.float32)
+    return token_grad.astype(jnp.bfloat16)[None]
 
 
 def solution(mesh):

time: 52.8 us -> 46.2 us (0.88)
  blocking collectives: 19.9 us -> 0 us
  waiting for transfers between devices: 0.07 us -> 12.5 us
  starting transfers between devices: 13.1 us -> 13.8 us
    all_gather x2 -> x0, blocking collectives: 13.2 us -> none  [the longest x1 8.12 us: on_device(): packed_all = lax.all_gather(packed, 'seq', axis=0)]
    all_to_all x1, waiting for transfers between devices: 0.07 us -> 8.14 us  [on_device(): lax.all_to_all(copies.reshape(clip_count * seq_count, local_slots, width)...]
    psum x1 -> x0, blocking collectives: 6.63 us -> none  [on_device(): slot_dots = lax.psum(jnp.sum(dispatch * disp_cot, axis=0), 'seq')]
    ppermute x0 -> x3, waiting for transfers between devices: none -> 4.31 us  [swap(): return lax.ppermute(value, 'seq', [(i, i ^ bit) for i in range(count)])]
    ppermute x0 -> x3, starting transfers between devices: none -> 2.43 us  [swap(): return lax.ppermute(value, 'seq', [(i, i ^ bit) for i in range(count)])]
    all_to_all x1, starting transfers between devices: 5.8 us -> 4.44 us  [on_device(): lax.all_to_all(copies.reshape(clip_count * seq_count, local_slots, width)...]
    reduce_max x2 -> x1, other arithmetic: 1.1 us -> 0.01 us  [on_device(): local_max = jnp.max(scores, axis=0)]
    reduce_max x1 -> x2, other arithmetic: 0.01 us -> 1.1 us  [on_device(): combine = jax.nn.softmax(scores, axis=1)]
  transfers between devices with their start and end apart: 2 -> 5, of which waited for: 1 -> 2; matrix products, arithmetic and copies ran while one was open for 9% -> 29% of each run, Pallas kernels for 0% -> 0%
where the time goes in v2:
time: 46.2 us; the launch traced here: 45.7 us
  starting transfers between devices  13.8 us (30%)
  matrix products  13.6 us (29%)
  waiting for transfers between devices  12.5 us (27%)
  local copies, waits for them, and re-layouts  3.27 us (7%)
  other arithmetic  2.15 us (5%)
    all_to_all x1, waiting for transfers between devices, on_device(): lax.all_to_all(copies.reshape(clip_count * seq_count, local_slots, width)...  8.14 us
    all_to_all x1, starting transfers between devices, on_device(): lax.all_to_all(blocks, BOTH, split_axis=0, concat_axis=0, tiled=True)  6.95 us
    dot_general x1, matrix products, on_device(): jnp.einsum('cejh,edh->cejd', hidden_cot, expert_in, preferred_element_typ...  6.57 us
    all_to_all x1, starting transfers between devices, on_device(): lax.all_to_all(copies.reshape(clip_count * seq_count, local_slots, width)...  4.44 us
    ppermute x3, waiting for transfers between devices, swap(): return lax.ppermute(value, 'seq', [(i, i ^ bit) for i in range(count)])  4.31 us
    dot_general x1, matrix products, on_device(): jnp.einsum('cejd,edh->cejh', expert_feed, expert_in, preferred_element_ty...  3.22 us
    ppermute x3, starting transfers between devices, swap(): return lax.ppermute(value, 'seq', [(i, i ^ bit) for i in range(count)])  2.43 us
    dot_general x1, matrix products, on_device(): jnp.einsum('ts,td->sd', raised.astype(jnp.bfloat16), tok_feats, preferred...  1.46 us
  transfers between devices with their start and end apart: 5, of which 2 were waited for; matrix products, arithmetic and copies ran while one was open for 29% of the time, Pallas kernels for 0%

profile of v2, /device:TPU:0, one launch (start us, length us, event | category | flops | bytes accessed | tf_op | source)
XLA Modules:
  0.0 45.7 jit_solution(6662571469270029242)
XLA Ops:
  0.0 1.1 %fusion.106 = (bf16[512]{0:T(512)(128)(2,1)S(1)}, bf16[128]{0:T(256)(128)(2,1)S(1)}) fusion(bf16[1,512,128]{2,1,0:T(8,128)(2,1)} %param.10), kind=kLoop, calls=%fused_computation.139 | loop fusion | flops 130432 | bytes 132352 | tf_op jit(solution)/shard_map/reduce_max | solution.py:101
  1.1 1.0 %copy.19 = bf16[1,512,128]{1,2,0:T(8,128)(2,1)S(1)} copy(bf16[1,512,128]{2,1,0:T(8,128)(2,1)} %param.10) | data formatting | bytes 262144 | tf_op args[2]
  2.2 0.2 fusion.53
  2.4 1.5 %fusion.23 = f32[128,768]{1,0:T(8,128)S(1)} fusion(bf16[1,512,768]{2,1,0:T(8,128)(2,1)} %param.8, bf16[1,512,128]{1,2,0:T(8,128)(2,1)S(1)} %copy.19, f32[128]{0:T(128)S(1)} %reduce_max.29), kind=kOutput, calls=%fused_computation.21 | convolution fusion | flops 100859904 | bytes 1311232 | tf_op jit(solution)/shard_map/ts,td->sd/dot_general | solution.py:112
  3.9 0.5 %collective-permute-start = (bf16[72,768]{1,0:T(8,128)(2,1)S(1)}, bf16[72,768]{1,0:T(8,128)(2,1)S(1)}, u32[]{:S(2)}, u32[]{:S(2)}) collective-permute-start(bf16[72,768]{1,0:T(8,128)(2,1)S(1)} %pad_maximum_fusion.5), channel_id=1, source_target_pairs={{0,1},{1,0},{2,3},{3,2},{4,5},{5,4},{6,7},{7,6},{8,9},{9,8},{10,11... | collective-permute-start | bytes 331784 | tf_op jit(solution)/shard_map/ppermute | solution.py:11
  4.5 0.3 convolution_convert_fusion.1
  4.7 0.7 %reshape.200 = bf16[32,4,768]{2,1,0:T(4,128)(2,1)} reshape(bf16[128,768]{1,0:T(8,128)(2,1)S(1)} %convolution_convert_fusion.1) | data formatting | bytes 393216 | tf_op jit(solution)/shard_map/reshape | solution.py:105
  5.5 7.0 %all-to-all-start = ((bf16[32,4,768]{2,1,0:T(4,128)(2,1)}), bf16[32,4,768]{2,1,0:T(4,128)(2,1)S(1)}, u32[]{:S(2)}, u32[]{:S(2)}) async-start(bf16[32,4,768]{2,1,0:T(4,128)(2,1)} %reshape.200), calls=%async_computation | async-start | bytes 393216 | tf_op jit(solution)/shard_map/all_to_all | solution.py:108
  12.4 0.0 collective-permute-done
  12.6 0.1 dynamic_slice.12
  12.6 0.1 dynamic_slice.13
  12.8 0.1 fusion.105
  12.9 1.8 %collective-permute-start.1 = (bf16[136,768]{1,0:T(8,128)(2,1)S(1)}, bf16[136,768]{1,0:T(8,128)(2,1)S(1)}, u32[]{:S(2)}, u32[]{:S(2)}) collective-permute-start(bf16[136,768]{1,0:T(8,128)(2,1)S(1)} %pad_maximum_fusion.2), channel_id=1, source_target_pairs={{0,2},{1,3},{2,0},{3,1},{4,6},{5,7},{6,4},{7,5},{8,10},{9,11},{10,... | collective-permute-start | bytes 626696 | tf_op jit(solution)/shard_map/ppermute | solution.py:11
  14.8 3.2 %fusion.9 = f32[8,1,4,3072]{3,0,2,1:T(8,128)S(1)} fusion(bf16[1,768,3072]{2,1,0:T(8,128)(2,1)} %param.14, bf16[8,4,768]{2,1,0:T(4,128)(2,1)S(1)} %copy-done.4), kind=kOutput, calls=%fused_computation.7 | convolution fusion | flops 150994944 | bytes 5160960 | tf_op jit(solution)/shard_map/cejd,edh->cejh/dot_general | solution.py:126
  18.0 4.3 %collective-permute-done.1 = bf16[136,768]{1,0:T(8,128)(2,1)S(1)} collective-permute-done((bf16[136,768]{1,0:T(8,128)(2,1)S(1)}, bf16[136,768]{1,0:T(8,128)(2,1)S(1)}, u32[]{:S(2)}, u32[]{:S(2)}) %collective-permute-start.1) | collective-permute-done | bytes 208928 | tf_op jit(solution)/shard_map/ppermute | solution.py:11
  22.4 0.1 dynamic_slice.14
  22.5 0.1 dynamic_slice.15
  22.6 0.1 add_convert_fusion
  22.7 0.1 collective-permute-start.2
  22.8 0.1 bitcast_reduce_fusion
  22.9 6.6 %fusion.17 = bf16[8,4,768]{2,0,1:T(8,128)(2,1)S(1)} fusion(bf16[1,768,3072]{2,1,0:T(8,128)(2,1)} %param.14, f32[8,1,4,3072]{3,0,2,1:T(8,128)S(1)} %fusion.9, bf16[1,3072,768]{2,1,0:T(8,128)(2,1)} %param.15, bf16[8,4,768]{2,1,0:T(4,128)(2,1)S(1)} %bitcast_reduce_fusion), kind=kOutput, calls=%fused_computation.17 | convolution fusion | flops 303980544 | bytes 9928704 | tf_op jit(solution)/shard_map/cejh,edh->cejd/dot_general | solution.py:136
  29.5 0.0 copy-start.1
  29.5 0.7 %broadcast_in_dim.4 = bf16[8,4,4,768]{3,2,1,0:T(4,128)(2,1)} broadcast(bf16[8,4,768]{2,1,0:T(4,128)(2,1)S(1)} %copy.24), dimensions={0,2,3} | broadcast | bytes 245760 | tf_op jit(solution)/shard_map/broadcast_in_dim | solution.py:140
  30.3 4.4 %all-to-all-start.1 = ((bf16[32,4,768]{2,1,0:T(4,128)(2,1)}), bf16[32,4,768]{2,1,0:T(4,128)(2,1)S(1)}, u32[]{:S(2)}, u32[]{:S(2)}) async-start(bf16[32,4,768]{2,1,0:T(4,128)(2,1)} %bitcast.32), calls=%async_computation.1 | async-start | bytes 393216 | tf_op jit(solution)/shard_map/all_to_all | solution.py:141
  34.9 0.1 reshape.209
  35.1 0.4 fusion.50
  35.5 8.1 %all-to-all-done.1 = bf16[32,4,768]{2,1,0:T(4,128)(2,1)S(1)} async-done(((bf16[32,4,768]{2,1,0:T(4,128)(2,1)}), bf16[32,4,768]{2,1,0:T(4,128)(2,1)S(1)}, u32[]{:S(2)}, u32[]{:S(2)}) %all-to-all-start.1) | async-done | bytes 196640 | tf_op jit(solution)/shard_map/all_to_all | solution.py:141
  43.6 0.2 multiply_reduce_fusion
  43.8 0.1 reduce_sum.55
  43.9 0.1 reshape.206
  44.0 0.4 fusion.16
  44.4 1.3 %fusion.12 = bf16[1,512,768]{2,1,0:T(8,128)(2,1)} fusion(bf16[128,768]{1,0:T(8,128)(2,1)S(1)} %bitcast.124, bf16[128,768]{1,0:T(8,128)(2,1)S(1)} %reshape.206, bf16[512,128]{0,1:T(8,128)(2,1)S(1)} %fusion.16, bf16[512,128]{0,1:T(8,128)(2,1)S(1)} %get-tuple-element.29), kind=kOutput, calls=%fused_computation.9 | convolution fusion | flops 203030528 | bytes 1441792 | tf_op jit(solution)/shard_map/dot_general | solution.py:156
  (42 shorter events, 0.6 us)
Async XLA Ops:
  0.0 4.5 %copy-start = (bf16[1,512,768]{2,1,0:T(8,128)(2,1)S(1)}, bf16[1,512,768]{2,1,0:T(8,128)(2,1)}, u32[]{:S(2)}) copy-start(bf16[1,512,768]{2,1,0:T(8,128)(2,1)} %param.9) | copy-start | bytes 2359300
  0.0 12.9 %copy-start.3 = (bf16[768,32]{0,1:T(8,128)(2,1)S(1)}, bf16[768,32]{0,1:T(8,128)(2,1)}, u32[]{:S(2)}) copy-start(bf16[768,32]{0,1:T(8,128)(2,1)} %param.11) | copy-start | bytes 147460
  0.0 12.9 %copy-start.2 = (bf16[1,32,768]{2,1,0:T(8,128)(2,1)S(1)}, bf16[1,32,768]{2,1,0:T(8,128)(2,1)}, u32[]{:S(2)}) copy-start(bf16[1,32,768]{2,1,0:T(8,128)(2,1)} %param.13) | copy-start | bytes 147460
  0.0 14.7 %copy-start.4 = (bf16[8,4,768]{2,1,0:T(4,128)(2,1)S(1)}, bf16[8,4,768]{2,1,0:T(4,128)(2,1)}, u32[]{:S(2)}) copy-start(bf16[8,4,768]{2,1,0:T(4,128)(2,1)} %param.12) | copy-start | bytes 147460
  3.9 8.5 %collective-permute-start = (bf16[72,768]{1,0:T(8,128)(2,1)S(1)}, bf16[72,768]{1,0:T(8,128)(2,1)S(1)}, u32[]{:S(2)}, u32[]{:S(2)}) collective-permute-start(bf16[72,768]{1,0:T(8,128)(2,1)S(1)} %pad_maximum_fusion.5), channel_id=1, source_target_pairs={{0,1},{1,0},{2,3},{3,2},{4,5},{5,4},{6,7},{7,6},{8,9},{9,8},{10,11... | collective-permute-start | bytes 331784 | tf_op jit(solution)/shard_map/ppermute | solution.py:11
  5.5 17.3 %all-to-all-start = ((bf16[32,4,768]{2,1,0:T(4,128)(2,1)}), bf16[32,4,768]{2,1,0:T(4,128)(2,1)S(1)}, u32[]{:S(2)}, u32[]{:S(2)}) async-start(bf16[32,4,768]{2,1,0:T(4,128)(2,1)} %reshape.200), calls=%async_computation | async-start | bytes 393216 | tf_op jit(solution)/shard_map/all_to_all | solution.py:108
  12.9 9.4 %collective-permute-start.1 = (bf16[136,768]{1,0:T(8,128)(2,1)S(1)}, bf16[136,768]{1,0:T(8,128)(2,1)S(1)}, u32[]{:S(2)}, u32[]{:S(2)}) collective-permute-start(bf16[136,768]{1,0:T(8,128)(2,1)S(1)} %pad_maximum_fusion.2), channel_id=1, source_target_pairs={{0,2},{1,3},{2,0},{3,1},{4,6},{5,7},{6,4},{7,5},{8,10},{9,11},{10,... | collective-permute-start | bytes 626696 | tf_op jit(solution)/shard_map/ppermute | solution.py:11
  22.7 12.0 %collective-permute-start.2 = (bf16[192,768]{1,0:T(8,128)(2,1)S(1)}, bf16[192,768]{1,0:T(8,128)(2,1)S(1)}, u32[]{:S(2)}, u32[]{:S(2)}) collective-permute-start(bf16[192,768]{1,0:T(8,128)(2,1)S(1)} %pad_maximum_fusion.1), channel_id=1, source_target_pairs={{0,1},{1,0},{2,3},{3,2},{4,5},{5,4},{6,7},{7,6},{8,9},{9,8},{10,11... | collective-permute-start | bytes 884744 | tf_op jit(solution)/shard_map/ppermute | solution.py:11
  29.5 14.5 %copy-start.1 = (bf16[1,512,768]{2,1,0:T(8,128)(2,1)S(1)}, bf16[1,512,768]{2,1,0:T(8,128)(2,1)}, u32[]{:S(2)}) copy-start(bf16[1,512,768]{2,1,0:T(8,128)(2,1)} %param.8) | copy-start | bytes 2359300
  30.3 13.3 %all-to-all-start.1 = ((bf16[32,4,768]{2,1,0:T(4,128)(2,1)}), bf16[32,4,768]{2,1,0:T(4,128)(2,1)S(1)}, u32[]{:S(2)}, u32[]{:S(2)}) async-start(bf16[32,4,768]{2,1,0:T(4,128)(2,1)} %bitcast.32), calls=%async_computation.1 | async-start | bytes 393216 | tf_op jit(solution)/shard_map/all_to_all | solution.py:141

commit v3 on v1

v3 whole, which is shorter than its diff:
```python
import functools
import math
import jax
import jax.numpy as jnp
from jax import lax
from jax.experimental import pallas as pl
from jax.experimental.pallas import tpu as pltpu
from jax.sharding import PartitionSpec as P

BOTH = ("clip", "seq")
WHOLE = pl.BlockSpec(memory_space=pltpu.VMEM)
PLACED = pl.BlockSpec(memory_space=pl.ANY)
STAYS = pl.BlockSpec(memory_space=pltpu.HBM)
GROUP = 128
MIB = 1 << 20
FREE = pl.CostEstimate(flops=0, bytes_accessed=0, transcendentals=0)


def dot_nn(a, b):
    return jnp.dot(a, b, preferred_element_type=jnp.float32)


def dot_nt(a, b):
    return lax.dot_general(a, b, (((1,), (1,)), ((), ())), preferred_element_type=jnp.float32)


def dot_tn(a, b):
    return lax.dot_general(a, b, (((0,), (0,)), ((), ())), preferred_element_type=jnp.float32)


def fold_of(rows):
    return max(1, 8 // rows)


def pick(part, rows, fold, count):
    wide = fold * count
    row = lax.broadcasted_iota(jnp.int32, (wide, count), 0)
    col = lax.broadcasted_iota(jnp.int32, (wide, count), 1)
    span = fold * rows
    inner = lax.rem(row, span) - part * rows
    base = lax.div(row, span) * rows
    hit = (inner >= 0) & (inner < rows) & (col == base + inner)
    return jnp.where(hit, 1.0, 0.0).astype(jnp.bfloat16)


def fold_rows(value, rows, fold):
    if fold == 1:
        return value
    lanes = value.shape[1] // fold
    count = min(value.shape[0], GROUP)
    picks = [pick(part, rows, fold, count) for part in range(fold)]
    groups = []
    for at in range(0, value.shape[0], count):
        groups.append(
            sum(
                dot_nn(picks[part], value[at : at + count, part * lanes : (part + 1) * lanes])
                for part in range(fold)
            )
        )
    return jnp.concatenate(groups, axis=0).astype(jnp.bfloat16)


def unfold_rows(value, rows, fold):
    if fold == 1:
        return value
    count = min(value.shape[0] // fold, GROUP)
    picks = [pick(part, rows, fold, count) for part in range(fold)]
    groups = []
    for at in range(0, value.shape[0], fold * count):
        piece = value[at : at + fold * count]
        groups.append(
            jnp.concatenate([dot_tn(picks[part], piece) for part in range(fold)], axis=1)
        )
    return jnp.concatenate(groups, axis=0).astype(jnp.bfloat16)


def fetch(pairs, sems):
    copies = [
        pltpu.make_async_copy(source, held, sems.at[at]) for at, (source, held) in enumerate(pairs)
    ]
    for copy in copies:
        copy.start()
    return copies


def cot_kernel(rows, fold, logit_hbm, grad_hbm, out_ref, logit_ref, grad_ref, sems):
    got_logits, got_grad = fetch([(logit_hbm, logit_ref), (grad_hbm, grad_ref)], sems)
    got_logits.wait()
    scores = logit_ref[...].astype(jnp.float32)
    raised = jnp.exp(scores - jnp.max(scores, axis=1, keepdims=True))
    combine = raised / jnp.sum(raised, axis=1, keepdims=True)
    got_grad.wait()
    cot = dot_tn(combine.astype(jnp.bfloat16), grad_ref[...]).astype(jnp.bfloat16)
    out_ref[...] = fold_rows(cot, rows, fold)


def expert_kernel(
    clips, seqs, rows, fold, parts, got_ref, slope_ref, in_hbm, out_hbm, send_ref, in_ref, out_ref, sems
):
    span, lanes = fold * rows, got_ref.shape[1]
    hid = in_hbm.shape[1]
    chunk = hid // parts
    places = [pl.ds(part * chunk, chunk) for part in range(parts)]
    copies = [
        (
            pltpu.make_async_copy(out_hbm.at[at, :], out_ref.at[at, :], sems.at[0, part]),
            pltpu.make_async_copy(in_hbm.at[:, at], in_ref.at[:, at], sems.at[1, part]),
        )
        for part, at in enumerate(places)
    ]
    for pair in copies:
        for copy in pair:
            copy.start()
    got = got_ref[...].astype(jnp.float32).reshape(clips, seqs, span, lanes)
    cot = jnp.sum(got, axis=1).reshape(clips * span, lanes).astype(jnp.bfloat16)
    cot = unfold_rows(cot, rows, fold)
    grad = 0.0
    for pair, at in zip(copies, places):
        pair[0].wait()
        act_cot = dot_nt(cot, out_ref[at, :])
        hidden_cot = (act_cot * slope_ref[:, at]).astype(jnp.bfloat16)
        pair[1].wait()
        grad += dot_nt(hidden_cot, in_ref[:, at])
    grad = fold_rows(grad.astype(jnp.bfloat16), rows, fold).reshape(clips, 1, span, lanes)
    grad = jnp.broadcast_to(grad, (clips, seqs, span, lanes))
    send_ref[...] = grad.reshape(clips * seqs * span, lanes)


def token_kernel(
    rows, fold, chunk, tok_ref, got_ref, sum_ref, disp_ref, comb_ref, param_ref,
    out_hbm, stage, sems
):
    slot_grad = unfold_rows(got_ref[...], rows, fold)
    slots = slot_grad.shape[0]
    cross = dot_nt(sum_ref[...], slot_grad)
    row = lax.broadcasted_iota(jnp.int32, (slots, slots), 0)
    col = lax.broadcasted_iota(jnp.int32, (slots, slots), 1)
    slot_dots = jnp.sum(jnp.where(row == col, cross, 0.0), axis=0, keepdims=True)
    both_rows = jnp.concatenate([slot_grad, param_ref[...]], axis=0)
    copies = []
    for step in range(tok_ref.shape[0] // chunk):
        part = pl.ds(step * chunk, chunk)
        dispatch = disp_ref[part, :]
        disp_cot = dot_nt(tok_ref[part, :], slot_grad)
        logit_grad = comb_ref[part, :] + dispatch * (disp_cot - slot_dots)
        weights = jnp.concatenate([dispatch, logit_grad], axis=1).astype(jnp.bfloat16)
        stage[part, :] = dot_nn(weights, both_rows).astype(jnp.bfloat16)
        copy = pltpu.make_async_copy(stage.at[part, :], out_hbm.at[part, :], sems.at[step])
        copy.start()
        copies.append(copy)
    for copy in copies:
        copy.wait()


def stays(value):
    return pltpu.with_memory_space_constraint(value, pltpu.HBM)


def after(value, token):
    return lax.optimization_barrier((value, token))[0]


def seq_bits():
    count = lax.axis_size("seq")
    return [1 << place for place in reversed(range(count.bit_length() - 1))]


def swap(value, bit):
    count = lax.axis_size("seq")
    return lax.ppermute(value, "seq", [(i, i ^ bit) for i in range(count)])


def stat_places(slots, width):
    groups, per_row = slots // GROUP, width // GROUP
    return [
        [(g * GROUP, (v * groups + g) // per_row, (v * groups + g) % per_row * GROUP) for g in range(groups)]
        for v in range(4)
    ]


def stat_rows(slots, width):
    return -(-4 * slots // (16 * width)) * 16


def side_kernel(
    parts, logit_hbm, tok_hbm, param_hbm, slot_hbm, feed_ref, in_hbm,
    pack_ref, slope_ref, logit_ref, tok_ref, stat_ref, in_ref, sems
):
    slots, width = logit_ref.shape[1], tok_ref.shape[1]
    seq_slots = slot_hbm.shape[0]
    hid = in_hbm.shape[1]
    places = [pl.ds(part * (hid // parts), hid // parts) for part in range(parts)]
    copies = fetch(
        [
            (logit_hbm, logit_ref),
            (tok_hbm, tok_ref),
            (param_hbm, pack_ref.at[pl.ds(slots, seq_slots)]),
            (slot_hbm, pack_ref.at[pl.ds(slots + seq_slots, seq_slots)]),
        ]
        + [(in_hbm.at[:, at], in_ref.at[:, at]) for at in places],
        sems,
    )
    copies[0].wait()
    scores = logit_ref[...].astype(jnp.float32)
    highest = jnp.max(scores, axis=0, keepdims=True)
    raised = jnp.exp(scores - highest)
    total = jnp.sum(raised, axis=0, keepdims=True)
    part0 = total.astype(jnp.bfloat16).astype(jnp.float32)
    part1 = (total - part0).astype(jnp.bfloat16).astype(jnp.float32)
    part2 = total - part0 - part1
    stat_ref[...] = jnp.zeros_like(stat_ref)
    for vector, spots in zip((highest, part0, part1, part2), stat_places(slots, width)):
        for slot, row, lane in spots:
            stat_ref[row : row + 1, lane : lane + GROUP] = vector[:, slot : slot + GROUP]
    pack_ref[slots + 2 * seq_slots :] = stat_ref[...].astype(jnp.bfloat16)
    copies[1].wait()
    pack_ref[:slots] = dot_tn(raised.astype(jnp.bfloat16), tok_ref[...]).astype(jnp.bfloat16)
    feed = [feed_ref[clip].astype(jnp.float32) for clip in range(feed_ref.shape[0])]
    feed = jnp.concatenate(feed, axis=0).astype(jnp.bfloat16)
    root = math.sqrt(2.0 / math.pi)
    for at, copy in zip(places, copies[4:]):
        copy.wait()
        x = dot_nn(feed, in_ref[:, at])
        bend = jnp.tanh(root * (x + 0.044715 * (x * x * x)))
        grown = root * (1.0 + 3.0 * 0.044715 * (x * x))
        slope_ref[:, at] = 0.5 * (1.0 + bend) + 0.5 * x * (1.0 - bend * bend) * grown
    copies[2].wait()
    copies[3].wait()


def weight_kernel(seqs, me_ref, logit_hbm, grad_hbm, *refs):
    packs, (disp_ref, comb_ref, sum_ref, param_ref) = refs[:seqs], refs[seqs + 1 : seqs + 5]
    slot_ref, logit_ref, grad_ref, sems = refs[seqs + 5 :]
    slots, width = logit_ref.shape[1], grad_ref.shape[1]
    got_logits, got_grad = fetch([(logit_hbm, logit_ref), (grad_hbm, grad_ref)], sems)
    seq_slots = slots // seqs
    me = me_ref[0]
    stats = []
    for other, pack in enumerate(packs):
        base = slots + 2 * seq_slots
        rows = pack[base : base + stat_rows(slots, width)].astype(jnp.float32)
        parts = [
            jnp.concatenate([rows[r : r + 1, lane : lane + GROUP] for _, r, lane in places], axis=1)
            for places in stat_places(slots, width)
        ]
        stats.append((parts[0], parts[1] + parts[2] + parts[3]))
        at = pl.ds(pl.multiple_of((me ^ other) * seq_slots, seq_slots), seq_slots)
        param_ref[at, :] = pack[slots : slots + seq_slots]
        slot_ref[at, :] = pack[slots + seq_slots : slots + 2 * seq_slots]
    highest = functools.reduce(jnp.maximum, [top for top, _ in stats])
    total = sum(part * jnp.exp(top - highest) for top, part in stats)
    row = lax.broadcasted_iota(jnp.int32, (slots, slots), 0)
    col = lax.broadcasted_iota(jnp.int32, (slots, slots), 1)
    token_sum = jnp.zeros((slots, width), jnp.float32)
    for pack, (top, _) in zip(packs, stats):
        share = jnp.exp(top - highest) / total
        share = jnp.sum(jnp.where(row == col, share, 0.0), axis=1, keepdims=True)
        token_sum += share * pack[:slots].astype(jnp.float32)
    sum_ref[...] = token_sum.astype(jnp.bfloat16)
    got_logits.wait()
    scores = logit_ref[...].astype(jnp.float32)
    disp_ref[...] = jnp.exp(scores - highest) / total
    raised = jnp.exp(scores - jnp.max(scores, axis=1, keepdims=True))
    combine = raised / jnp.sum(raised, axis=1, keepdims=True)
    got_grad.wait()
    comb_cot = dot_nt(grad_ref[...], slot_ref[...])
    comb_ref[...] = combine * (comb_cot - jnp.sum(combine * comb_cot, axis=1, keepdims=True))


def on_device(
    tokens, out_grad, saved_logits, slot_params, slot_inputs, slot_outputs, expert_in, expert_out
):
    clip_count = lax.axis_size("clip")
    seq_count = lax.axis_size("seq")
    device_count = clip_count * seq_count
    tok_feats, out_cot, logit_raw = tokens[0], out_grad[0], saved_logits[0]
    token_total, width = tok_feats.shape
    slot_total = logit_raw.shape[1]
    clip_total, local_slots = slot_inputs.shape[:2]
    hid = expert_in.shape[2]
    fold = fold_of(local_slots)
    span, lanes = fold * local_slots, width // fold
    feed_rows = clip_total * local_slots
    f32, b16 = jnp.float32, jnp.bfloat16

    still_logits, still_grad = stays(logit_raw), stays(out_cot)
    blocks = pl.pallas_call(
        functools.partial(cot_kernel, local_slots, fold),
        out_shape=jax.ShapeDtypeStruct((device_count * span, lanes), b16),
        in_specs=[STAYS, STAYS],
        out_specs=WHOLE,
        scratch_shapes=[
            pltpu.VMEM((token_total, slot_total), b16),
            pltpu.VMEM((token_total, width), b16),
            pltpu.SemaphoreType.DMA((2,)),
        ],
        compiler_params=pltpu.CompilerParams(vmem_limit_bytes=16 * MIB),
        cost_estimate=FREE,
    )(still_logits, still_grad)
    received = lax.all_to_all(
        blocks.reshape(device_count, span, lanes), BOTH, split_axis=0, concat_axis=0, tiled=True
    )

    parts = math.gcd(hid // GROUP, 4)
    seq_slots = slot_params.shape[1]
    pack_rows = slot_total + 2 * seq_slots + stat_rows(slot_total, width)
    own, slope = pl.pallas_call(
        functools.partial(side_kernel, parts),
        out_shape=(
            jax.ShapeDtypeStruct((pack_rows, width), b16),
            jax.ShapeDtypeStruct((feed_rows, hid), f32),
        ),
        in_specs=[STAYS] * 4 + [WHOLE, STAYS],
        out_specs=(WHOLE, WHOLE),
        scratch_shapes=[
            pltpu.VMEM((token_total, slot_total), b16),
            pltpu.VMEM((token_total, width), b16),
            pltpu.VMEM((stat_rows(slot_total, width), width), f32),
            pltpu.VMEM((width, hid), b16),
            pltpu.SemaphoreType.DMA((4 + parts,)),
        ],
        compiler_params=pltpu.CompilerParams(vmem_limit_bytes=24 * MIB),
        cost_estimate=FREE,
    )(
        still_logits,
        stays(tok_feats),
        stays(slot_params.T),
        stays(slot_outputs[0]),
        slot_inputs,
        stays(expert_in[0]),
    )

    send = pl.pallas_call(
        functools.partial(expert_kernel, clip_count, seq_count, local_slots, fold, parts),
        out_shape=jax.ShapeDtypeStruct((device_count * span, lanes), b16),
        in_specs=[WHOLE, WHOLE, STAYS, STAYS],
        out_specs=WHOLE,
        scratch_shapes=[
            pltpu.VMEM((width, hid), b16),
            pltpu.VMEM((hid, width), b16),
            pltpu.SemaphoreType.DMA((2, parts)),
        ],
        compiler_params=pltpu.CompilerParams(vmem_limit_bytes=20 * MIB),
        cost_estimate=pl.CostEstimate(
            flops=4 * feed_rows * width * hid,
            bytes_accessed=4 * width * hid,
            transcendentals=0,
        ),
    )(received.reshape(device_count * span, lanes), slope, stays(expert_in[0]), stays(expert_out[0]))
    returned = lax.all_to_all(
        send.reshape(device_count, span, lanes), BOTH, split_axis=0, concat_axis=0, tiled=True
    )

    held = {0: own}
    for bit in seq_bits():
        for other in list(held):
            held[other ^ bit] = swap(held[other] if other == 0 else after(held[other], send), bit)
    dispatch, comb_logit, token_sum, param_all = pl.pallas_call(
        functools.partial(weight_kernel, seq_count),
        out_shape=(
            jax.ShapeDtypeStruct((token_total, slot_total), f32),
            jax.ShapeDtypeStruct((token_total, slot_total), f32),
            jax.ShapeDtypeStruct((slot_total, width), b16),
            jax.ShapeDtypeStruct((slot_total, width), b16),
        ),
        in_specs=[pl.BlockSpec(memory_space=pltpu.SMEM), STAYS, STAYS] + [WHOLE] * seq_count + [PLACED],
        out_specs=(WHOLE,) * 4,
        scratch_shapes=[
            pltpu.VMEM((slot_total, width), b16),
            pltpu.VMEM((token_total, slot_total), b16),
            pltpu.VMEM((token_total, width), b16),
            pltpu.SemaphoreType.DMA((2,)),
        ],
        compiler_params=pltpu.CompilerParams(vmem_limit_bytes=32 * MIB),
        cost_estimate=FREE,
    )(
        lax.axis_index("seq")[None],
        still_logits,
        still_grad,
        *[held[other] for other in range(seq_count)],
        send,
    )

    chunk = math.gcd(token_total, 128)
    token_grad = pl.pallas_call(
        functools.partial(token_kernel, local_slots, fold, chunk),
        out_shape=jax.ShapeDtypeStruct((token_total, width), b16),
        in_specs=[WHOLE] * 6,
        out_specs=PLACED,
        scratch_shapes=[
            pltpu.VMEM((token_total, width), b16),
            pltpu.SemaphoreType.DMA((token_total // chunk,)),
        ],
        compiler_params=pltpu.CompilerParams(vmem_limit_bytes=16 * MIB),
        cost_estimate=pl.CostEstimate(
            flops=6 * token_total * width * slot_total,
            bytes_accessed=4 * token_total * width,
            transcendentals=0,
        ),
    )(
        tok_feats,
        returned.reshape(device_count * span, lanes),
        token_sum,
        dispatch,
        comb_logit,
        param_all,
    )
    return token_grad[None]


def solution(mesh):
    placed = (
        P("clip", "seq", None),
        P("clip", "seq", None),
        P("clip", "seq", None),
        P(None, "seq"),
        P(None, BOTH, None),
        P("clip", "seq", None),
        P(BOTH, None, None),
        P(BOTH, None, None),
    )
    return jax.shard_map(
        on_device, mesh=mesh, in_specs=placed, out_specs=P("clip", "seq", None), check_vma=False
    )
```

time: 52.8 us -> 39.1 us (0.74)
  blocking collectives: 19.9 us -> 0 us
  Pallas kernels: 0 us -> 15.7 us
  matrix products: 13.7 us -> 0 us
  waiting for transfers between devices: 0.07 us -> 9.79 us
  local copies, waits for them, and re-layouts: 3.25 us -> 0.8 us
  other arithmetic: 2.28 us -> 0 us
  starting transfers between devices: 13.1 us -> 12.3 us
    pallas_call x0 -> x5, Pallas kernels: none -> 15.7 us  [the longest x1 6.43 us: on_device(): pl.pallas_call(functools.partial(expert_kernel, clip_count, seq_count, lo...]
    dot_general x7 -> x0, matrix products: 13.7 us -> none  [the longest x1 6.63 us: on_device(): jnp.einsum('cejh,edh->cejd', hidden_cot, expert_in, preferred_element_typ...]
    all_gather x2 -> x0, blocking collectives: 13.2 us -> none  [the longest x1 8.12 us: on_device(): packed_all = lax.all_gather(packed, 'seq', axis=0)]
    all_to_all x2, waiting for transfers between devices: 0.07 us -> 8.23 us  [the longest x1 5.07 us: on_device(): lax.all_to_all(send.reshape(device_count, span, lanes), BOTH, split_axis=...]
    psum x1 -> x0, blocking collectives: 6.63 us -> none  [on_device(): slot_dots = lax.psum(jnp.sum(dispatch * disp_cot, axis=0), 'seq')]
    all_to_all x2, starting transfers between devices: 13.1 us -> 9.92 us  [the longest x1 7.3 us: on_device(): lax.all_to_all(blocks.reshape(device_count, span, lanes), BOTH, split_axi...]
    ppermute x0 -> x3, starting transfers between devices: none -> 2.41 us  [swap(): return lax.ppermute(value, 'seq', [(i, i ^ bit) for i in range(count)])]
    ppermute x0 -> x3, waiting for transfers between devices: none -> 1.56 us  [swap(): return lax.ppermute(value, 'seq', [(i, i ^ bit) for i in range(count)])]
  transfers between devices with their start and end apart: 2 -> 5, of which waited for: 1 -> 4; matrix products, arithmetic and copies ran while one was open for 9% -> 0% of each run, Pallas kernels for 0% -> 29%
where the time goes in v3:
time: 39.1 us; the launch traced here: 38.7 us
  Pallas kernels  15.7 us (40%)
  starting transfers between devices  12.3 us (31%)
  waiting for transfers between devices  9.79 us (25%)
  local copies, waits for them, and re-layouts  0.8 us (2%)
    all_to_all x1, starting transfers between devices, on_device(): lax.all_to_all(blocks.reshape(device_count, span, lanes), BOTH, split_axi...  7.3 us
    pallas_call x1, Pallas kernels, on_device(): pl.pallas_call(functools.partial(expert_kernel, clip_count, seq_count, lo...  6.43 us
    all_to_all x1, waiting for transfers between devices, on_device(): lax.all_to_all(send.reshape(device_count, span, lanes), BOTH, split_axis=...  5.07 us
    pallas_call x1, Pallas kernels, on_device(): pl.pallas_call(functools.partial(side_kernel, parts), out_shape=(jax.Shap...  3.18 us
    all_to_all x1, waiting for transfers between devices, on_device(): lax.all_to_all(blocks.reshape(device_count, span, lanes), BOTH, split_axi...  3.16 us
    all_to_all x1, starting transfers between devices, on_device(): lax.all_to_all(send.reshape(device_count, span, lanes), BOTH, split_axis=...  2.62 us
    pallas_call x1, Pallas kernels, on_device(): pl.pallas_call(functools.partial(cot_kernel, local_slots, fold), out_shap...  2.51 us
    ppermute x3, starting transfers between devices, swap(): return lax.ppermute(value, 'seq', [(i, i ^ bit) for i in range(count)])  2.41 us
  transfers between devices with their start and end apart: 5, of which 4 were waited for; matrix products, arithmetic and copies ran while one was open for 0% of the time, Pallas kernels for 29%

profile of v3, /device:TPU:0, one launch (start us, length us, event | category | flops | bytes accessed | tf_op | source)
XLA Modules:
  0.0 38.7 jit_solution(17820757313231256539)
XLA Ops:
  0.0 2.5 %shard_map.82 = bf16[256,384]{1,0:T(8,128)(2,1)} custom-call(bf16[512,128]{1,0:T(8,128)(2,1)} %bitcast.22, bf16[512,768]{1,0:T(8,128)(2,1)} %bitcast.20), custom_call_target="tpu_custom_call" | custom-call | tf_op jit(solution)/shard_map/pallas_call | solution.py:287
  2.5 7.3 %all-to-all-start = ((bf16[32,8,384]{2,1,0:T(8,128)(2,1)}), bf16[32,8,384]{2,1,0:T(8,128)(2,1)S(1)}, u32[]{:S(2)}, u32[]{:S(2)}) async-start(bf16[32,8,384]{2,1,0:T(8,128)(2,1)} %bitcast.3), calls=%async_computation | async-start | bytes 393216 | tf_op jit(solution)/shard_map/all_to_all | solution.py:300
  9.8 0.0 copy-start.1
  9.8 0.8 %copy-done.1 = bf16[8,4,768]{2,1,0:T(4,128)(2,1)S(1)} copy-done((bf16[8,4,768]{2,1,0:T(4,128)(2,1)S(1)}, bf16[8,4,768]{2,1,0:T(4,128)(2,1)}, u32[]{:S(2)}) %copy-start.1) | copy-done | bytes 49176
  10.6 3.2 %shard_map.83 = (bf16[208,768]{1,0:T(8,128)(2,1)S(1)}, f32[32,3072]{1,0:T(8,128)S(1)}) custom-call(bf16[512,128]{1,0:T(8,128)(2,1)} %bitcast.23, bf16[512,768]{1,0:T(8,128)(2,1)} %bitcast.13, bf16[32,768]{1,0:T(8,128)(2,1)} %bitcast.25, bf16[32,768]{1,0:T(8,128)(2,1)} %bitcast.26, bf16[8,4,768]{2,1,0:T(4,128)(2,1)S(1)} %copy-done.1, bf16[768,3072]{1,0:T(8,128)(2,1)} %bitcast.17), custom_call_target="tpu_custom_call" | custom-call | tf_op jit(solution)/shard_map/pallas_call | solution.py:307
  13.8 1.8 %collective-permute-start.1 = (bf16[208,768]{1,0:T(8,128)(2,1)S(1)}, bf16[208,768]{1,0:T(8,128)(2,1)S(1)}, u32[]{:S(2)}, u32[]{:S(2)}) collective-permute-start(bf16[208,768]{1,0:T(8,128)(2,1)S(1)} %get-tuple-element.13.refs_0_), channel_id=1, source_target_pairs={{0,2},{1,3},{2,0},{3,1},{4,6},{5,7},{6,4},{7,5},{8,10},{9,11},{10,... | collective-permute-start | bytes 958472 | tf_op jit(solution)/shard_map/ppermute | solution.py:170
  15.7 3.2 %all-to-all-done = bf16[32,8,384]{2,1,0:T(8,128)(2,1)S(1)} async-done(((bf16[32,8,384]{2,1,0:T(8,128)(2,1)}), bf16[32,8,384]{2,1,0:T(8,128)(2,1)S(1)}, u32[]{:S(2)}, u32[]{:S(2)}) %all-to-all-start) | async-done | bytes 196640 | tf_op jit(solution)/shard_map/all_to_all | solution.py:300
  18.8 0.0 copy-start
  18.8 6.4 %shard_map.84.refs_4_ = bf16[256,384]{1,0:T(8,128)(2,1)} custom-call(bf16[256,384]{1,0:T(8,128)(2,1)S(1)} %bitcast.16, f32[32,3072]{1,0:T(8,128)S(1)} %get-tuple-element.12.slope_ref, bf16[768,3072]{1,0:T(8,128)(2,1)} %bitcast.18, bf16[3072,768]{1,0:T(8,128)(2,1)} %bitcast.19), custom_call_target="tpu_custom_call" | custom-call | flops 301989888 | bytes 9437184 | tf_op jit(solution)/shard_map/pallas_call | solution.py:333
  25.3 2.6 %all-to-all-start.1 = ((bf16[32,8,384]{2,1,0:T(8,128)(2,1)}), bf16[32,8,384]{2,1,0:T(8,128)(2,1)S(1)}, u32[]{:S(2)}, u32[]{:S(2)}) async-start(bf16[32,8,384]{2,1,0:T(8,128)(2,1)} %bitcast.9), calls=%async_computation.1 | async-start | bytes 393216 | tf_op jit(solution)/shard_map/all_to_all | solution.py:350
  27.9 0.4 collective-permute-start
  28.3 0.0 collective-permute-done.1.refs_2_
  28.3 0.2 collective-permute-start.2
  28.5 1.1 %collective-permute-done.refs_1_ = bf16[208,768]{1,0:T(8,128)(2,1)S(1)} collective-permute-done((bf16[208,768]{1,0:T(8,128)(2,1)S(1)}, bf16[208,768]{1,0:T(8,128)(2,1)S(1)}, u32[]{:S(2)}, u32[]{:S(2)}) %collective-permute-start) | collective-permute-done | bytes 319520 | tf_op jit(solution)/shard_map/ppermute | solution.py:170
  29.6 0.5 %collective-permute-done.2.refs_3_ = bf16[208,768]{1,0:T(8,128)(2,1)S(1)} collective-permute-done((bf16[208,768]{1,0:T(8,128)(2,1)S(1)}, bf16[208,768]{1,0:T(8,128)(2,1)S(1)}, u32[]{:S(2)}, u32[]{:S(2)}) %collective-permute-start.2) | collective-permute-done | bytes 319520 | tf_op jit(solution)/shard_map/ppermute | solution.py:170
  30.0 1.7 %shard_map.85 = (f32[512,128]{1,0:T(8,128)S(1)}, f32[512,128]{1,0:T(8,128)S(1)}, bf16[128,768]{1,0:T(8,128)(2,1)S(1)}, bf16[128,768]{1,0:T(8,128)(2,1)S(1)}) custom-call(s32[1]{0:T(128)} %bitcast.11.me_ref, bf16[512,128]{1,0:T(8,128)(2,1)} %bitcast.24, bf16[512,768]{1,0:T(8,128)(2,1)} %bitcast.21, bf16[208,768]{1,0:T(8,128)(2,1)S(1)} %get-tuple-element.13.refs_0_, ...), custom_call_target="tpu_custom_call" | custom-call | tf_op jit(solution)/shard_map/pallas_call | solution.py:358
  31.7 5.1 %all-to-all-done.1 = bf16[32,8,384]{2,1,0:T(8,128)(2,1)S(1)} async-done(((bf16[32,8,384]{2,1,0:T(8,128)(2,1)}), bf16[32,8,384]{2,1,0:T(8,128)(2,1)S(1)}, u32[]{:S(2)}, u32[]{:S(2)}) %all-to-all-start.1) | async-done | bytes 196640 | tf_op jit(solution)/shard_map/all_to_all | solution.py:350
  36.8 0.0 copy-done
  36.8 1.9 %shard_map.86 = bf16[512,768]{1,0:T(8,128)(2,1)} custom-call(bf16[512,768]{1,0:T(8,128)(2,1)S(1)} %bitcast.14, bf16[256,384]{1,0:T(8,128)(2,1)S(1)} %bitcast.15, bf16[128,768]{1,0:T(8,128)(2,1)S(1)} %get-tuple-element.15.sum_ref, f32[512,128]{1,0:T(8,128)S(1)} %get-tuple-element.16.disp_ref, f32[512,128]{1,0:T(8,128)S(1)} %get-tuple-element.17.comb_ref, ...), custom_call_target="tpu_custom_call" | custom-call | flops 301989888 | bytes 1572864 | tf_op jit(solution)/shard_map/pallas_call | solution.py:385
Async XLA Ops:
  2.5 16.3 %all-to-all-start = ((bf16[32,8,384]{2,1,0:T(8,128)(2,1)}), bf16[32,8,384]{2,1,0:T(8,128)(2,1)S(1)}, u32[]{:S(2)}, u32[]{:S(2)}) async-start(bf16[32,8,384]{2,1,0:T(8,128)(2,1)} %bitcast.3), calls=%async_computation | async-start | bytes 393216 | tf_op jit(solution)/shard_map/all_to_all | solution.py:300
  9.8 0.8 %copy-start.1 = (bf16[8,4,768]{2,1,0:T(4,128)(2,1)S(1)}, bf16[8,4,768]{2,1,0:T(4,128)(2,1)}, u32[]{:S(2)}) copy-start(bf16[8,4,768]{2,1,0:T(4,128)(2,1)} %feed_ref.1) | copy-start | bytes 147460
  13.8 14.4 %collective-permute-start.1 = (bf16[208,768]{1,0:T(8,128)(2,1)S(1)}, bf16[208,768]{1,0:T(8,128)(2,1)S(1)}, u32[]{:S(2)}, u32[]{:S(2)}) collective-permute-start(bf16[208,768]{1,0:T(8,128)(2,1)S(1)} %get-tuple-element.13.refs_0_), channel_id=1, source_target_pairs={{0,2},{1,3},{2,0},{3,1},{4,6},{5,7},{6,4},{7,5},{8,10},{9,11},{10,... | collective-permute-start | bytes 958472 | tf_op jit(solution)/shard_map/ppermute | solution.py:170
  18.8 18.0 %copy-start = (bf16[1,512,768]{2,1,0:T(8,128)(2,1)S(1)}, bf16[1,512,768]{2,1,0:T(8,128)(2,1)}, u32[]{:S(2)}) copy-start(bf16[1,512,768]{2,1,0:T(8,128)(2,1)} %param.8) | copy-start | bytes 2359300
  25.3 11.5 %all-to-all-start.1 = ((bf16[32,8,384]{2,1,0:T(8,128)(2,1)}), bf16[32,8,384]{2,1,0:T(8,128)(2,1)S(1)}, u32[]{:S(2)}, u32[]{:S(2)}) async-start(bf16[32,8,384]{2,1,0:T(8,128)(2,1)} %bitcast.9), calls=%async_computation.1 | async-start | bytes 393216 | tf_op jit(solution)/shard_map/all_to_all | solution.py:350
  27.9 1.7 %collective-permute-start = (bf16[208,768]{1,0:T(8,128)(2,1)S(1)}, bf16[208,768]{1,0:T(8,128)(2,1)S(1)}, u32[]{:S(2)}, u32[]{:S(2)}) collective-permute-start(bf16[208,768]{1,0:T(8,128)(2,1)S(1)} %get-tuple-element.13.refs_0_), channel_id=1, source_target_pairs={{0,1},{1,0},{2,3},{3,2},{4,5},{5,4},{6,7},{7,6},{8,9},{9,8},{10,11... | collective-permute-start | bytes 958472 | tf_op jit(solution)/shard_map/ppermute | solution.py:170
  28.3 1.8 %collective-permute-start.2 = (bf16[208,768]{1,0:T(8,128)(2,1)S(1)}, bf16[208,768]{1,0:T(8,128)(2,1)S(1)}, u32[]{:S(2)}, u32[]{:S(2)}) collective-permute-start(bf16[208,768]{1,0:T(8,128)(2,1)S(1)} %collective-permute-done.1.refs_2_), channel_id=1, source_target_pairs={{0,1},{1,0},{2,3},{3,2},{4,5},{5,4},{6,7},{7,6},{8,9},{9,8},{10,11... | collective-permute-start | bytes 958472 | tf_op jit(solution)/shard_map/ppermute | solution.py:170

commit v4 on v3

--- a/solution.py
+++ b/solution.py
@@ -8,6 +8,7 @@
 from jax.sharding import PartitionSpec as P
 
 BOTH = ("clip", "seq")
+ROUND = ("seq", "clip")
 WHOLE = pl.BlockSpec(memory_space=pltpu.VMEM)
 PLACED = pl.BlockSpec(memory_space=pl.ANY)
 STAYS = pl.BlockSpec(memory_space=pltpu.HBM)
@@ -26,52 +27,6 @@
 
 def dot_tn(a, b):
     return lax.dot_general(a, b, (((0,), (0,)), ((), ())), preferred_element_type=jnp.float32)
-
-
-def fold_of(rows):
-    return max(1, 8 // rows)
-
-
-def pick(part, rows, fold, count):
-    wide = fold * count
-    row = lax.broadcasted_iota(jnp.int32, (wide, count), 0)
-    col = lax.broadcasted_iota(jnp.int32, (wide, count), 1)
-    span = fold * rows
-    inner = lax.rem(row, span) - part * rows
-    base = lax.div(row, span) * rows
-    hit = (inner >= 0) & (inner < rows) & (col == base + inner)
-    return jnp.where(hit, 1.0, 0.0).astype(jnp.bfloat16)
-
-
-def fold_rows(value, rows, fold):
-    if fold == 1:
-        return value
-    lanes = value.shape[1] // fold
-    count = min(value.shape[0], GROUP)
-    picks = [pick(part, rows, fold, count) for part in range(fold)]
-    groups = []
-    for at in range(0, value.shape[0], count):
-        groups.append(
-            sum(
-                dot_nn(picks[part], value[at : at + count, part * lanes : (part + 1) * lanes])
-                for part in range(fold)
-            )
-        )
-    return jnp.concatenate(groups, axis=0).astype(jnp.bfloat16)
-
-
-def unfold_rows(value, rows, fold):
-    if fold == 1:
-        return value
-    count = min(value.shape[0] // fold, GROUP)
-    picks = [pick(part, rows, fold, count) for part in range(fold)]
-    groups = []
-    for at in range(0, value.shape[0], fold * count):
-        piece = value[at : at + fold * count]
-        groups.append(
-            jnp.concatenate([dot_tn(picks[part], piece) for part in range(fold)], axis=1)
-        )
-    return jnp.concatenate(groups, axis=0).astype(jnp.bfloat16)
 
 
 def fetch(pairs, sems):
@@ -83,55 +38,73 @@
     return copies
 
 
-def cot_kernel(rows, fold, logit_hbm, grad_hbm, out_ref, logit_ref, grad_ref, sems):
+def cot_kernel(seqs, logit_hbm, grad_hbm, out_ref, logit_ref, grad_ref, sems):
     got_logits, got_grad = fetch([(logit_hbm, logit_ref), (grad_hbm, grad_ref)], sems)
     got_logits.wait()
     scores = logit_ref[...].astype(jnp.float32)
     raised = jnp.exp(scores - jnp.max(scores, axis=1, keepdims=True))
     combine = raised / jnp.sum(raised, axis=1, keepdims=True)
     got_grad.wait()
-    cot = dot_tn(combine.astype(jnp.bfloat16), grad_ref[...]).astype(jnp.bfloat16)
-    out_ref[...] = fold_rows(cot, rows, fold)
+    cot = dot_tn(combine.astype(jnp.bfloat16), grad_ref[...])
+    devices, rows, width = out_ref.shape
+    cot = cot.reshape(devices // seqs, seqs, rows, width).swapaxes(0, 1)
+    out_ref[...] = cot.reshape(out_ref.shape).astype(jnp.bfloat16)
 
 
 def expert_kernel(
-    clips, seqs, rows, fold, parts, got_ref, slope_ref, in_hbm, out_hbm, send_ref, in_ref, out_ref, sems
+    clips, seqs, got_ref, slope_ref, kept_ref, in_hbm, out_hbm, send_ref, in_ref, out_ref, cot_ref, sems
 ):
-    span, lanes = fold * rows, got_ref.shape[1]
-    hid = in_hbm.shape[1]
-    chunk = hid // parts
-    places = [pl.ds(part * chunk, chunk) for part in range(parts)]
-    copies = [
-        (
-            pltpu.make_async_copy(out_hbm.at[at, :], out_ref.at[at, :], sems.at[0, part]),
-            pltpu.make_async_copy(in_hbm.at[:, at], in_ref.at[:, at], sems.at[1, part]),
+    rows, width = got_ref.shape[1:]
+    hid, chunk = in_hbm.shape[1], kept_ref.shape[0]
+    parts = hid // chunk
+
+    def place(part):
+        return pl.ds(pl.multiple_of(part * chunk, chunk), chunk)
+
+    def out_copy(part):
+        return pltpu.make_async_copy(
+            out_hbm.at[place(part), :], out_ref.at[place(part - 1), :], sems.at[part - 1]
         )
-        for part, at in enumerate(places)
-    ]
-    for pair in copies:
-        for copy in pair:
-            copy.start()
-    got = got_ref[...].astype(jnp.float32).reshape(clips, seqs, span, lanes)
-    cot = jnp.sum(got, axis=1).reshape(clips * span, lanes).astype(jnp.bfloat16)
-    cot = unfold_rows(cot, rows, fold)
-    grad = 0.0
-    for pair, at in zip(copies, places):
-        pair[0].wait()
-        act_cot = dot_nt(cot, out_ref[at, :])
-        hidden_cot = (act_cot * slope_ref[:, at]).astype(jnp.bfloat16)
-        pair[1].wait()
-        grad += dot_nt(hidden_cot, in_ref[:, at])
-    grad = fold_rows(grad.astype(jnp.bfloat16), rows, fold).reshape(clips, 1, span, lanes)
-    grad = jnp.broadcast_to(grad, (clips, seqs, span, lanes))
-    send_ref[...] = grad.reshape(clips * seqs * span, lanes)
+
+    def in_copy(part):
+        at = place(part)
+        return pltpu.make_async_copy(in_hbm.at[:, at], in_ref.at[:, at], sems.at[parts - 1 + part])
+
+    for part in range(1, parts):
+        out_copy(part).start()
+    for part in range(parts):
+        in_copy(part).start()
+    got = got_ref[...].astype(jnp.float32).reshape(seqs, clips, rows, width)
+    cot = jnp.sum(got, axis=0).reshape(clips * rows, width).astype(jnp.bfloat16)
+    first = dot_nt(cot, kept_ref[...]) * slope_ref[:, :chunk]
+    cot_ref[:, :chunk] = first.astype(jnp.bfloat16)
+
+    @pl.loop(1, parts)
+    def _(part):
+        out_copy(part).wait()
+        at = place(part)
+        act_cot = dot_nt(cot, out_ref[place(part - 1), :])
+        cot_ref[:, at] = (act_cot * slope_ref[:, at]).astype(jnp.bfloat16)
+
+    def add(part, total):
+        in_copy(part).wait()
+        at = place(part)
+        return total + dot_nt(cot_ref[:, at], in_ref[:, at])
+
+    grad = lax.fori_loop(0, parts, add, jnp.zeros((clips * rows, width), jnp.float32))
+    grad = grad.reshape(1, clips, rows, width)
+    grad = jnp.broadcast_to(grad, (seqs, clips, rows, width))
+    send_ref[...] = grad.reshape(send_ref.shape).astype(jnp.bfloat16)
 
 
 def token_kernel(
-    rows, fold, chunk, tok_ref, got_ref, sum_ref, disp_ref, comb_ref, param_ref,
+    seqs, chunk, tok_ref, got_ref, sum_ref, disp_ref, comb_ref, param_ref,
     out_hbm, stage, sems
 ):
-    slot_grad = unfold_rows(got_ref[...], rows, fold)
-    slots = slot_grad.shape[0]
+    slots, width = param_ref.shape
+    devices, rows = got_ref.shape[:2]
+    slot_grad = got_ref[...].astype(jnp.float32).reshape(seqs, devices // seqs, rows, width)
+    slot_grad = slot_grad.swapaxes(0, 1).reshape(slots, width).astype(jnp.bfloat16)
     cross = dot_nt(sum_ref[...], slot_grad)
     row = lax.broadcasted_iota(jnp.int32, (slots, slots), 0)
     col = lax.broadcasted_iota(jnp.int32, (slots, slots), 1)
@@ -183,8 +156,8 @@
 
 
 def side_kernel(
-    parts, logit_hbm, tok_hbm, param_hbm, slot_hbm, feed_ref, in_hbm,
-    pack_ref, slope_ref, logit_ref, tok_ref, stat_ref, in_ref, sems
+    parts, logit_hbm, tok_hbm, param_hbm, slot_hbm, feed_hbm, in_hbm, out_hbm,
+    pack_ref, slope_ref, kept_ref, logit_ref, tok_ref, feed_ref, stat_ref, in_ref, sems
 ):
     slots, width = logit_ref.shape[1], tok_ref.shape[1]
     seq_slots = slot_hbm.shape[0]
@@ -196,8 +169,10 @@
             (tok_hbm, tok_ref),
             (param_hbm, pack_ref.at[pl.ds(slots, seq_slots)]),
             (slot_hbm, pack_ref.at[pl.ds(slots + seq_slots, seq_slots)]),
+            (feed_hbm, feed_ref),
         ]
-        + [(in_hbm.at[:, at], in_ref.at[:, at]) for at in places],
+        + [(in_hbm.at[:, at], in_ref.at[:, at]) for at in places]
+        + [(out_hbm.at[pl.ds(0, kept_ref.shape[0])], kept_ref)],
         sems,
     )
     copies[0].wait()
@@ -215,10 +190,11 @@
     pack_ref[slots + 2 * seq_slots :] = stat_ref[...].astype(jnp.bfloat16)
     copies[1].wait()
     pack_ref[:slots] = dot_tn(raised.astype(jnp.bfloat16), tok_ref[...]).astype(jnp.bfloat16)
+    copies[4].wait()
     feed = [feed_ref[clip].astype(jnp.float32) for clip in range(feed_ref.shape[0])]
     feed = jnp.concatenate(feed, axis=0).astype(jnp.bfloat16)
     root = math.sqrt(2.0 / math.pi)
-    for at, copy in zip(places, copies[4:]):
+    for at, copy in zip(places, copies[5:]):
         copy.wait()
         x = dot_nn(feed, in_ref[:, at])
         bend = jnp.tanh(root * (x + 0.044715 * (x * x * x)))
@@ -226,6 +202,7 @@
         slope_ref[:, at] = 0.5 * (1.0 + bend) + 0.5 * x * (1.0 - bend * bend) * grown
     copies[2].wait()
     copies[3].wait()
+    copies[-1].wait()
 
 
 def weight_kernel(seqs, me_ref, logit_hbm, grad_hbm, *refs):
@@ -278,15 +255,14 @@
     slot_total = logit_raw.shape[1]
     clip_total, local_slots = slot_inputs.shape[:2]
     hid = expert_in.shape[2]
-    fold = fold_of(local_slots)
-    span, lanes = fold * local_slots, width // fold
     feed_rows = clip_total * local_slots
     f32, b16 = jnp.float32, jnp.bfloat16
 
     still_logits, still_grad = stays(logit_raw), stays(out_cot)
+    still_in, still_out = stays(expert_in[0]), stays(expert_out[0])
     blocks = pl.pallas_call(
-        functools.partial(cot_kernel, local_slots, fold),
-        out_shape=jax.ShapeDtypeStruct((device_count * span, lanes), b16),
+        functools.partial(cot_kernel, seq_count),
+        out_shape=jax.ShapeDtypeStruct((device_count, local_slots, width), b16),
         in_specs=[STAYS, STAYS],
         out_specs=WHOLE,
         scratch_shapes=[
@@ -297,27 +273,29 @@
         compiler_params=pltpu.CompilerParams(vmem_limit_bytes=16 * MIB),
         cost_estimate=FREE,
     )(still_logits, still_grad)
-    received = lax.all_to_all(
-        blocks.reshape(device_count, span, lanes), BOTH, split_axis=0, concat_axis=0, tiled=True
-    )
+    received = lax.all_to_all(blocks, ROUND, split_axis=0, concat_axis=0, tiled=True)
 
     parts = math.gcd(hid // GROUP, 4)
     seq_slots = slot_params.shape[1]
     pack_rows = slot_total + 2 * seq_slots + stat_rows(slot_total, width)
-    own, slope = pl.pallas_call(
+    thirds = math.gcd(hid // GROUP, 3)
+    kept_rows = hid // thirds if thirds > 1 else GROUP
+    own, slope, kept = pl.pallas_call(
         functools.partial(side_kernel, parts),
         out_shape=(
             jax.ShapeDtypeStruct((pack_rows, width), b16),
             jax.ShapeDtypeStruct((feed_rows, hid), f32),
+            pltpu.VMEM((kept_rows, width), b16),
         ),
-        in_specs=[STAYS] * 4 + [WHOLE, STAYS],
-        out_specs=(WHOLE, WHOLE),
+        in_specs=[STAYS] * 7,
+        out_specs=(WHOLE,) * 3,
         scratch_shapes=[
             pltpu.VMEM((token_total, slot_total), b16),
             pltpu.VMEM((token_total, width), b16),
+            pltpu.VMEM(slot_inputs.shape, b16),
             pltpu.VMEM((stat_rows(slot_total, width), width), f32),
             pltpu.VMEM((width, hid), b16),
-            pltpu.SemaphoreType.DMA((4 + parts,)),
+            pltpu.SemaphoreType.DMA((6 + parts,)),
         ],
         compiler_params=pltpu.CompilerParams(vmem_limit_bytes=24 * MIB),
         cost_estimate=FREE,
@@ -326,19 +304,21 @@
         stays(tok_feats),
         stays(slot_params.T),
         stays(slot_outputs[0]),
-        slot_inputs,
-        stays(expert_in[0]),
+        stays(slot_inputs),
+        still_in,
+        still_out,
     )
 
     send = pl.pallas_call(
-        functools.partial(expert_kernel, clip_count, seq_count, local_slots, fold, parts),
-        out_shape=jax.ShapeDtypeStruct((device_count * span, lanes), b16),
-        in_specs=[WHOLE, WHOLE, STAYS, STAYS],
+        functools.partial(expert_kernel, clip_count, seq_count),
+        out_shape=jax.ShapeDtypeStruct((device_count, local_slots, width), b16),
+        in_specs=[WHOLE, WHOLE, WHOLE, STAYS, STAYS],
         out_specs=WHOLE,
         scratch_shapes=[
             pltpu.VMEM((width, hid), b16),
-            pltpu.VMEM((hid, width), b16),
-            pltpu.SemaphoreType.DMA((2, parts)),
+            pltpu.VMEM((hid - kept_rows, width), b16),
+            pltpu.VMEM((feed_rows, hid), b16),
+            pltpu.SemaphoreType.DMA((2 * (hid // kept_rows) - 1,)),
         ],
         compiler_params=pltpu.CompilerParams(vmem_limit_bytes=20 * MIB),
         cost_estimate=pl.CostEstimate(
@@ -346,10 +326,14 @@
             bytes_accessed=4 * width * hid,
             transcendentals=0,
         ),
-    )(received.reshape(device_count * span, lanes), slope, stays(expert_in[0]), stays(expert_out[0]))
-    returned = lax.all_to_all(
-        send.reshape(device_count, span, lanes), BOTH, split_axis=0, concat_axis=0, tiled=True
-    )
+    )(
+        received,
+        slope,
+        pltpu.with_memory_space_constraint(kept, pltpu.VMEM),
+        still_in,
+        still_out,
+    )
+    returned = lax.all_to_all(send, ROUND, split_axis=0, concat_axis=0, tiled=True)
 
     held = {0: own}
     for bit in seq_bits():
@@ -383,7 +367,7 @@
 
     chunk = math.gcd(token_total, 128)
     token_grad = pl.pallas_call(
-        functools.partial(token_kernel, local_slots, fold, chunk),
+        functools.partial(token_kernel, seq_count, chunk),
         out_shape=jax.ShapeDtypeStruct((token_total, width), b16),
         in_specs=[WHOLE] * 6,
         out_specs=PLACED,
@@ -399,7 +383,7 @@
         ),
     )(
         tok_feats,
-        returned.reshape(device_count * span, lanes),
+        returned,
         token_sum,
         dispatch,
         comb_logit,

time: 39.1 us -> 37 us (0.946)
  waiting for transfers between devices: 9.79 us -> 8.72 us
  local copies, waits for them, and re-layouts: 0.8 us -> 0.01 us
  Pallas kernels: 15.7 us -> 15.2 us
  starting transfers between devices: 12.3 us -> 12.8 us
    pallas_call x3, Pallas kernels: 10.8 us -> 9.24 us  [the longest x1 5.38 us: on_device(): pl.pallas_call(functools.partial(expert_kernel, clip_count, seq_count), o...]
    all_to_all x2, waiting for transfers between devices: 8.23 us -> 6.95 us  [the longest x1 3.53 us: on_device(): lax.all_to_all(send, ROUND, split_axis=0, concat_axis=0, tiled=True)]
    pallas_call x1, Pallas kernels: 1.67 us -> 2.67 us  [on_device(): pl.pallas_call(functools.partial(weight_kernel, seq_count), out_shape=(ja...]
    unnamed x4 -> x2, local copies, waits for them, and re-layouts: 0.8 us -> 0.01 us
    all_to_all x2, starting transfers between devices: 9.92 us -> 10.3 us  [the longest x1 7.3 us: on_device(): lax.all_to_all(blocks, ROUND, split_axis=0, concat_axis=0, tiled=True)]
  transfers between devices with their start and end apart: 5 -> 5, of which waited for: 4 -> 4; matrix products, arithmetic and copies ran while one was open for 0% -> 0% of each run, Pallas kernels for 29% -> 31%
where the time goes in v4:
time: 37 us; the launch traced here: 36.7 us
  Pallas kernels  15.2 us (41%)
  starting transfers between devices  12.8 us (35%)
  waiting for transfers between devices  8.72 us (24%)
    all_to_all x1, starting transfers between devices, on_device(): lax.all_to_all(blocks, ROUND, split_axis=0, concat_axis=0, tiled=True)  7.3 us
    pallas_call x1, Pallas kernels, on_device(): pl.pallas_call(functools.partial(expert_kernel, clip_count, seq_count), o...  5.38 us
    all_to_all x1, waiting for transfers between devices, on_device(): lax.all_to_all(send, ROUND, split_axis=0, concat_axis=0, tiled=True)  3.53 us
    all_to_all x1, waiting for transfers between devices, on_device(): lax.all_to_all(blocks, ROUND, split_axis=0, concat_axis=0, tiled=True)  3.42 us
    pallas_call x1, Pallas kernels, on_device(): pl.pallas_call(functools.partial(side_kernel, parts), out_shape=(jax.Shap...  3.3 us
    all_to_all x1, starting transfers between devices, on_device(): lax.all_to_all(send, ROUND, split_axis=0, concat_axis=0, tiled=True)  3.04 us
    pallas_call x1, Pallas kernels, on_device(): pl.pallas_call(functools.partial(weight_kernel, seq_count), out_shape=(ja...  2.67 us
    ppermute x3, starting transfers between devices, swap(): return lax.ppermute(value, 'seq', [(i, i ^ bit) for i in range(count)])  2.41 us
  transfers between devices with their start and end apart: 5, of which 4 were waited for; matrix products, arithmetic and copies ran while one was open for 0% of the time, Pallas kernels for 31%

profile of v4, /device:TPU:0, one launch (start us, length us, event | category | flops | bytes accessed | tf_op | source)
XLA Modules:
  0.0 36.7 jit_solution(5395183670303840210)
XLA Ops:
  0.0 2.2 %shard_map.82 = bf16[32,4,768]{2,1,0:T(4,128)(2,1)} custom-call(bf16[512,128]{1,0:T(8,128)(2,1)} %bitcast.17, bf16[512,768]{1,0:T(8,128)(2,1)} %bitcast.15), custom_call_target="tpu_custom_call" | custom-call | tf_op jit(solution)/shard_map/pallas_call | solution.py:263
  2.2 7.3 %all-to-all-start = ((bf16[32,4,768]{2,1,0:T(4,128)(2,1)}), bf16[32,4,768]{2,1,0:T(4,128)(2,1)S(1)}, u32[]{:S(2)}, u32[]{:S(2)}) async-start(bf16[32,4,768]{2,1,0:T(4,128)(2,1)} %shard_map.82), calls=%async_computation | async-start | bytes 393216 | tf_op jit(solution)/shard_map/all_to_all | solution.py:276
  9.5 3.3 %shard_map.83 = (bf16[208,768]{1,0:T(8,128)(2,1)S(1)}, f32[32,3072]{1,0:T(8,128)S(1)}, bf16[1024,768]{1,0:T(8,128)(2,1)S(1)}) custom-call(bf16[512,128]{1,0:T(8,128)(2,1)} %bitcast.18, bf16[512,768]{1,0:T(8,128)(2,1)} %bitcast.9, bf16[32,768]{1,0:T(8,128)(2,1)} %bitcast.20, bf16[32,768]{1,0:T(8,128)(2,1)} %bitcast.21, bf16[8,4,768]{2,1,0:T(4,128)(2,1)} %feed_hbm.1, ...), custom_call_target="tpu_custom_call" | custom-call | tf_op jit(solution)/shard_map/pallas_call | solution.py:283
  12.8 1.8 %collective-permute-start.1 = (bf16[208,768]{1,0:T(8,128)(2,1)S(1)}, bf16[208,768]{1,0:T(8,128)(2,1)}, u32[]{:S(2)}, u32[]{:S(2)}) collective-permute-start(bf16[208,768]{1,0:T(8,128)(2,1)S(1)} %get-tuple-element.15.refs_0_), channel_id=1, source_target_pairs={{0,2},{1,3},{2,0},{3,1},{4,6},{5,7},{6,4},{7,5},{8,10},{9,11},{10,... | collective-permute-start | bytes 958472 | tf_op jit(solution)/shard_map/ppermute | solution.py:143
  14.7 3.4 %all-to-all-done.got_ref = bf16[32,4,768]{2,1,0:T(4,128)(2,1)S(1)} async-done(((bf16[32,4,768]{2,1,0:T(4,128)(2,1)}), bf16[32,4,768]{2,1,0:T(4,128)(2,1)S(1)}, u32[]{:S(2)}, u32[]{:S(2)}) %all-to-all-start) | async-done | bytes 196640 | tf_op jit(solution)/shard_map/all_to_all | solution.py:276
  18.1 0.0 copy-start
  18.1 5.4 %shard_map.84.refs_4_ = bf16[32,4,768]{2,1,0:T(4,128)(2,1)} custom-call(bf16[32,4,768]{2,1,0:T(4,128)(2,1)S(1)} %all-to-all-done.got_ref, f32[32,3072]{1,0:T(8,128)S(1)} %get-tuple-element.13.slope_ref, bf16[1024,768]{1,0:T(8,128)(2,1)S(1)} %get-tuple-element.14.kept_ref, bf16[768,3072]{1,0:T(8,128)(2,1)} %bitcast.12, bf16[3072,768]{1,0:T(8,128)(2,1)} %bitcast.14), custom_call_target="tpu_custom_call" | custom-call | flops 301989888 | bytes 9437184 | tf_op jit(solution)/shard_map/pallas_call | solution.py:312
  23.5 3.0 %all-to-all-start.1 = ((bf16[32,4,768]{2,1,0:T(4,128)(2,1)}), bf16[32,4,768]{2,1,0:T(4,128)(2,1)S(1)}, u32[]{:S(2)}, u32[]{:S(2)}) async-start(bf16[32,4,768]{2,1,0:T(4,128)(2,1)} %shard_map.84.refs_4_), calls=%async_computation.1 | async-start | bytes 393216 | tf_op jit(solution)/shard_map/all_to_all | solution.py:336
  26.5 0.3 collective-permute-start
  26.8 0.0 collective-permute-done.1.refs_2_
  26.8 0.3 collective-permute-start.2
  27.1 1.1 %collective-permute-done.refs_1_ = bf16[208,768]{1,0:T(8,128)(2,1)S(1)} collective-permute-done((bf16[208,768]{1,0:T(8,128)(2,1)S(1)}, bf16[208,768]{1,0:T(8,128)(2,1)S(1)}, u32[]{:S(2)}, u32[]{:S(2)}) %collective-permute-start) | collective-permute-done | bytes 319520 | tf_op jit(solution)/shard_map/ppermute | solution.py:143
  28.2 0.7 %collective-permute-done.2.refs_3_ = bf16[208,768]{1,0:T(8,128)(2,1)S(1)} collective-permute-done((bf16[208,768]{1,0:T(8,128)(2,1)}, bf16[208,768]{1,0:T(8,128)(2,1)S(1)}, u32[]{:S(2)}, u32[]{:S(2)}) %collective-permute-start.2) | collective-permute-done | bytes 319520 | tf_op jit(solution)/shard_map/ppermute | solution.py:143
  28.9 2.7 %shard_map.85 = (f32[512,128]{1,0:T(8,128)S(1)}, f32[512,128]{1,0:T(8,128)S(1)}, bf16[128,768]{1,0:T(8,128)(2,1)S(1)}, bf16[128,768]{1,0:T(8,128)(2,1)S(1)}) custom-call(s32[1]{0:T(128)} %bitcast.7.me_ref, bf16[512,128]{1,0:T(8,128)(2,1)} %bitcast.19, bf16[512,768]{1,0:T(8,128)(2,1)} %bitcast.16, bf16[208,768]{1,0:T(8,128)(2,1)S(1)} %get-tuple-element.15.refs_0_, ...), custom_call_target="tpu_custom_call" | custom-call | tf_op jit(solution)/shard_map/pallas_call | solution.py:342
  31.6 3.5 %all-to-all-done.1.got_ref = bf16[32,4,768]{2,1,0:T(4,128)(2,1)S(1)} async-done(((bf16[32,4,768]{2,1,0:T(4,128)(2,1)}), bf16[32,4,768]{2,1,0:T(4,128)(2,1)S(1)}, u32[]{:S(2)}, u32[]{:S(2)}) %all-to-all-start.1) | async-done | bytes 196640 | tf_op jit(solution)/shard_map/all_to_all | solution.py:336
  35.1 0.0 copy-done
  35.1 1.7 %shard_map.86 = bf16[512,768]{1,0:T(8,128)(2,1)} custom-call(bf16[512,768]{1,0:T(8,128)(2,1)S(1)} %bitcast.10, bf16[32,4,768]{2,1,0:T(4,128)(2,1)S(1)} %all-to-all-done.1.got_ref, bf16[128,768]{1,0:T(8,128)(2,1)S(1)} %get-tuple-element.17.sum_ref, f32[512,128]{1,0:T(8,128)S(1)} %get-tuple-element.18.disp_ref, f32[512,128]{1,0:T(8,128)S(1)} %get-tuple-element.19.comb_ref, ...), custom_call_target="tpu_custom_call" | custom-call | flops 301989888 | bytes 1572864 | tf_op jit(solution)/shard_map/pallas_call | solution.py:369
Async XLA Ops:
  2.2 15.9 %all-to-all-start = ((bf16[32,4,768]{2,1,0:T(4,128)(2,1)}), bf16[32,4,768]{2,1,0:T(4,128)(2,1)S(1)}, u32[]{:S(2)}, u32[]{:S(2)}) async-start(bf16[32,4,768]{2,1,0:T(4,128)(2,1)} %shard_map.82), calls=%async_computation | async-start | bytes 393216 | tf_op jit(solution)/shard_map/all_to_all | solution.py:276
  12.8 14.0 %collective-permute-start.1 = (bf16[208,768]{1,0:T(8,128)(2,1)S(1)}, bf16[208,768]{1,0:T(8,128)(2,1)}, u32[]{:S(2)}, u32[]{:S(2)}) collective-permute-start(bf16[208,768]{1,0:T(8,128)(2,1)S(1)} %get-tuple-element.15.refs_0_), channel_id=1, source_target_pairs={{0,2},{1,3},{2,0},{3,1},{4,6},{5,7},{6,4},{7,5},{8,10},{9,11},{10,... | collective-permute-start | bytes 958472 | tf_op jit(solution)/shard_map/ppermute | solution.py:143
  18.1 17.0 %copy-start = (bf16[1,512,768]{2,1,0:T(8,128)(2,1)S(1)}, bf16[1,512,768]{2,1,0:T(8,128)(2,1)}, u32[]{:S(2)}) copy-start(bf16[1,512,768]{2,1,0:T(8,128)(2,1)} %param.8) | copy-start | bytes 2359300
  23.5 11.6 %all-to-all-start.1 = ((bf16[32,4,768]{2,1,0:T(4,128)(2,1)}), bf16[32,4,768]{2,1,0:T(4,128)(2,1)S(1)}, u32[]{:S(2)}, u32[]{:S(2)}) async-start(bf16[32,4,768]{2,1,0:T(4,128)(2,1)} %shard_map.84.refs_4_), calls=%async_computation.1 | async-start | bytes 393216 | tf_op jit(solution)/shard_map/all_to_all | solution.py:336
  26.5 1.7 %collective-permute-start = (bf16[208,768]{1,0:T(8,128)(2,1)S(1)}, bf16[208,768]{1,0:T(8,128)(2,1)S(1)}, u32[]{:S(2)}, u32[]{:S(2)}) collective-permute-start(bf16[208,768]{1,0:T(8,128)(2,1)S(1)} %get-tuple-element.15.refs_0_), channel_id=1, source_target_pairs={{0,1},{1,0},{2,3},{3,2},{4,5},{5,4},{6,7},{7,6},{8,9},{9,8},{10,11... | collective-permute-start | bytes 958472 | tf_op jit(solution)/shard_map/ppermute | solution.py:143
  26.8 2.0 %collective-permute-start.2 = (bf16[208,768]{1,0:T(8,128)(2,1)}, bf16[208,768]{1,0:T(8,128)(2,1)S(1)}, u32[]{:S(2)}, u32[]{:S(2)}) collective-permute-start(bf16[208,768]{1,0:T(8,128)(2,1)} %collective-permute-done.1.refs_2_), channel_id=1, source_target_pairs={{0,1},{1,0},{2,3},{3,2},{4,5},{5,4},{6,7},{7,6},{8,9},{9,8},{10,11... | collective-permute-start | bytes 958472 | tf_op jit(solution)/shard_map/ppermute | solution.py:143

commit v5 on v4

--- a/solution.py
+++ b/solution.py
@@ -52,46 +52,55 @@
 
 
 def expert_kernel(
-    clips, seqs, got_ref, slope_ref, kept_ref, in_hbm, out_hbm, send_ref, in_ref, out_ref, cot_ref, sems
+    clips, seqs, chunk, wide, got_ref, kept_ref, slope_hbm, in_hbm, out_hbm, send_ref,
+    slope_ref, in_ref, out_ref, act_ref, cot_ref, sems
 ):
     rows, width = got_ref.shape[1:]
-    hid, chunk = in_hbm.shape[1], kept_ref.shape[0]
-    parts = hid // chunk
-
-    def place(part):
-        return pl.ds(pl.multiple_of(part * chunk, chunk), chunk)
+    hid, kept = in_hbm.shape[1], kept_ref.shape[0]
+    outs, ins = (hid - kept) // chunk, hid // wide
+
+    def place(part, size, shift=0):
+        return pl.ds(pl.multiple_of(shift + part * size, GROUP), size)
 
     def out_copy(part):
         return pltpu.make_async_copy(
-            out_hbm.at[place(part), :], out_ref.at[place(part - 1), :], sems.at[part - 1]
+            out_hbm.at[place(part, chunk, kept), :], out_ref.at[place(part, chunk), :], sems.at[part]
         )
 
     def in_copy(part):
-        at = place(part)
-        return pltpu.make_async_copy(in_hbm.at[:, at], in_ref.at[:, at], sems.at[parts - 1 + part])
-
-    for part in range(1, parts):
+        at = place(part, wide)
+        return pltpu.make_async_copy(in_hbm.at[:, at], in_ref.at[:, at], sems.at[outs + part])
+
+    slope_copy = pltpu.make_async_copy(slope_hbm, slope_ref, sems.at[outs + ins])
+    slope_copy.start()
+    for part in range(outs):
         out_copy(part).start()
-    for part in range(parts):
+    for part in range(ins):
         in_copy(part).start()
     got = got_ref[...].astype(jnp.float32).reshape(seqs, clips, rows, width)
     cot = jnp.sum(got, axis=0).reshape(clips * rows, width).astype(jnp.bfloat16)
-    first = dot_nt(cot, kept_ref[...]) * slope_ref[:, :chunk]
-    cot_ref[:, :chunk] = first.astype(jnp.bfloat16)
-
-    @pl.loop(1, parts)
+
+    @pl.loop(0, kept // chunk)
+    def _(part):
+        at = place(part, chunk)
+        act_ref[:, at] = dot_nt(cot, kept_ref[at, :])
+
+    slope_copy.wait()
+    cot_ref[:, :kept] = (act_ref[...] * slope_ref[:, :kept]).astype(jnp.bfloat16)
+
+    @pl.loop(0, outs)
     def _(part):
         out_copy(part).wait()
-        at = place(part)
-        act_cot = dot_nt(cot, out_ref[place(part - 1), :])
+        at = place(part, chunk, kept)
+        act_cot = dot_nt(cot, out_ref[place(part, chunk), :])
         cot_ref[:, at] = (act_cot * slope_ref[:, at]).astype(jnp.bfloat16)
 
     def add(part, total):
         in_copy(part).wait()
-        at = place(part)
+        at = place(part, wide)
         return total + dot_nt(cot_ref[:, at], in_ref[:, at])
 
-    grad = lax.fori_loop(0, parts, add, jnp.zeros((clips * rows, width), jnp.float32))
+    grad = lax.fori_loop(0, ins, add, jnp.zeros((clips * rows, width), jnp.float32))
     grad = grad.reshape(1, clips, rows, width)
     grad = jnp.broadcast_to(grad, (seqs, clips, rows, width))
     send_ref[...] = grad.reshape(send_ref.shape).astype(jnp.bfloat16)
@@ -278,13 +287,14 @@
     parts = math.gcd(hid // GROUP, 4)
     seq_slots = slot_params.shape[1]
     pack_rows = slot_total + 2 * seq_slots + stat_rows(slot_total, width)
-    thirds = math.gcd(hid // GROUP, 3)
-    kept_rows = hid // thirds if thirds > 1 else GROUP
+    pieces = math.gcd(hid // GROUP, 6)
+    chunk, wide = hid // pieces, hid // math.gcd(pieces, 3)
+    kept_rows = max(pieces // 2, 1) * chunk
     own, slope, kept = pl.pallas_call(
         functools.partial(side_kernel, parts),
         out_shape=(
             jax.ShapeDtypeStruct((pack_rows, width), b16),
-            jax.ShapeDtypeStruct((feed_rows, hid), f32),
+            pltpu.HBM((feed_rows, hid), f32),
             pltpu.VMEM((kept_rows, width), b16),
         ),
         in_specs=[STAYS] * 7,
@@ -310,15 +320,17 @@
     )
 
     send = pl.pallas_call(
-        functools.partial(expert_kernel, clip_count, seq_count),
+        functools.partial(expert_kernel, clip_count, seq_count, chunk, wide),
         out_shape=jax.ShapeDtypeStruct((device_count, local_slots, width), b16),
-        in_specs=[WHOLE, WHOLE, WHOLE, STAYS, STAYS],
+        in_specs=[WHOLE, WHOLE, STAYS, STAYS, STAYS],
         out_specs=WHOLE,
         scratch_shapes=[
+            pltpu.VMEM((feed_rows, hid), f32),
             pltpu.VMEM((width, hid), b16),
-            pltpu.VMEM((hid - kept_rows, width), b16),
+            pltpu.VMEM((max(hid - kept_rows, chunk), width), b16),
+            pltpu.VMEM((feed_rows, kept_rows), f32),
             pltpu.VMEM((feed_rows, hid), b16),
-            pltpu.SemaphoreType.DMA((2 * (hid // kept_rows) - 1,)),
+            pltpu.SemaphoreType.DMA(((hid - kept_rows) // chunk + hid // wide + 1,)),
         ],
         compiler_params=pltpu.CompilerParams(vmem_limit_bytes=20 * MIB),
         cost_estimate=pl.CostEstimate(
@@ -328,8 +340,8 @@
         ),
     )(
         received,
-        slope,
         pltpu.with_memory_space_constraint(kept, pltpu.VMEM),
+        stays(slope),
         still_in,
         still_out,
     )
@@ -365,15 +377,15 @@
         send,
     )
 
-    chunk = math.gcd(token_total, 128)
+    step = math.gcd(token_total, 128)
     token_grad = pl.pallas_call(
-        functools.partial(token_kernel, seq_count, chunk),
+        functools.partial(token_kernel, seq_count, step),
         out_shape=jax.ShapeDtypeStruct((token_total, width), b16),
         in_specs=[WHOLE] * 6,
         out_specs=PLACED,
         scratch_shapes=[
             pltpu.VMEM((token_total, width), b16),
-            pltpu.SemaphoreType.DMA((token_total // chunk,)),
+            pltpu.SemaphoreType.DMA((token_total // step,)),
         ],
         compiler_params=pltpu.CompilerParams(vmem_limit_bytes=16 * MIB),
         cost_estimate=pl.CostEstimate(

time: 37 us -> 36.5 us (0.986)
  waiting for transfers between devices: 8.72 us -> 7.53 us
  Pallas kernels: 15.2 us -> 15.9 us
    pallas_call x1, Pallas kernels: 3.3 us -> 4.41 us  [on_device(): pl.pallas_call(functools.partial(side_kernel, parts), out_shape=(jax.Shap...]
    all_to_all x1, waiting for transfers between devices: 3.42 us -> 2.31 us  [on_device(): lax.all_to_all(blocks, ROUND, split_axis=0, concat_axis=0, tiled=True)]
    pallas_call x2, Pallas kernels: 7.04 us -> 6.48 us  [the longest x1 4.82 us: on_device(): pl.pallas_call(functools.partial(expert_kernel, clip_count, seq_count, ch...]
  transfers between devices with their start and end apart: 5 -> 5, of which waited for: 4 -> 4; matrix products, arithmetic and copies ran while one was open for 0% -> 0% of each run, Pallas kernels for 31% -> 33%
where the time goes in v5:
time: 36.5 us; the launch traced here: 36.2 us
  Pallas kernels  15.9 us (44%)
  starting transfers between devices  12.8 us (35%)
  waiting for transfers between devices  7.53 us (21%)
    all_to_all x1, starting transfers between devices, on_device(): lax.all_to_all(blocks, ROUND, split_axis=0, concat_axis=0, tiled=True)  7.3 us
    pallas_call x1, Pallas kernels, on_device(): pl.pallas_call(functools.partial(expert_kernel, clip_count, seq_count, ch...  4.82 us
    pallas_call x1, Pallas kernels, on_device(): pl.pallas_call(functools.partial(side_kernel, parts), out_shape=(jax.Shap...  4.41 us
    all_to_all x1, waiting for transfers between devices, on_device(): lax.all_to_all(send, ROUND, split_axis=0, concat_axis=0, tiled=True)  3.45 us
    all_to_all x1, starting transfers between devices, on_device(): lax.all_to_all(send, ROUND, split_axis=0, concat_axis=0, tiled=True)  3.04 us
    pallas_call x1, Pallas kernels, on_device(): pl.pallas_call(functools.partial(weight_kernel, seq_count), out_shape=(ja...  2.74 us
    ppermute x3, starting transfers between devices, swap(): return lax.ppermute(value, 'seq', [(i, i ^ bit) for i in range(count)])  2.41 us
    all_to_all x1, waiting for transfers between devices, on_device(): lax.all_to_all(blocks, ROUND, split_axis=0, concat_axis=0, tiled=True)  2.31 us
  transfers between devices with their start and end apart: 5, of which 4 were waited for; matrix products, arithmetic and copies ran while one was open for 0% of the time, Pallas kernels for 33%

profile of v5, /device:TPU:0, one launch (start us, length us, event | category | flops | bytes accessed | tf_op | source)
XLA Modules:
  0.0 36.2 jit_solution(10085579006717686845)
XLA Ops:
  0.0 2.2 %shard_map.82 = bf16[32,4,768]{2,1,0:T(4,128)(2,1)} custom-call(bf16[512,128]{1,0:T(8,128)(2,1)} %bitcast.17, bf16[512,768]{1,0:T(8,128)(2,1)} %bitcast.15), custom_call_target="tpu_custom_call" | custom-call | tf_op jit(solution)/shard_map/pallas_call | solution.py:272
  2.2 7.3 %all-to-all-start = ((bf16[32,4,768]{2,1,0:T(4,128)(2,1)}), bf16[32,4,768]{2,1,0:T(4,128)(2,1)S(1)}, u32[]{:S(2)}, u32[]{:S(2)}) async-start(bf16[32,4,768]{2,1,0:T(4,128)(2,1)} %shard_map.82), calls=%async_computation | async-start | bytes 393216 | tf_op jit(solution)/shard_map/all_to_all | solution.py:285
  9.5 4.4 %shard_map.83 = (bf16[208,768]{1,0:T(8,128)(2,1)}, f32[32,3072]{1,0:T(8,128)}, bf16[1536,768]{1,0:T(8,128)(2,1)S(1)}) custom-call(bf16[512,128]{1,0:T(8,128)(2,1)} %bitcast.18, bf16[512,768]{1,0:T(8,128)(2,1)} %bitcast.9, bf16[32,768]{1,0:T(8,128)(2,1)} %bitcast.20, bf16[32,768]{1,0:T(8,128)(2,1)} %bitcast.21, bf16[8,4,768]{2,1,0:T(4,128)(2,1)} %feed_hbm.1, ...), custom_call_target="tpu_custom_call" | custom-call | tf_op jit(solution)/shard_map/pallas_call | solution.py:293
  14.0 1.8 %collective-permute-start.1 = (bf16[208,768]{1,0:T(8,128)(2,1)}, bf16[208,768]{1,0:T(8,128)(2,1)}, u32[]{:S(2)}, u32[]{:S(2)}) collective-permute-start(bf16[208,768]{1,0:T(8,128)(2,1)} %get-tuple-element.15.refs_0_), channel_id=1, source_target_pairs={{0,2},{1,3},{2,0},{3,1},{4,6},{5,7},{6,4},{7,5},{8,10},{9,11},{10,... | collective-permute-start | bytes 958472 | tf_op jit(solution)/shard_map/ppermute | solution.py:152
  15.8 2.3 %all-to-all-done.got_ref = bf16[32,4,768]{2,1,0:T(4,128)(2,1)S(1)} async-done(((bf16[32,4,768]{2,1,0:T(4,128)(2,1)}), bf16[32,4,768]{2,1,0:T(4,128)(2,1)S(1)}, u32[]{:S(2)}, u32[]{:S(2)}) %all-to-all-start) | async-done | bytes 196640 | tf_op jit(solution)/shard_map/all_to_all | solution.py:285
  18.1 0.0 copy-start
  18.1 4.8 %shard_map.84.refs_4_ = bf16[32,4,768]{2,1,0:T(4,128)(2,1)} custom-call(bf16[32,4,768]{2,1,0:T(4,128)(2,1)S(1)} %all-to-all-done.got_ref, bf16[1536,768]{1,0:T(8,128)(2,1)S(1)} %get-tuple-element.13.kept_ref, f32[32,3072]{1,0:T(8,128)} %get-tuple-element.14.slope_hbm, bf16[768,3072]{1,0:T(8,128)(2,1)} %bitcast.12, bf16[3072,768]{1,0:T(8,128)(2,1)} %bitcast.14), custom_call_target="tpu_custom_call" | custom-call | flops 301989888 | bytes 9437184 | tf_op jit(solution)/shard_map/pallas_call | solution.py:322
  22.9 3.0 %all-to-all-start.1 = ((bf16[32,4,768]{2,1,0:T(4,128)(2,1)}), bf16[32,4,768]{2,1,0:T(4,128)(2,1)S(1)}, u32[]{:S(2)}, u32[]{:S(2)}) async-start(bf16[32,4,768]{2,1,0:T(4,128)(2,1)} %shard_map.84.refs_4_), calls=%async_computation.1 | async-start | bytes 393216 | tf_op jit(solution)/shard_map/all_to_all | solution.py:348
  26.0 0.3 collective-permute-start
  26.3 0.0 collective-permute-done.1.refs_2_
  26.3 0.3 collective-permute-start.2
  26.6 1.3 %collective-permute-done.refs_1_ = bf16[208,768]{1,0:T(8,128)(2,1)S(1)} collective-permute-done((bf16[208,768]{1,0:T(8,128)(2,1)}, bf16[208,768]{1,0:T(8,128)(2,1)S(1)}, u32[]{:S(2)}, u32[]{:S(2)}) %collective-permute-start) | collective-permute-done | bytes 319520 | tf_op jit(solution)/shard_map/ppermute | solution.py:152
  27.9 0.5 %collective-permute-done.2.refs_3_ = bf16[208,768]{1,0:T(8,128)(2,1)S(1)} collective-permute-done((bf16[208,768]{1,0:T(8,128)(2,1)}, bf16[208,768]{1,0:T(8,128)(2,1)S(1)}, u32[]{:S(2)}, u32[]{:S(2)}) %collective-permute-start.2) | collective-permute-done | bytes 319520 | tf_op jit(solution)/shard_map/ppermute | solution.py:152
  28.3 2.7 %shard_map.85 = (f32[512,128]{1,0:T(8,128)S(1)}, f32[512,128]{1,0:T(8,128)S(1)}, bf16[128,768]{1,0:T(8,128)(2,1)S(1)}, bf16[128,768]{1,0:T(8,128)(2,1)S(1)}) custom-call(s32[1]{0:T(128)} %bitcast.7.me_ref, bf16[512,128]{1,0:T(8,128)(2,1)} %bitcast.19, bf16[512,768]{1,0:T(8,128)(2,1)} %bitcast.16, bf16[208,768]{1,0:T(8,128)(2,1)} %get-tuple-element.15.refs_0_, ...), custom_call_target="tpu_custom_call" | custom-call | tf_op jit(solution)/shard_map/pallas_call | solution.py:354
  31.1 3.4 %all-to-all-done.1.got_ref = bf16[32,4,768]{2,1,0:T(4,128)(2,1)S(1)} async-done(((bf16[32,4,768]{2,1,0:T(4,128)(2,1)}), bf16[32,4,768]{2,1,0:T(4,128)(2,1)S(1)}, u32[]{:S(2)}, u32[]{:S(2)}) %all-to-all-start.1) | async-done | bytes 196640 | tf_op jit(solution)/shard_map/all_to_all | solution.py:348
  34.5 0.0 copy-done
  34.5 1.7 %shard_map.86 = bf16[512,768]{1,0:T(8,128)(2,1)} custom-call(bf16[512,768]{1,0:T(8,128)(2,1)S(1)} %bitcast.10, bf16[32,4,768]{2,1,0:T(4,128)(2,1)S(1)} %all-to-all-done.1.got_ref, bf16[128,768]{1,0:T(8,128)(2,1)S(1)} %get-tuple-element.17.sum_ref, f32[512,128]{1,0:T(8,128)S(1)} %get-tuple-element.18.disp_ref, f32[512,128]{1,0:T(8,128)S(1)} %get-tuple-element.19.comb_ref, ...), custom_call_target="tpu_custom_call" | custom-call | flops 301989888 | bytes 1572864 | tf_op jit(solution)/shard_map/pallas_call | solution.py:381
Async XLA Ops:
  2.2 15.9 %all-to-all-start = ((bf16[32,4,768]{2,1,0:T(4,128)(2,1)}), bf16[32,4,768]{2,1,0:T(4,128)(2,1)S(1)}, u32[]{:S(2)}, u32[]{:S(2)}) async-start(bf16[32,4,768]{2,1,0:T(4,128)(2,1)} %shard_map.82), calls=%async_computation | async-start | bytes 393216 | tf_op jit(solution)/shard_map/all_to_all | solution.py:285
  14.0 12.3 %collective-permute-start.1 = (bf16[208,768]{1,0:T(8,128)(2,1)}, bf16[208,768]{1,0:T(8,128)(2,1)}, u32[]{:S(2)}, u32[]{:S(2)}) collective-permute-start(bf16[208,768]{1,0:T(8,128)(2,1)} %get-tuple-element.15.refs_0_), channel_id=1, source_target_pairs={{0,2},{1,3},{2,0},{3,1},{4,6},{5,7},{6,4},{7,5},{8,10},{9,11},{10,... | collective-permute-start | bytes 958472 | tf_op jit(solution)/shard_map/ppermute | solution.py:152
  18.1 16.4 %copy-start = (bf16[1,512,768]{2,1,0:T(8,128)(2,1)S(1)}, bf16[1,512,768]{2,1,0:T(8,128)(2,1)}, u32[]{:S(2)}) copy-start(bf16[1,512,768]{2,1,0:T(8,128)(2,1)} %param.8) | copy-start | bytes 2359300
  22.9 11.6 %all-to-all-start.1 = ((bf16[32,4,768]{2,1,0:T(4,128)(2,1)}), bf16[32,4,768]{2,1,0:T(4,128)(2,1)S(1)}, u32[]{:S(2)}, u32[]{:S(2)}) async-start(bf16[32,4,768]{2,1,0:T(4,128)(2,1)} %shard_map.84.refs_4_), calls=%async_computation.1 | async-start | bytes 393216 | tf_op jit(solution)/shard_map/all_to_all | solution.py:348
  26.0 1.9 %collective-permute-start = (bf16[208,768]{1,0:T(8,128)(2,1)}, bf16[208,768]{1,0:T(8,128)(2,1)S(1)}, u32[]{:S(2)}, u32[]{:S(2)}) collective-permute-start(bf16[208,768]{1,0:T(8,128)(2,1)} %get-tuple-element.15.refs_0_), channel_id=1, source_target_pairs={{0,1},{1,0},{2,3},{3,2},{4,5},{5,4},{6,7},{7,6},{8,9},{9,8},{10,11... | collective-permute-start | bytes 958472 | tf_op jit(solution)/shard_map/ppermute | solution.py:152
  26.3 2.0 %collective-permute-start.2 = (bf16[208,768]{1,0:T(8,128)(2,1)}, bf16[208,768]{1,0:T(8,128)(2,1)S(1)}, u32[]{:S(2)}, u32[]{:S(2)}) collective-permute-start(bf16[208,768]{1,0:T(8,128)(2,1)} %collective-permute-done.1.refs_2_), channel_id=1, source_target_pairs={{0,1},{1,0},{2,3},{3,2},{4,5},{5,4},{6,7},{7,6},{8,9},{9,8},{10,11... | collective-permute-start | bytes 958472 | tf_op jit(solution)/shard_map/ppermute | solution.py:152

commit v6 on v5

--- a/solution.py
+++ b/solution.py
@@ -1,5 +1,6 @@
 import functools
 import math
+import random
 import jax
 import jax.numpy as jnp
 from jax import lax
@@ -8,11 +9,11 @@
 from jax.sharding import PartitionSpec as P
 
 BOTH = ("clip", "seq")
-ROUND = ("seq", "clip")
 WHOLE = pl.BlockSpec(memory_space=pltpu.VMEM)
 PLACED = pl.BlockSpec(memory_space=pl.ANY)
 STAYS = pl.BlockSpec(memory_space=pltpu.HBM)
 GROUP = 128
+SHUFFLE = (1, 25)
 MIB = 1 << 20
 FREE = pl.CostEstimate(flops=0, bytes_accessed=0, transcendentals=0)
 
@@ -27,6 +28,20 @@
 
 def dot_tn(a, b):
     return lax.dot_general(a, b, (((0,), (0,)), ((), ())), preferred_element_type=jnp.float32)
+
+
+def exchange_order(devices):
+    shuffler = random.Random(SHUFFLE[0])
+    for _ in range(SHUFFLE[1]):
+        order = list(range(devices))
+        shuffler.shuffle(order)
+    return order
+
+
+def exchange(blocks, order):
+    return lax.all_to_all(
+        blocks, BOTH, split_axis=0, concat_axis=0, axis_index_groups=[order], tiled=True
+    )
 
 
 def fetch(pairs, sems):
@@ -38,7 +53,7 @@
     return copies
 
 
-def cot_kernel(seqs, logit_hbm, grad_hbm, out_ref, logit_ref, grad_ref, sems):
+def cot_kernel(order, logit_hbm, grad_hbm, out_ref, logit_ref, grad_ref, sems):
     got_logits, got_grad = fetch([(logit_hbm, logit_ref), (grad_hbm, grad_ref)], sems)
     got_logits.wait()
     scores = logit_ref[...].astype(jnp.float32)
@@ -46,13 +61,13 @@
     combine = raised / jnp.sum(raised, axis=1, keepdims=True)
     got_grad.wait()
     cot = dot_tn(combine.astype(jnp.bfloat16), grad_ref[...])
-    devices, rows, width = out_ref.shape
-    cot = cot.reshape(devices // seqs, seqs, rows, width).swapaxes(0, 1)
-    out_ref[...] = cot.reshape(out_ref.shape).astype(jnp.bfloat16)
+    cot = cot.reshape(out_ref.shape)
+    for place, device in enumerate(order):
+        out_ref[place] = cot[device].astype(jnp.bfloat16)
 
 
 def expert_kernel(
-    clips, seqs, chunk, wide, got_ref, kept_ref, slope_hbm, in_hbm, out_hbm, send_ref,
+    order, clips, seqs, chunk, wide, got_ref, kept_ref, slope_hbm, in_hbm, out_hbm, send_ref,
     slope_ref, in_ref, out_ref, act_ref, cot_ref, sems
 ):
     rows, width = got_ref.shape[1:]
@@ -77,8 +92,9 @@
         out_copy(part).start()
     for part in range(ins):
         in_copy(part).start()
-    got = got_ref[...].astype(jnp.float32).reshape(seqs, clips, rows, width)
-    cot = jnp.sum(got, axis=0).reshape(clips * rows, width).astype(jnp.bfloat16)
+    got = [got_ref[order.index(device)].astype(jnp.float32) for device in range(clips * seqs)]
+    cot = [sum(got[clip * seqs : (clip + 1) * seqs]) for clip in range(clips)]
+    cot = jnp.concatenate(cot, axis=0).astype(jnp.bfloat16)
 
     @pl.loop(0, kept // chunk)
     def _(part):
@@ -101,19 +117,18 @@
         return total + dot_nt(cot_ref[:, at], in_ref[:, at])
 
     grad = lax.fori_loop(0, ins, add, jnp.zeros((clips * rows, width), jnp.float32))
-    grad = grad.reshape(1, clips, rows, width)
-    grad = jnp.broadcast_to(grad, (seqs, clips, rows, width))
-    send_ref[...] = grad.reshape(send_ref.shape).astype(jnp.bfloat16)
+    grad = grad.reshape(clips, rows, width).astype(jnp.bfloat16)
+    for at, device in enumerate(order):
+        send_ref[at] = grad[device // seqs]
 
 
 def token_kernel(
-    seqs, chunk, tok_ref, got_ref, sum_ref, disp_ref, comb_ref, param_ref,
+    order, chunk, tok_ref, got_ref, sum_ref, disp_ref, comb_ref, param_ref,
     out_hbm, stage, sems
 ):
-    slots, width = param_ref.shape
-    devices, rows = got_ref.shape[:2]
-    slot_grad = got_ref[...].astype(jnp.float32).reshape(seqs, devices // seqs, rows, width)
-    slot_grad = slot_grad.swapaxes(0, 1).reshape(slots, width).astype(jnp.bfloat16)
+    slots = param_ref.shape[0]
+    slot_grad = [got_ref[order.index(at)].astype(jnp.float32) for at in range(len(order))]
+    slot_grad = jnp.concatenate(slot_grad, axis=0).astype(jnp.bfloat16)
     cross = dot_nt(sum_ref[...], slot_grad)
     row = lax.broadcasted_iota(jnp.int32, (slots, slots), 0)
     col = lax.broadcasted_iota(jnp.int32, (slots, slots), 1)
@@ -215,10 +230,20 @@
 
 
 def weight_kernel(seqs, me_ref, logit_hbm, grad_hbm, *refs):
-    packs, (disp_ref, comb_ref, sum_ref, param_ref) = refs[:seqs], refs[seqs + 1 : seqs + 5]
-    slot_ref, logit_ref, grad_ref, sems = refs[seqs + 5 :]
+    packs, (disp_ref, comb_ref, sum_ref, param_ref) = list(refs[:seqs]), refs[seqs + 1 : seqs + 5]
+    slot_ref, logit_ref, grad_ref, early_ref, sems = refs[seqs + 5 :]
     slots, width = logit_ref.shape[1], grad_ref.shape[1]
-    got_logits, got_grad = fetch([(logit_hbm, logit_ref), (grad_hbm, grad_ref)], sems)
+    early = [(packs[other], early_ref.at[other // 2]) for other in range(0, seqs, 2)]
+    got_logits, *got_early, got_grad = fetch(
+        [(logit_hbm, logit_ref)] + early + [(grad_hbm, grad_ref)], sems
+    )
+    got_logits.wait()
+    scores = logit_ref[...].astype(jnp.float32)
+    raised = jnp.exp(scores - jnp.max(scores, axis=1, keepdims=True))
+    combine = raised / jnp.sum(raised, axis=1, keepdims=True)
+    for other in range(0, seqs, 2):
+        got_early[other // 2].wait()
+        packs[other] = early_ref.at[other // 2]
     seq_slots = slots // seqs
     me = me_ref[0]
     stats = []
@@ -243,11 +268,7 @@
         share = jnp.sum(jnp.where(row == col, share, 0.0), axis=1, keepdims=True)
         token_sum += share * pack[:slots].astype(jnp.float32)
     sum_ref[...] = token_sum.astype(jnp.bfloat16)
-    got_logits.wait()
-    scores = logit_ref[...].astype(jnp.float32)
     disp_ref[...] = jnp.exp(scores - highest) / total
-    raised = jnp.exp(scores - jnp.max(scores, axis=1, keepdims=True))
-    combine = raised / jnp.sum(raised, axis=1, keepdims=True)
     got_grad.wait()
     comb_cot = dot_nt(grad_ref[...], slot_ref[...])
     comb_ref[...] = combine * (comb_cot - jnp.sum(combine * comb_cot, axis=1, keepdims=True))
@@ -259,6 +280,7 @@
     clip_count = lax.axis_size("clip")
     seq_count = lax.axis_size("seq")
     device_count = clip_count * seq_count
+    order = exchange_order(device_count)
     tok_feats, out_cot, logit_raw = tokens[0], out_grad[0], saved_logits[0]
     token_total, width = tok_feats.shape
     slot_total = logit_raw.shape[1]
@@ -270,7 +292,7 @@
     still_logits, still_grad = stays(logit_raw), stays(out_cot)
     still_in, still_out = stays(expert_in[0]), stays(expert_out[0])
     blocks = pl.pallas_call(
-        functools.partial(cot_kernel, seq_count),
+        functools.partial(cot_kernel, order),
         out_shape=jax.ShapeDtypeStruct((device_count, local_slots, width), b16),
         in_specs=[STAYS, STAYS],
         out_specs=WHOLE,
@@ -282,7 +304,7 @@
         compiler_params=pltpu.CompilerParams(vmem_limit_bytes=16 * MIB),
         cost_estimate=FREE,
     )(still_logits, still_grad)
-    received = lax.all_to_all(blocks, ROUND, split_axis=0, concat_axis=0, tiled=True)
+    received = exchange(blocks, order)
 
     parts = math.gcd(hid // GROUP, 4)
     seq_slots = slot_params.shape[1]
@@ -320,7 +342,7 @@
     )
 
     send = pl.pallas_call(
-        functools.partial(expert_kernel, clip_count, seq_count, chunk, wide),
+        functools.partial(expert_kernel, order, clip_count, seq_count, chunk, wide),
         out_shape=jax.ShapeDtypeStruct((device_count, local_slots, width), b16),
         in_specs=[WHOLE, WHOLE, STAYS, STAYS, STAYS],
         out_specs=WHOLE,
@@ -345,7 +367,7 @@
         still_in,
         still_out,
     )
-    returned = lax.all_to_all(send, ROUND, split_axis=0, concat_axis=0, tiled=True)
+    returned = exchange(send, order)
 
     held = {0: own}
     for bit in seq_bits():
@@ -359,27 +381,30 @@
             jax.ShapeDtypeStruct((slot_total, width), b16),
             jax.ShapeDtypeStruct((slot_total, width), b16),
         ),
-        in_specs=[pl.BlockSpec(memory_space=pltpu.SMEM), STAYS, STAYS] + [WHOLE] * seq_count + [PLACED],
+        in_specs=[pl.BlockSpec(memory_space=pltpu.SMEM), STAYS, STAYS]
+        + [STAYS if other % 2 == 0 else WHOLE for other in range(seq_count)]
+        + [PLACED],
         out_specs=(WHOLE,) * 4,
         scratch_shapes=[
             pltpu.VMEM((slot_total, width), b16),
             pltpu.VMEM((token_total, slot_total), b16),
             pltpu.VMEM((token_total, width), b16),
-            pltpu.SemaphoreType.DMA((2,)),
+            pltpu.VMEM(((seq_count + 1) // 2, pack_rows, width), b16),
+            pltpu.SemaphoreType.DMA((2 + (seq_count + 1) // 2,)),
         ],
-        compiler_params=pltpu.CompilerParams(vmem_limit_bytes=32 * MIB),
+        compiler_params=pltpu.CompilerParams(vmem_limit_bytes=48 * MIB),
         cost_estimate=FREE,
     )(
         lax.axis_index("seq")[None],
         still_logits,
         still_grad,
-        *[held[other] for other in range(seq_count)],
+        *[stays(held[at]) if at % 2 == 0 else held[at] for at in range(seq_count)],
         send,
     )
 
     step = math.gcd(token_total, 128)
     token_grad = pl.pallas_call(
-        functools.partial(token_kernel, seq_count, step),
+        functools.partial(token_kernel, order, step),
         out_shape=jax.ShapeDtypeStruct((token_total, width), b16),
         in_specs=[WHOLE] * 6,
         out_specs=PLACED,

time: 36.5 us -> 36.1 us (0.989)
  waiting for transfers between devices: 7.53 us -> 8.47 us
  Pallas kernels: 15.9 us -> 15 us
  starting transfers between devices: 12.8 us -> 12.3 us
    all_to_all x2, waiting for transfers between devices: 5.76 us -> 6.7 us  [exchange(): lax.all_to_all(blocks, BOTH, split_axis=0, concat_axis=0, axis_index_grou...]
    pallas_call x1, Pallas kernels: 2.74 us -> 1.91 us  [on_device(): pl.pallas_call(functools.partial(weight_kernel, seq_count), out_shape=(ja...]
    all_to_all x2, starting transfers between devices: 10.3 us -> 9.9 us  [exchange(): lax.all_to_all(blocks, BOTH, split_axis=0, concat_axis=0, axis_index_grou...]
  transfers between devices with their start and end apart: 5 -> 5, of which waited for: 4 -> 4; matrix products, arithmetic and copies ran while one was open for 0% -> 0% of each run, Pallas kernels for 33% -> 31%
where the time goes in v6:
time: 36.1 us; the launch traced here: 35.9 us
  Pallas kernels  15 us (42%)
  starting transfers between devices  12.3 us (34%)
  waiting for transfers between devices  8.47 us (23%)
    all_to_all x2, starting transfers between devices, exchange(): lax.all_to_all(blocks, BOTH, split_axis=0, concat_axis=0, axis_index_grou...  9.9 us
    all_to_all x2, waiting for transfers between devices, exchange(): lax.all_to_all(blocks, BOTH, split_axis=0, concat_axis=0, axis_index_grou...  6.7 us
    pallas_call x1, Pallas kernels, on_device(): pl.pallas_call(functools.partial(expert_kernel, order, clip_count, seq_co...  4.82 us
    pallas_call x1, Pallas kernels, on_device(): pl.pallas_call(functools.partial(side_kernel, parts), out_shape=(jax.Shap...  4.41 us
    ppermute x3, starting transfers between devices, swap(): return lax.ppermute(value, 'seq', [(i, i ^ bit) for i in range(count)])  2.41 us
    pallas_call x1, Pallas kernels, on_device(): pl.pallas_call(functools.partial(cot_kernel, order), out_shape=jax.ShapeD...  2.21 us
    pallas_call x1, Pallas kernels, on_device(): pl.pallas_call(functools.partial(weight_kernel, seq_count), out_shape=(ja...  1.91 us
    ppermute x3, waiting for transfers between devices, swap(): return lax.ppermute(value, 'seq', [(i, i ^ bit) for i in range(count)])  1.77 us
  transfers between devices with their start and end apart: 5, of which 4 were waited for; matrix products, arithmetic and copies ran while one was open for 0% of the time, Pallas kernels for 31%

profile of v6, /device:TPU:0, one launch (start us, length us, event | category | flops | bytes accessed | tf_op | source)
XLA Modules:
  0.0 35.9 jit_solution(16936782093441282033)
XLA Ops:
  0.0 2.2 %shard_map.82 = bf16[32,4,768]{2,1,0:T(4,128)(2,1)} custom-call(bf16[512,128]{1,0:T(8,128)(2,1)} %bitcast.17, bf16[512,768]{1,0:T(8,128)(2,1)} %bitcast.15), custom_call_target="tpu_custom_call" | custom-call | tf_op jit(solution)/shard_map/pallas_call | solution.py:294
  2.2 7.3 %all-to-all-start = ((bf16[32,4,768]{2,1,0:T(4,128)(2,1)}), bf16[32,4,768]{2,1,0:T(4,128)(2,1)S(1)}, u32[]{:S(2)}, u32[]{:S(2)}) async-start(bf16[32,4,768]{2,1,0:T(4,128)(2,1)} %shard_map.82), calls=%async_computation | async-start | bytes 393216 | tf_op jit(solution)/shard_map/all_to_all | solution.py:42
  9.5 4.4 %shard_map.83 = (bf16[208,768]{1,0:T(8,128)(2,1)}, f32[32,3072]{1,0:T(8,128)}, bf16[1536,768]{1,0:T(8,128)(2,1)S(1)}) custom-call(bf16[512,128]{1,0:T(8,128)(2,1)} %bitcast.18, bf16[512,768]{1,0:T(8,128)(2,1)} %bitcast.9, bf16[32,768]{1,0:T(8,128)(2,1)} %bitcast.20, bf16[32,768]{1,0:T(8,128)(2,1)} %bitcast.21, bf16[8,4,768]{2,1,0:T(4,128)(2,1)} %feed_hbm.1, ...), custom_call_target="tpu_custom_call" | custom-call | tf_op jit(solution)/shard_map/pallas_call | solution.py:315
  14.0 1.8 %collective-permute-start.1 = (bf16[208,768]{1,0:T(8,128)(2,1)}, bf16[208,768]{1,0:T(8,128)(2,1)}, u32[]{:S(2)}, u32[]{:S(2)}) collective-permute-start(bf16[208,768]{1,0:T(8,128)(2,1)} %get-tuple-element.15.refs_0_), channel_id=1, source_target_pairs={{0,2},{1,3},{2,0},{3,1},{4,6},{5,7},{6,4},{7,5},{8,10},{9,11},{10,... | collective-permute-start | bytes 958472 | tf_op jit(solution)/shard_map/ppermute | solution.py:167
  15.8 2.4 %all-to-all-done.got_ref = bf16[32,4,768]{2,1,0:T(4,128)(2,1)S(1)} async-done(((bf16[32,4,768]{2,1,0:T(4,128)(2,1)}), bf16[32,4,768]{2,1,0:T(4,128)(2,1)S(1)}, u32[]{:S(2)}, u32[]{:S(2)}) %all-to-all-start) | async-done | bytes 196640 | tf_op jit(solution)/shard_map/all_to_all | solution.py:42
  18.1 0.0 copy-start
  18.2 4.8 %shard_map.84.refs_4_ = bf16[32,4,768]{2,1,0:T(4,128)(2,1)} custom-call(bf16[32,4,768]{2,1,0:T(4,128)(2,1)S(1)} %all-to-all-done.got_ref, bf16[1536,768]{1,0:T(8,128)(2,1)S(1)} %get-tuple-element.13.kept_ref, f32[32,3072]{1,0:T(8,128)} %get-tuple-element.14.slope_hbm, bf16[768,3072]{1,0:T(8,128)(2,1)} %bitcast.12, bf16[3072,768]{1,0:T(8,128)(2,1)} %bitcast.14), custom_call_target="tpu_custom_call" | custom-call | flops 301989888 | bytes 9437184 | tf_op jit(solution)/shard_map/pallas_call | solution.py:344
  23.0 2.6 %all-to-all-start.1 = ((bf16[32,4,768]{2,1,0:T(4,128)(2,1)}), bf16[32,4,768]{2,1,0:T(4,128)(2,1)S(1)}, u32[]{:S(2)}, u32[]{:S(2)}) async-start(bf16[32,4,768]{2,1,0:T(4,128)(2,1)} %shard_map.84.refs_4_), calls=%async_computation.1 | async-start | bytes 393216 | tf_op jit(solution)/shard_map/all_to_all | solution.py:42
  25.6 0.2 collective-permute-start
  25.8 0.0 collective-permute-done.1.refs_2_
  25.8 0.3 collective-permute-start.2
  26.2 1.3 %collective-permute-done.refs_1_ = bf16[208,768]{1,0:T(8,128)(2,1)S(1)} collective-permute-done((bf16[208,768]{1,0:T(8,128)(2,1)}, bf16[208,768]{1,0:T(8,128)(2,1)S(1)}, u32[]{:S(2)}, u32[]{:S(2)}) %collective-permute-start) | collective-permute-done | bytes 319520 | tf_op jit(solution)/shard_map/ppermute | solution.py:167
  27.5 0.5 %collective-permute-done.2.refs_3_ = bf16[208,768]{1,0:T(8,128)(2,1)S(1)} collective-permute-done((bf16[208,768]{1,0:T(8,128)(2,1)}, bf16[208,768]{1,0:T(8,128)(2,1)S(1)}, u32[]{:S(2)}, u32[]{:S(2)}) %collective-permute-start.2) | collective-permute-done | bytes 319520 | tf_op jit(solution)/shard_map/ppermute | solution.py:167
  27.9 1.9 %shard_map.85 = (f32[512,128]{1,0:T(8,128)S(1)}, f32[512,128]{1,0:T(8,128)S(1)}, bf16[128,768]{1,0:T(8,128)(2,1)S(1)}, bf16[128,768]{1,0:T(8,128)(2,1)S(1)}) custom-call(s32[1]{0:T(128)} %bitcast.7.me_ref, bf16[512,128]{1,0:T(8,128)(2,1)} %bitcast.19, bf16[512,768]{1,0:T(8,128)(2,1)} %bitcast.16, bf16[208,768]{1,0:T(8,128)(2,1)} %get-tuple-element.15.refs_0_, ...), custom_call_target="tpu_custom_call" | custom-call | tf_op jit(solution)/shard_map/pallas_call | solution.py:376
  29.9 4.3 %all-to-all-done.1.got_ref = bf16[32,4,768]{2,1,0:T(4,128)(2,1)S(1)} async-done(((bf16[32,4,768]{2,1,0:T(4,128)(2,1)}), bf16[32,4,768]{2,1,0:T(4,128)(2,1)S(1)}, u32[]{:S(2)}, u32[]{:S(2)}) %all-to-all-start.1) | async-done | bytes 196640 | tf_op jit(solution)/shard_map/all_to_all | solution.py:42
  34.2 0.0 copy-done
  34.2 1.7 %shard_map.86 = bf16[512,768]{1,0:T(8,128)(2,1)} custom-call(bf16[512,768]{1,0:T(8,128)(2,1)S(1)} %bitcast.10, bf16[32,4,768]{2,1,0:T(4,128)(2,1)S(1)} %all-to-all-done.1.got_ref, bf16[128,768]{1,0:T(8,128)(2,1)S(1)} %get-tuple-element.17.sum_ref, f32[512,128]{1,0:T(8,128)S(1)} %get-tuple-element.18.disp_ref, f32[512,128]{1,0:T(8,128)S(1)} %get-tuple-element.19.comb_ref, ...), custom_call_target="tpu_custom_call" | custom-call | flops 301989888 | bytes 1572864 | tf_op jit(solution)/shard_map/pallas_call | solution.py:406
Async XLA Ops:
  2.2 15.9 %all-to-all-start = ((bf16[32,4,768]{2,1,0:T(4,128)(2,1)}), bf16[32,4,768]{2,1,0:T(4,128)(2,1)S(1)}, u32[]{:S(2)}, u32[]{:S(2)}) async-start(bf16[32,4,768]{2,1,0:T(4,128)(2,1)} %shard_map.82), calls=%async_computation | async-start | bytes 393216 | tf_op jit(solution)/shard_map/all_to_all | solution.py:42
  14.0 11.9 %collective-permute-start.1 = (bf16[208,768]{1,0:T(8,128)(2,1)}, bf16[208,768]{1,0:T(8,128)(2,1)}, u32[]{:S(2)}, u32[]{:S(2)}) collective-permute-start(bf16[208,768]{1,0:T(8,128)(2,1)} %get-tuple-element.15.refs_0_), channel_id=1, source_target_pairs={{0,2},{1,3},{2,0},{3,1},{4,6},{5,7},{6,4},{7,5},{8,10},{9,11},{10,... | collective-permute-start | bytes 958472 | tf_op jit(solution)/shard_map/ppermute | solution.py:167
  18.1 16.1 %copy-start = (bf16[1,512,768]{2,1,0:T(8,128)(2,1)S(1)}, bf16[1,512,768]{2,1,0:T(8,128)(2,1)}, u32[]{:S(2)}) copy-start(bf16[1,512,768]{2,1,0:T(8,128)(2,1)} %param.8) | copy-start | bytes 2359300
  23.0 11.2 %all-to-all-start.1 = ((bf16[32,4,768]{2,1,0:T(4,128)(2,1)}), bf16[32,4,768]{2,1,0:T(4,128)(2,1)S(1)}, u32[]{:S(2)}, u32[]{:S(2)}) async-start(bf16[32,4,768]{2,1,0:T(4,128)(2,1)} %shard_map.84.refs_4_), calls=%async_computation.1 | async-start | bytes 393216 | tf_op jit(solution)/shard_map/all_to_all | solution.py:42
  25.6 1.9 %collective-permute-start = (bf16[208,768]{1,0:T(8,128)(2,1)}, bf16[208,768]{1,0:T(8,128)(2,1)S(1)}, u32[]{:S(2)}, u32[]{:S(2)}) collective-permute-start(bf16[208,768]{1,0:T(8,128)(2,1)} %get-tuple-element.15.refs_0_), channel_id=1, source_target_pairs={{0,1},{1,0},{2,3},{3,2},{4,5},{5,4},{6,7},{7,6},{8,9},{9,8},{10,11... | collective-permute-start | bytes 958472 | tf_op jit(solution)/shard_map/ppermute | solution.py:167
  25.8 2.1 %collective-permute-start.2 = (bf16[208,768]{1,0:T(8,128)(2,1)}, bf16[208,768]{1,0:T(8,128)(2,1)S(1)}, u32[]{:S(2)}, u32[]{:S(2)}) collective-permute-start(bf16[208,768]{1,0:T(8,128)(2,1)} %collective-permute-done.1.refs_2_), channel_id=1, source_target_pairs={{0,1},{1,0},{2,3},{3,2},{4,5},{5,4},{6,7},{7,6},{8,9},{9,8},{10,11... | collective-permute-start | bytes 958472 | tf_op jit(solution)/shard_map/ppermute | solution.py:167

commit v7 on v6

--- a/solution.py
+++ b/solution.py
@@ -13,7 +13,7 @@
 PLACED = pl.BlockSpec(memory_space=pl.ANY)
 STAYS = pl.BlockSpec(memory_space=pltpu.HBM)
 GROUP = 128
-SHUFFLE = (1, 25)
+SHUFFLES = ((1, 25), (1, 12))
 MIB = 1 << 20
 FREE = pl.CostEstimate(flops=0, bytes_accessed=0, transcendentals=0)
 
@@ -30,9 +30,9 @@
     return lax.dot_general(a, b, (((0,), (0,)), ((), ())), preferred_element_type=jnp.float32)
 
 
-def exchange_order(devices):
-    shuffler = random.Random(SHUFFLE[0])
-    for _ in range(SHUFFLE[1]):
+def exchange_order(devices, seed, turns):
+    shuffler = random.Random(seed)
+    for _ in range(turns):
         order = list(range(devices))
         shuffler.shuffle(order)
     return order
@@ -67,7 +67,7 @@
 
 
 def expert_kernel(
-    order, clips, seqs, chunk, wide, got_ref, kept_ref, slope_hbm, in_hbm, out_hbm, send_ref,
+    there, back, clips, seqs, chunk, wide, got_ref, kept_ref, slope_hbm, in_hbm, out_hbm, send_ref,
     slope_ref, in_ref, out_ref, act_ref, cot_ref, sems
 ):
     rows, width = got_ref.shape[1:]
@@ -92,7 +92,7 @@
         out_copy(part).start()
     for part in range(ins):
         in_copy(part).start()
-    got = [got_ref[order.index(device)].astype(jnp.float32) for device in range(clips * seqs)]
+    got = [got_ref[there.index(device)].astype(jnp.float32) for device in range(clips * seqs)]
     cot = [sum(got[clip * seqs : (clip + 1) * seqs]) for clip in range(clips)]
     cot = jnp.concatenate(cot, axis=0).astype(jnp.bfloat16)
 
@@ -118,7 +118,7 @@
 
     grad = lax.fori_loop(0, ins, add, jnp.zeros((clips * rows, width), jnp.float32))
     grad = grad.reshape(clips, rows, width).astype(jnp.bfloat16)
-    for at, device in enumerate(order):
+    for at, device in enumerate(back):
         send_ref[at] = grad[device // seqs]
 
 
@@ -280,7 +280,7 @@
     clip_count = lax.axis_size("clip")
     seq_count = lax.axis_size("seq")
     device_count = clip_count * seq_count
-    order = exchange_order(device_count)
+    there, back = (exchange_order(device_count, *seed) for seed in SHUFFLES)
     tok_feats, out_cot, logit_raw = tokens[0], out_grad[0], saved_logits[0]
     token_total, width = tok_feats.shape
     slot_total = logit_raw.shape[1]
@@ -292,7 +292,7 @@
     still_logits, still_grad = stays(logit_raw), stays(out_cot)
     still_in, still_out = stays(expert_in[0]), stays(expert_out[0])
     blocks = pl.pallas_call(
-        functools.partial(cot_kernel, order),
+        functools.partial(cot_kernel, there),
         out_shape=jax.ShapeDtypeStruct((device_count, local_slots, width), b16),
         in_specs=[STAYS, STAYS],
         out_specs=WHOLE,
@@ -304,7 +304,7 @@
         compiler_params=pltpu.CompilerParams(vmem_limit_bytes=16 * MIB),
         cost_estimate=FREE,
     )(still_logits, still_grad)
-    received = exchange(blocks, order)
+    received = exchange(blocks, there)
 
     parts = math.gcd(hid // GROUP, 4)
     seq_slots = slot_params.shape[1]
@@ -342,7 +342,7 @@
     )
 
     send = pl.pallas_call(
-        functools.partial(expert_kernel, order, clip_count, seq_count, chunk, wide),
+        functools.partial(expert_kernel, there, back, clip_count, seq_count, chunk, wide),
         out_shape=jax.ShapeDtypeStruct((device_count, local_slots, width), b16),
         in_specs=[WHOLE, WHOLE, STAYS, STAYS, STAYS],
         out_specs=WHOLE,
@@ -367,7 +367,7 @@
         still_in,
         still_out,
     )
-    returned = exchange(send, order)
+    returned = exchange(send, back)
 
     held = {0: own}
     for bit in seq_bits():
@@ -404,7 +404,7 @@
 
     step = math.gcd(token_total, 128)
     token_grad = pl.pallas_call(
-        functools.partial(token_kernel, order, step),
+        functools.partial(token_kernel, back, step),
         out_shape=jax.ShapeDtypeStruct((token_total, width), b16),
         in_specs=[WHOLE] * 6,
         out_specs=PLACED,

time: 36.1 us -> 35.5 us (0.983)
  waiting for transfers between devices: 8.47 us -> 7.88 us
    all_to_all x2, waiting for transfers between devices: 6.7 us -> 6.11 us  [exchange(): lax.all_to_all(blocks, BOTH, split_axis=0, concat_axis=0, axis_index_grou...]
  transfers between devices with their start and end apart: 5 -> 5, of which waited for: 4 -> 4; matrix products, arithmetic and copies ran while one was open for 0% -> 0% of each run, Pallas kernels for 31% -> 32%
where the time goes in v7:
time: 35.5 us; the launch traced here: 35.3 us
  Pallas kernels  15 us (42%)
  starting transfers between devices  12.3 us (35%)
  waiting for transfers between devices  7.88 us (22%)
    all_to_all x2, starting transfers between devices, exchange(): lax.all_to_all(blocks, BOTH, split_axis=0, concat_axis=0, axis_index_grou...  9.9 us
    all_to_all x2, waiting for transfers between devices, exchange(): lax.all_to_all(blocks, BOTH, split_axis=0, concat_axis=0, axis_index_grou...  6.11 us
    pallas_call x1, Pallas kernels, on_device(): pl.pallas_call(functools.partial(expert_kernel, there, back, clip_count,...  4.82 us
    pallas_call x1, Pallas kernels, on_device(): pl.pallas_call(functools.partial(side_kernel, parts), out_shape=(jax.Shap...  4.41 us
    ppermute x3, starting transfers between devices, swap(): return lax.ppermute(value, 'seq', [(i, i ^ bit) for i in range(count)])  2.41 us
    pallas_call x1, Pallas kernels, on_device(): pl.pallas_call(functools.partial(cot_kernel, there), out_shape=jax.ShapeD...  2.21 us
    pallas_call x1, Pallas kernels, on_device(): pl.pallas_call(functools.partial(weight_kernel, seq_count), out_shape=(ja...  1.91 us
    ppermute x3, waiting for transfers between devices, swap(): return lax.ppermute(value, 'seq', [(i, i ^ bit) for i in range(count)])  1.77 us
  transfers between devices with their start and end apart: 5, of which 4 were waited for; matrix products, arithmetic and copies ran while one was open for 0% of the time, Pallas kernels for 32%

profile of v7, /device:TPU:0, one launch (start us, length us, event | category | flops | bytes accessed | tf_op | source)
XLA Modules:
  0.0 35.3 jit_solution(9325731003974685413)
XLA Ops:
  0.0 2.2 %shard_map.82 = bf16[32,4,768]{2,1,0:T(4,128)(2,1)} custom-call(bf16[512,128]{1,0:T(8,128)(2,1)} %bitcast.17, bf16[512,768]{1,0:T(8,128)(2,1)} %bitcast.15), custom_call_target="tpu_custom_call" | custom-call | tf_op jit(solution)/shard_map/pallas_call | solution.py:294
  2.2 7.3 %all-to-all-start = ((bf16[32,4,768]{2,1,0:T(4,128)(2,1)}), bf16[32,4,768]{2,1,0:T(4,128)(2,1)S(1)}, u32[]{:S(2)}, u32[]{:S(2)}) async-start(bf16[32,4,768]{2,1,0:T(4,128)(2,1)} %shard_map.82), calls=%async_computation | async-start | bytes 393216 | tf_op jit(solution)/shard_map/all_to_all | solution.py:42
  9.5 4.4 %shard_map.83 = (bf16[208,768]{1,0:T(8,128)(2,1)}, f32[32,3072]{1,0:T(8,128)}, bf16[1536,768]{1,0:T(8,128)(2,1)S(1)}) custom-call(bf16[512,128]{1,0:T(8,128)(2,1)} %bitcast.18, bf16[512,768]{1,0:T(8,128)(2,1)} %bitcast.9, bf16[32,768]{1,0:T(8,128)(2,1)} %bitcast.20, bf16[32,768]{1,0:T(8,128)(2,1)} %bitcast.21, bf16[8,4,768]{2,1,0:T(4,128)(2,1)} %feed_hbm.1, ...), custom_call_target="tpu_custom_call" | custom-call | tf_op jit(solution)/shard_map/pallas_call | solution.py:315
  14.0 1.8 %collective-permute-start.1 = (bf16[208,768]{1,0:T(8,128)(2,1)}, bf16[208,768]{1,0:T(8,128)(2,1)}, u32[]{:S(2)}, u32[]{:S(2)}) collective-permute-start(bf16[208,768]{1,0:T(8,128)(2,1)} %get-tuple-element.15.refs_0_), channel_id=1, source_target_pairs={{0,2},{1,3},{2,0},{3,1},{4,6},{5,7},{6,4},{7,5},{8,10},{9,11},{10,... | collective-permute-start | bytes 958472 | tf_op jit(solution)/shard_map/ppermute | solution.py:167
  15.8 2.4 %all-to-all-done.got_ref = bf16[32,4,768]{2,1,0:T(4,128)(2,1)S(1)} async-done(((bf16[32,4,768]{2,1,0:T(4,128)(2,1)}), bf16[32,4,768]{2,1,0:T(4,128)(2,1)S(1)}, u32[]{:S(2)}, u32[]{:S(2)}) %all-to-all-start) | async-done | bytes 196640 | tf_op jit(solution)/shard_map/all_to_all | solution.py:42
  18.1 0.0 copy-start
  18.2 4.8 %shard_map.84.refs_4_ = bf16[32,4,768]{2,1,0:T(4,128)(2,1)} custom-call(bf16[32,4,768]{2,1,0:T(4,128)(2,1)S(1)} %all-to-all-done.got_ref, bf16[1536,768]{1,0:T(8,128)(2,1)S(1)} %get-tuple-element.13.kept_ref, f32[32,3072]{1,0:T(8,128)} %get-tuple-element.14.slope_hbm, bf16[768,3072]{1,0:T(8,128)(2,1)} %bitcast.12, bf16[3072,768]{1,0:T(8,128)(2,1)} %bitcast.14), custom_call_target="tpu_custom_call" | custom-call | flops 301989888 | bytes 9437184 | tf_op jit(solution)/shard_map/pallas_call | solution.py:344
  23.0 2.6 %all-to-all-start.1 = ((bf16[32,4,768]{2,1,0:T(4,128)(2,1)}), bf16[32,4,768]{2,1,0:T(4,128)(2,1)S(1)}, u32[]{:S(2)}, u32[]{:S(2)}) async-start(bf16[32,4,768]{2,1,0:T(4,128)(2,1)} %shard_map.84.refs_4_), calls=%async_computation.1 | async-start | bytes 393216 | tf_op jit(solution)/shard_map/all_to_all | solution.py:42
  25.6 0.2 collective-permute-start
  25.8 0.0 collective-permute-done.1.refs_2_
  25.8 0.3 collective-permute-start.2
  26.2 1.3 %collective-permute-done.refs_1_ = bf16[208,768]{1,0:T(8,128)(2,1)S(1)} collective-permute-done((bf16[208,768]{1,0:T(8,128)(2,1)}, bf16[208,768]{1,0:T(8,128)(2,1)S(1)}, u32[]{:S(2)}, u32[]{:S(2)}) %collective-permute-start) | collective-permute-done | bytes 319520 | tf_op jit(solution)/shard_map/ppermute | solution.py:167
  27.5 0.5 %collective-permute-done.2.refs_3_ = bf16[208,768]{1,0:T(8,128)(2,1)S(1)} collective-permute-done((bf16[208,768]{1,0:T(8,128)(2,1)}, bf16[208,768]{1,0:T(8,128)(2,1)S(1)}, u32[]{:S(2)}, u32[]{:S(2)}) %collective-permute-start.2) | collective-permute-done | bytes 319520 | tf_op jit(solution)/shard_map/ppermute | solution.py:167
  27.9 1.9 %shard_map.85 = (f32[512,128]{1,0:T(8,128)S(1)}, f32[512,128]{1,0:T(8,128)S(1)}, bf16[128,768]{1,0:T(8,128)(2,1)S(1)}, bf16[128,768]{1,0:T(8,128)(2,1)S(1)}) custom-call(s32[1]{0:T(128)} %bitcast.7.me_ref, bf16[512,128]{1,0:T(8,128)(2,1)} %bitcast.19, bf16[512,768]{1,0:T(8,128)(2,1)} %bitcast.16, bf16[208,768]{1,0:T(8,128)(2,1)} %get-tuple-element.15.refs_0_, ...), custom_call_target="tpu_custom_call" | custom-call | tf_op jit(solution)/shard_map/pallas_call | solution.py:376
  29.9 3.7 %all-to-all-done.1.got_ref = bf16[32,4,768]{2,1,0:T(4,128)(2,1)S(1)} async-done(((bf16[32,4,768]{2,1,0:T(4,128)(2,1)}), bf16[32,4,768]{2,1,0:T(4,128)(2,1)S(1)}, u32[]{:S(2)}, u32[]{:S(2)}) %all-to-all-start.1) | async-done | bytes 196640 | tf_op jit(solution)/shard_map/all_to_all | solution.py:42
  33.6 0.0 copy-done
  33.6 1.7 %shard_map.86 = bf16[512,768]{1,0:T(8,128)(2,1)} custom-call(bf16[512,768]{1,0:T(8,128)(2,1)S(1)} %bitcast.10, bf16[32,4,768]{2,1,0:T(4,128)(2,1)S(1)} %all-to-all-done.1.got_ref, bf16[128,768]{1,0:T(8,128)(2,1)S(1)} %get-tuple-element.17.sum_ref, f32[512,128]{1,0:T(8,128)S(1)} %get-tuple-element.18.disp_ref, f32[512,128]{1,0:T(8,128)S(1)} %get-tuple-element.19.comb_ref, ...), custom_call_target="tpu_custom_call" | custom-call | flops 301989888 | bytes 1572864 | tf_op jit(solution)/shard_map/pallas_call | solution.py:406
Async XLA Ops:
  2.2 15.9 %all-to-all-start = ((bf16[32,4,768]{2,1,0:T(4,128)(2,1)}), bf16[32,4,768]{2,1,0:T(4,128)(2,1)S(1)}, u32[]{:S(2)}, u32[]{:S(2)}) async-start(bf16[32,4,768]{2,1,0:T(4,128)(2,1)} %shard_map.82), calls=%async_computation | async-start | bytes 393216 | tf_op jit(solution)/shard_map/all_to_all | solution.py:42
  14.0 11.9 %collective-permute-start.1 = (bf16[208,768]{1,0:T(8,128)(2,1)}, bf16[208,768]{1,0:T(8,128)(2,1)}, u32[]{:S(2)}, u32[]{:S(2)}) collective-permute-start(bf16[208,768]{1,0:T(8,128)(2,1)} %get-tuple-element.15.refs_0_), channel_id=1, source_target_pairs={{0,2},{1,3},{2,0},{3,1},{4,6},{5,7},{6,4},{7,5},{8,10},{9,11},{10,... | collective-permute-start | bytes 958472 | tf_op jit(solution)/shard_map/ppermute | solution.py:167
  18.1 15.5 %copy-start = (bf16[1,512,768]{2,1,0:T(8,128)(2,1)S(1)}, bf16[1,512,768]{2,1,0:T(8,128)(2,1)}, u32[]{:S(2)}) copy-start(bf16[1,512,768]{2,1,0:T(8,128)(2,1)} %param.8) | copy-start | bytes 2359300
  23.0 10.6 %all-to-all-start.1 = ((bf16[32,4,768]{2,1,0:T(4,128)(2,1)}), bf16[32,4,768]{2,1,0:T(4,128)(2,1)S(1)}, u32[]{:S(2)}, u32[]{:S(2)}) async-start(bf16[32,4,768]{2,1,0:T(4,128)(2,1)} %shard_map.84.refs_4_), calls=%async_computation.1 | async-start | bytes 393216 | tf_op jit(solution)/shard_map/all_to_all | solution.py:42
  25.6 1.9 %collective-permute-start = (bf16[208,768]{1,0:T(8,128)(2,1)}, bf16[208,768]{1,0:T(8,128)(2,1)S(1)}, u32[]{:S(2)}, u32[]{:S(2)}) collective-permute-start(bf16[208,768]{1,0:T(8,128)(2,1)} %get-tuple-element.15.refs_0_), channel_id=1, source_target_pairs={{0,1},{1,0},{2,3},{3,2},{4,5},{5,4},{6,7},{7,6},{8,9},{9,8},{10,11... | collective-permute-start | bytes 958472 | tf_op jit(solution)/shard_map/ppermute | solution.py:167
  25.8 2.1 %collective-permute-start.2 = (bf16[208,768]{1,0:T(8,128)(2,1)}, bf16[208,768]{1,0:T(8,128)(2,1)S(1)}, u32[]{:S(2)}, u32[]{:S(2)}) collective-permute-start(bf16[208,768]{1,0:T(8,128)(2,1)} %collective-permute-done.1.refs_2_), channel_id=1, source_target_pairs={{0,1},{1,0},{2,3},{3,2},{4,5},{5,4},{6,7},{7,6},{8,9},{9,8},{10,11... | collective-permute-start | bytes 958472 | tf_op jit(solution)/shard_map/ppermute | solution.py:167

commit v8 on v7

--- a/solution.py
+++ b/solution.py
@@ -67,8 +67,8 @@
 
 
 def expert_kernel(
-    there, back, clips, seqs, chunk, wide, got_ref, kept_ref, slope_hbm, in_hbm, out_hbm, send_ref,
-    slope_ref, in_ref, out_ref, act_ref, cot_ref, sems
+    there, back, clips, seqs, chunk, wide, got_ref, kept_ref, slope_ref, in_hbm, out_hbm, send_ref,
+    in_ref, out_ref, cot_ref, sems
 ):
     rows, width = got_ref.shape[1:]
     hid, kept = in_hbm.shape[1], kept_ref.shape[0]
@@ -86,8 +86,6 @@
         at = place(part, wide)
         return pltpu.make_async_copy(in_hbm.at[:, at], in_ref.at[:, at], sems.at[outs + part])
 
-    slope_copy = pltpu.make_async_copy(slope_hbm, slope_ref, sems.at[outs + ins])
-    slope_copy.start()
     for part in range(outs):
         out_copy(part).start()
     for part in range(ins):
@@ -99,10 +97,7 @@
     @pl.loop(0, kept // chunk)
     def _(part):
         at = place(part, chunk)
-        act_ref[:, at] = dot_nt(cot, kept_ref[at, :])
-
-    slope_copy.wait()
-    cot_ref[:, :kept] = (act_ref[...] * slope_ref[:, :kept]).astype(jnp.bfloat16)
+        cot_ref[:, at] = (dot_nt(cot, kept_ref[at, :]) * slope_ref[:, at]).astype(jnp.bfloat16)
 
     @pl.loop(0, outs)
     def _(part):
@@ -223,7 +218,8 @@
         x = dot_nn(feed, in_ref[:, at])
         bend = jnp.tanh(root * (x + 0.044715 * (x * x * x)))
         grown = root * (1.0 + 3.0 * 0.044715 * (x * x))
-        slope_ref[:, at] = 0.5 * (1.0 + bend) + 0.5 * x * (1.0 - bend * bend) * grown
+        slope = 0.5 * (1.0 + bend) + 0.5 * x * (1.0 - bend * bend) * grown
+        slope_ref[:, at] = slope.astype(slope_ref.dtype)
     copies[2].wait()
     copies[3].wait()
     copies[-1].wait()
@@ -316,7 +312,7 @@
         functools.partial(side_kernel, parts),
         out_shape=(
             jax.ShapeDtypeStruct((pack_rows, width), b16),
-            pltpu.HBM((feed_rows, hid), f32),
+            jax.ShapeDtypeStruct((feed_rows, hid), b16),
             pltpu.VMEM((kept_rows, width), b16),
         ),
         in_specs=[STAYS] * 7,
@@ -344,15 +340,13 @@
     send = pl.pallas_call(
         functools.partial(expert_kernel, there, back, clip_count, seq_count, chunk, wide),
         out_shape=jax.ShapeDtypeStruct((device_count, local_slots, width), b16),
-        in_specs=[WHOLE, WHOLE, STAYS, STAYS, STAYS],
+        in_specs=[WHOLE, WHOLE, WHOLE, STAYS, STAYS],
         out_specs=WHOLE,
         scratch_shapes=[
-            pltpu.VMEM((feed_rows, hid), f32),
             pltpu.VMEM((width, hid), b16),
             pltpu.VMEM((max(hid - kept_rows, chunk), width), b16),
-            pltpu.VMEM((feed_rows, kept_rows), f32),
             pltpu.VMEM((feed_rows, hid), b16),
-            pltpu.SemaphoreType.DMA(((hid - kept_rows) // chunk + hid // wide + 1,)),
+            pltpu.SemaphoreType.DMA(((hid - kept_rows) // chunk + hid // wide,)),
         ],
         compiler_params=pltpu.CompilerParams(vmem_limit_bytes=20 * MIB),
         cost_estimate=pl.CostEstimate(
@@ -363,7 +357,7 @@
     )(
         received,
         pltpu.with_memory_space_constraint(kept, pltpu.VMEM),
-        stays(slope),
+        slope,
         still_in,
         still_out,
     )

time: 35.5 us -> 35.4 us (level)
  transfers between devices with their start and end apart: 5 -> 5, of which waited for: 4 -> 4; matrix products, arithmetic and copies ran while one was open for 0% -> 0% of each run, Pallas kernels for 32% -> 31%
where the time goes in v8:
time: 35.4 us; the launch traced here: 35.1 us
  Pallas kernels  14.8 us (42%)
  starting transfers between devices  12.3 us (35%)
  waiting for transfers between devices  8.01 us (23%)
    all_to_all x2, starting transfers between devices, exchange(): lax.all_to_all(blocks, BOTH, split_axis=0, concat_axis=0, axis_index_grou...  9.9 us
    all_to_all x2, waiting for transfers between devices, exchange(): lax.all_to_all(blocks, BOTH, split_axis=0, concat_axis=0, axis_index_grou...  6.24 us
    pallas_call x1, Pallas kernels, on_device(): pl.pallas_call(functools.partial(expert_kernel, there, back, clip_count,...  4.69 us
    pallas_call x1, Pallas kernels, on_device(): pl.pallas_call(functools.partial(side_kernel, parts), out_shape=(jax.Shap...  4.28 us
    ppermute x3, starting transfers between devices, swap(): return lax.ppermute(value, 'seq', [(i, i ^ bit) for i in range(count)])  2.41 us
    pallas_call x1, Pallas kernels, on_device(): pl.pallas_call(functools.partial(cot_kernel, there), out_shape=jax.ShapeD...  2.21 us
    pallas_call x1, Pallas kernels, on_device(): pl.pallas_call(functools.partial(weight_kernel, seq_count), out_shape=(ja...  1.91 us
    ppermute x3, waiting for transfers between devices, swap(): return lax.ppermute(value, 'seq', [(i, i ^ bit) for i in range(count)])  1.77 us
  transfers between devices with their start and end apart: 5, of which 4 were waited for; matrix products, arithmetic and copies ran while one was open for 0% of the time, Pallas kernels for 31%

profile of v8, /device:TPU:0, one launch (start us, length us, event | category | flops | bytes accessed | tf_op | source)
XLA Modules:
  0.0 35.1 jit_solution(10939101437469817347)
XLA Ops:
  0.0 2.2 %shard_map.82 = bf16[32,4,768]{2,1,0:T(4,128)(2,1)} custom-call(bf16[512,128]{1,0:T(8,128)(2,1)} %bitcast.17, bf16[512,768]{1,0:T(8,128)(2,1)} %bitcast.15), custom_call_target="tpu_custom_call" | custom-call | tf_op jit(solution)/shard_map/pallas_call | solution.py:290
  2.2 7.3 %all-to-all-start = ((bf16[32,4,768]{2,1,0:T(4,128)(2,1)}), bf16[32,4,768]{2,1,0:T(4,128)(2,1)S(1)}, u32[]{:S(2)}, u32[]{:S(2)}) async-start(bf16[32,4,768]{2,1,0:T(4,128)(2,1)} %shard_map.82), calls=%async_computation | async-start | bytes 393216 | tf_op jit(solution)/shard_map/all_to_all | solution.py:42
  9.5 4.3 %shard_map.83 = (bf16[208,768]{1,0:T(8,128)(2,1)}, bf16[32,3072]{1,0:T(8,128)(2,1)S(1)}, bf16[1536,768]{1,0:T(8,128)(2,1)S(1)}) custom-call(bf16[512,128]{1,0:T(8,128)(2,1)} %bitcast.18, bf16[512,768]{1,0:T(8,128)(2,1)} %bitcast.9, bf16[32,768]{1,0:T(8,128)(2,1)} %bitcast.20, bf16[32,768]{1,0:T(8,128)(2,1)} %bitcast.21, bf16[8,4,768]{2,1,0:T(4,128)(2,1)} %feed_hbm.1, ...), custom_call_target="tpu_custom_call" | custom-call | tf_op jit(solution)/shard_map/pallas_call | solution.py:311
  13.8 1.8 %collective-permute-start.1 = (bf16[208,768]{1,0:T(8,128)(2,1)}, bf16[208,768]{1,0:T(8,128)(2,1)}, u32[]{:S(2)}, u32[]{:S(2)}) collective-permute-start(bf16[208,768]{1,0:T(8,128)(2,1)} %get-tuple-element.15.refs_0_), channel_id=1, source_target_pairs={{0,2},{1,3},{2,0},{3,1},{4,6},{5,7},{6,4},{7,5},{8,10},{9,11},{10,... | collective-permute-start | bytes 958472 | tf_op jit(solution)/shard_map/ppermute | solution.py:162
  15.7 2.5 %all-to-all-done.got_ref = bf16[32,4,768]{2,1,0:T(4,128)(2,1)S(1)} async-done(((bf16[32,4,768]{2,1,0:T(4,128)(2,1)}), bf16[32,4,768]{2,1,0:T(4,128)(2,1)S(1)}, u32[]{:S(2)}, u32[]{:S(2)}) %all-to-all-start) | async-done | bytes 196640 | tf_op jit(solution)/shard_map/all_to_all | solution.py:42
  18.1 0.0 copy-start
  18.1 4.7 %shard_map.84.refs_4_ = bf16[32,4,768]{2,1,0:T(4,128)(2,1)} custom-call(bf16[32,4,768]{2,1,0:T(4,128)(2,1)S(1)} %all-to-all-done.got_ref, bf16[1536,768]{1,0:T(8,128)(2,1)S(1)} %get-tuple-element.13.kept_ref, bf16[32,3072]{1,0:T(8,128)(2,1)S(1)} %get-tuple-element.14.slope_ref, bf16[768,3072]{1,0:T(8,128)(2,1)} %bitcast.12, bf16[3072,768]{1,0:T(8,128)(2,1)} %bitcast.14), custom_call_target="tpu_custom_call" | custom-call | flops 301989888 | bytes 9437184 | tf_op jit(solution)/shard_map/pallas_call | solution.py:340
  22.9 2.6 %all-to-all-start.1 = ((bf16[32,4,768]{2,1,0:T(4,128)(2,1)}), bf16[32,4,768]{2,1,0:T(4,128)(2,1)S(1)}, u32[]{:S(2)}, u32[]{:S(2)}) async-start(bf16[32,4,768]{2,1,0:T(4,128)(2,1)} %shard_map.84.refs_4_), calls=%async_computation.1 | async-start | bytes 393216 | tf_op jit(solution)/shard_map/all_to_all | solution.py:42
  25.5 0.2 collective-permute-start
  25.7 0.0 collective-permute-done.1.refs_2_
  25.7 0.3 collective-permute-start.2
  26.0 1.3 %collective-permute-done.refs_1_ = bf16[208,768]{1,0:T(8,128)(2,1)S(1)} collective-permute-done((bf16[208,768]{1,0:T(8,128)(2,1)}, bf16[208,768]{1,0:T(8,128)(2,1)S(1)}, u32[]{:S(2)}, u32[]{:S(2)}) %collective-permute-start) | collective-permute-done | bytes 319520 | tf_op jit(solution)/shard_map/ppermute | solution.py:162
  27.4 0.5 %collective-permute-done.2.refs_3_ = bf16[208,768]{1,0:T(8,128)(2,1)S(1)} collective-permute-done((bf16[208,768]{1,0:T(8,128)(2,1)}, bf16[208,768]{1,0:T(8,128)(2,1)S(1)}, u32[]{:S(2)}, u32[]{:S(2)}) %collective-permute-start.2) | collective-permute-done | bytes 319520 | tf_op jit(solution)/shard_map/ppermute | solution.py:162
  27.8 1.9 %shard_map.85 = (f32[512,128]{1,0:T(8,128)S(1)}, f32[512,128]{1,0:T(8,128)S(1)}, bf16[128,768]{1,0:T(8,128)(2,1)S(1)}, bf16[128,768]{1,0:T(8,128)(2,1)S(1)}) custom-call(s32[1]{0:T(128)} %bitcast.7.me_ref, bf16[512,128]{1,0:T(8,128)(2,1)} %bitcast.19, bf16[512,768]{1,0:T(8,128)(2,1)} %bitcast.16, bf16[208,768]{1,0:T(8,128)(2,1)} %get-tuple-element.15.refs_0_, ...), custom_call_target="tpu_custom_call" | custom-call | tf_op jit(solution)/shard_map/pallas_call | solution.py:370
  29.7 3.7 %all-to-all-done.1.got_ref = bf16[32,4,768]{2,1,0:T(4,128)(2,1)S(1)} async-done(((bf16[32,4,768]{2,1,0:T(4,128)(2,1)}), bf16[32,4,768]{2,1,0:T(4,128)(2,1)S(1)}, u32[]{:S(2)}, u32[]{:S(2)}) %all-to-all-start.1) | async-done | bytes 196640 | tf_op jit(solution)/shard_map/all_to_all | solution.py:42
  33.5 0.0 copy-done
  33.5 1.7 %shard_map.86 = bf16[512,768]{1,0:T(8,128)(2,1)} custom-call(bf16[512,768]{1,0:T(8,128)(2,1)S(1)} %bitcast.10, bf16[32,4,768]{2,1,0:T(4,128)(2,1)S(1)} %all-to-all-done.1.got_ref, bf16[128,768]{1,0:T(8,128)(2,1)S(1)} %get-tuple-element.17.sum_ref, f32[512,128]{1,0:T(8,128)S(1)} %get-tuple-element.18.disp_ref, f32[512,128]{1,0:T(8,128)S(1)} %get-tuple-element.19.comb_ref, ...), custom_call_target="tpu_custom_call" | custom-call | flops 301989888 | bytes 1572864 | tf_op jit(solution)/shard_map/pallas_call | solution.py:400
Async XLA Ops:
  2.2 15.9 %all-to-all-start = ((bf16[32,4,768]{2,1,0:T(4,128)(2,1)}), bf16[32,4,768]{2,1,0:T(4,128)(2,1)S(1)}, u32[]{:S(2)}, u32[]{:S(2)}) async-start(bf16[32,4,768]{2,1,0:T(4,128)(2,1)} %shard_map.82), calls=%async_computation | async-start | bytes 393216 | tf_op jit(solution)/shard_map/all_to_all | solution.py:42
  13.8 11.9 %collective-permute-start.1 = (bf16[208,768]{1,0:T(8,128)(2,1)}, bf16[208,768]{1,0:T(8,128)(2,1)}, u32[]{:S(2)}, u32[]{:S(2)}) collective-permute-start(bf16[208,768]{1,0:T(8,128)(2,1)} %get-tuple-element.15.refs_0_), channel_id=1, source_target_pairs={{0,2},{1,3},{2,0},{3,1},{4,6},{5,7},{6,4},{7,5},{8,10},{9,11},{10,... | collective-permute-start | bytes 958472 | tf_op jit(solution)/shard_map/ppermute | solution.py:162
  18.1 15.3 %copy-start = (bf16[1,512,768]{2,1,0:T(8,128)(2,1)S(1)}, bf16[1,512,768]{2,1,0:T(8,128)(2,1)}, u32[]{:S(2)}) copy-start(bf16[1,512,768]{2,1,0:T(8,128)(2,1)} %param.8) | copy-start | bytes 2359300
  22.9 10.6 %all-to-all-start.1 = ((bf16[32,4,768]{2,1,0:T(4,128)(2,1)}), bf16[32,4,768]{2,1,0:T(4,128)(2,1)S(1)}, u32[]{:S(2)}, u32[]{:S(2)}) async-start(bf16[32,4,768]{2,1,0:T(4,128)(2,1)} %shard_map.84.refs_4_), calls=%async_computation.1 | async-start | bytes 393216 | tf_op jit(solution)/shard_map/all_to_all | solution.py:42
  25.5 1.9 %collective-permute-start = (bf16[208,768]{1,0:T(8,128)(2,1)}, bf16[208,768]{1,0:T(8,128)(2,1)S(1)}, u32[]{:S(2)}, u32[]{:S(2)}) collective-permute-start(bf16[208,768]{1,0:T(8,128)(2,1)} %get-tuple-element.15.refs_0_), channel_id=1, source_target_pairs={{0,1},{1,0},{2,3},{3,2},{4,5},{5,4},{6,7},{7,6},{8,9},{9,8},{10,11... | collective-permute-start | bytes 958472 | tf_op jit(solution)/shard_map/ppermute | solution.py:162
  25.7 2.1 %collective-permute-start.2 = (bf16[208,768]{1,0:T(8,128)(2,1)}, bf16[208,768]{1,0:T(8,128)(2,1)S(1)}, u32[]{:S(2)}, u32[]{:S(2)}) collective-permute-start(bf16[208,768]{1,0:T(8,128)(2,1)} %collective-permute-done.1.refs_2_), channel_id=1, source_target_pairs={{0,1},{1,0},{2,3},{3,2},{4,5},{5,4},{6,7},{7,6},{8,9},{9,8},{10,11... | collective-permute-start | bytes 958472 | tf_op jit(solution)/shard_map/ppermute | solution.py:162

commit v9 on v7

--- a/solution.py
+++ b/solution.py
@@ -130,6 +130,10 @@
     slot_grad = [got_ref[order.index(at)].astype(jnp.float32) for at in range(len(order))]
     slot_grad = jnp.concatenate(slot_grad, axis=0).astype(jnp.bfloat16)
     cross = dot_nt(sum_ref[...], slot_grad)
+    halves = math.gcd(tok_ref.shape[0] // chunk, 2)
+    half = tok_ref.shape[0] // halves
+    disp_cot = [dot_nt(tok_ref[pl.ds(at * half, half), :], slot_grad) for at in range(halves)]
+    disp_cot = jnp.concatenate(disp_cot, axis=0)
     row = lax.broadcasted_iota(jnp.int32, (slots, slots), 0)
     col = lax.broadcasted_iota(jnp.int32, (slots, slots), 1)
     slot_dots = jnp.sum(jnp.where(row == col, cross, 0.0), axis=0, keepdims=True)
@@ -138,8 +142,7 @@
     for step in range(tok_ref.shape[0] // chunk):
         part = pl.ds(step * chunk, chunk)
         dispatch = disp_ref[part, :]
-        disp_cot = dot_nt(tok_ref[part, :], slot_grad)
-        logit_grad = comb_ref[part, :] + dispatch * (disp_cot - slot_dots)
+        logit_grad = comb_ref[part, :] + dispatch * (disp_cot[part.start : part.start + chunk] - slot_dots)
         weights = jnp.concatenate([dispatch, logit_grad], axis=1).astype(jnp.bfloat16)
         stage[part, :] = dot_nn(weights, both_rows).astype(jnp.bfloat16)
         copy = pltpu.make_async_copy(stage.at[part, :], out_hbm.at[part, :], sems.at[step])

time: 35.5 us -> 35.3 us (level)
  no operation moved by 1% of the time
where the time goes in v9:
time: 35.3 us; the launch traced here: 35 us
  Pallas kernels  14.8 us (42%)
  starting transfers between devices  12.3 us (35%)
  waiting for transfers between devices  7.88 us (22%)
    all_to_all x2, starting transfers between devices, exchange(): lax.all_to_all(blocks, BOTH, split_axis=0, concat_axis=0, axis_index_grou...  9.9 us
    all_to_all x2, waiting for transfers between devices, exchange(): lax.all_to_all(blocks, BOTH, split_axis=0, concat_axis=0, axis_index_grou...  6.11 us
    pallas_call x1, Pallas kernels, on_device(): pl.pallas_call(functools.partial(expert_kernel, there, back, clip_count,...  4.82 us
    pallas_call x1, Pallas kernels, on_device(): pl.pallas_call(functools.partial(side_kernel, parts), out_shape=(jax.Shap...  4.41 us
    ppermute x3, starting transfers between devices, swap(): return lax.ppermute(value, 'seq', [(i, i ^ bit) for i in range(count)])  2.41 us
    pallas_call x1, Pallas kernels, on_device(): pl.pallas_call(functools.partial(cot_kernel, there), out_shape=jax.ShapeD...  2.21 us
    pallas_call x1, Pallas kernels, on_device(): pl.pallas_call(functools.partial(weight_kernel, seq_count), out_shape=(ja...  1.91 us
    ppermute x3, waiting for transfers between devices, swap(): return lax.ppermute(value, 'seq', [(i, i ^ bit) for i in range(count)])  1.77 us
  transfers between devices with their start and end apart: 5, of which 4 were waited for; matrix products, arithmetic and copies ran while one was open for 0% of the time, Pallas kernels for 32%

profile of v9, /device:TPU:0, one launch (start us, length us, event | category | flops | bytes accessed | tf_op | source)
XLA Modules:
  0.0 35.0 jit_solution(3061671656263375530)
XLA Ops:
  0.0 2.2 %shard_map.82 = bf16[32,4,768]{2,1,0:T(4,128)(2,1)} custom-call(bf16[512,128]{1,0:T(8,128)(2,1)} %bitcast.17, bf16[512,768]{1,0:T(8,128)(2,1)} %bitcast.15), custom_call_target="tpu_custom_call" | custom-call | tf_op jit(solution)/shard_map/pallas_call | solution.py:297
  2.2 7.3 %all-to-all-start = ((bf16[32,4,768]{2,1,0:T(4,128)(2,1)}), bf16[32,4,768]{2,1,0:T(4,128)(2,1)S(1)}, u32[]{:S(2)}, u32[]{:S(2)}) async-start(bf16[32,4,768]{2,1,0:T(4,128)(2,1)} %shard_map.82), calls=%async_computation | async-start | bytes 393216 | tf_op jit(solution)/shard_map/all_to_all | solution.py:42
  9.5 4.4 %shard_map.83 = (bf16[208,768]{1,0:T(8,128)(2,1)}, f32[32,3072]{1,0:T(8,128)}, bf16[1536,768]{1,0:T(8,128)(2,1)S(1)}) custom-call(bf16[512,128]{1,0:T(8,128)(2,1)} %bitcast.18, bf16[512,768]{1,0:T(8,128)(2,1)} %bitcast.9, bf16[32,768]{1,0:T(8,128)(2,1)} %bitcast.20, bf16[32,768]{1,0:T(8,128)(2,1)} %bitcast.21, bf16[8,4,768]{2,1,0:T(4,128)(2,1)} %feed_hbm.1, ...), custom_call_target="tpu_custom_call" | custom-call | tf_op jit(solution)/shard_map/pallas_call | solution.py:318
  14.0 1.8 %collective-permute-start.1 = (bf16[208,768]{1,0:T(8,128)(2,1)}, bf16[208,768]{1,0:T(8,128)(2,1)}, u32[]{:S(2)}, u32[]{:S(2)}) collective-permute-start(bf16[208,768]{1,0:T(8,128)(2,1)} %get-tuple-element.15.refs_0_), channel_id=1, source_target_pairs={{0,2},{1,3},{2,0},{3,1},{4,6},{5,7},{6,4},{7,5},{8,10},{9,11},{10,... | collective-permute-start | bytes 958472 | tf_op jit(solution)/shard_map/ppermute | solution.py:170
  15.8 2.4 %all-to-all-done.got_ref = bf16[32,4,768]{2,1,0:T(4,128)(2,1)S(1)} async-done(((bf16[32,4,768]{2,1,0:T(4,128)(2,1)}), bf16[32,4,768]{2,1,0:T(4,128)(2,1)S(1)}, u32[]{:S(2)}, u32[]{:S(2)}) %all-to-all-start) | async-done | bytes 196640 | tf_op jit(solution)/shard_map/all_to_all | solution.py:42
  18.1 0.0 copy-start
  18.2 4.8 %shard_map.84.refs_4_ = bf16[32,4,768]{2,1,0:T(4,128)(2,1)} custom-call(bf16[32,4,768]{2,1,0:T(4,128)(2,1)S(1)} %all-to-all-done.got_ref, bf16[1536,768]{1,0:T(8,128)(2,1)S(1)} %get-tuple-element.13.kept_ref, f32[32,3072]{1,0:T(8,128)} %get-tuple-element.14.slope_hbm, bf16[768,3072]{1,0:T(8,128)(2,1)} %bitcast.12, bf16[3072,768]{1,0:T(8,128)(2,1)} %bitcast.14), custom_call_target="tpu_custom_call" | custom-call | flops 301989888 | bytes 9437184 | tf_op jit(solution)/shard_map/pallas_call | solution.py:347
  23.0 2.6 %all-to-all-start.1 = ((bf16[32,4,768]{2,1,0:T(4,128)(2,1)}), bf16[32,4,768]{2,1,0:T(4,128)(2,1)S(1)}, u32[]{:S(2)}, u32[]{:S(2)}) async-start(bf16[32,4,768]{2,1,0:T(4,128)(2,1)} %shard_map.84.refs_4_), calls=%async_computation.1 | async-start | bytes 393216 | tf_op jit(solution)/shard_map/all_to_all | solution.py:42
  25.6 0.2 collective-permute-start
  25.8 0.0 collective-permute-done.1.refs_2_
  25.8 0.3 collective-permute-start.2
  26.2 1.3 %collective-permute-done.refs_1_ = bf16[208,768]{1,0:T(8,128)(2,1)S(1)} collective-permute-done((bf16[208,768]{1,0:T(8,128)(2,1)}, bf16[208,768]{1,0:T(8,128)(2,1)S(1)}, u32[]{:S(2)}, u32[]{:S(2)}) %collective-permute-start) | collective-permute-done | bytes 319520 | tf_op jit(solution)/shard_map/ppermute | solution.py:170
  27.5 0.5 %collective-permute-done.2.refs_3_ = bf16[208,768]{1,0:T(8,128)(2,1)S(1)} collective-permute-done((bf16[208,768]{1,0:T(8,128)(2,1)}, bf16[208,768]{1,0:T(8,128)(2,1)S(1)}, u32[]{:S(2)}, u32[]{:S(2)}) %collective-permute-start.2) | collective-permute-done | bytes 319520 | tf_op jit(solution)/shard_map/ppermute | solution.py:170
  27.9 1.9 %shard_map.85 = (f32[512,128]{1,0:T(8,128)S(1)}, f32[512,128]{1,0:T(8,128)S(1)}, bf16[128,768]{1,0:T(8,128)(2,1)S(1)}, bf16[128,768]{1,0:T(8,128)(2,1)S(1)}) custom-call(s32[1]{0:T(128)} %bitcast.7.me_ref, bf16[512,128]{1,0:T(8,128)(2,1)} %bitcast.19, bf16[512,768]{1,0:T(8,128)(2,1)} %bitcast.16, bf16[208,768]{1,0:T(8,128)(2,1)} %get-tuple-element.15.refs_0_, ...), custom_call_target="tpu_custom_call" | custom-call | tf_op jit(solution)/shard_map/pallas_call | solution.py:379
  29.9 3.7 %all-to-all-done.1.got_ref = bf16[32,4,768]{2,1,0:T(4,128)(2,1)S(1)} async-done(((bf16[32,4,768]{2,1,0:T(4,128)(2,1)}), bf16[32,4,768]{2,1,0:T(4,128)(2,1)S(1)}, u32[]{:S(2)}, u32[]{:S(2)}) %all-to-all-start.1) | async-done | bytes 196640 | tf_op jit(solution)/shard_map/all_to_all | solution.py:42
  33.6 0.0 copy-done
  33.6 1.4 %shard_map.86 = bf16[512,768]{1,0:T(8,128)(2,1)} custom-call(bf16[512,768]{1,0:T(8,128)(2,1)S(1)} %bitcast.10, bf16[32,4,768]{2,1,0:T(4,128)(2,1)S(1)} %all-to-all-done.1.got_ref, bf16[128,768]{1,0:T(8,128)(2,1)S(1)} %get-tuple-element.17.sum_ref, f32[512,128]{1,0:T(8,128)S(1)} %get-tuple-element.18.disp_ref, f32[512,128]{1,0:T(8,128)S(1)} %get-tuple-element.19.comb_ref, ...), custom_call_target="tpu_custom_call" | custom-call | flops 301989888 | bytes 1572864 | tf_op jit(solution)/shard_map/pallas_call | solution.py:409
Async XLA Ops:
  2.2 15.9 %all-to-all-start = ((bf16[32,4,768]{2,1,0:T(4,128)(2,1)}), bf16[32,4,768]{2,1,0:T(4,128)(2,1)S(1)}, u32[]{:S(2)}, u32[]{:S(2)}) async-start(bf16[32,4,768]{2,1,0:T(4,128)(2,1)} %shard_map.82), calls=%async_computation | async-start | bytes 393216 | tf_op jit(solution)/shard_map/all_to_all | solution.py:42
  14.0 11.9 %collective-permute-start.1 = (bf16[208,768]{1,0:T(8,128)(2,1)}, bf16[208,768]{1,0:T(8,128)(2,1)}, u32[]{:S(2)}, u32[]{:S(2)}) collective-permute-start(bf16[208,768]{1,0:T(8,128)(2,1)} %get-tuple-element.15.refs_0_), channel_id=1, source_target_pairs={{0,2},{1,3},{2,0},{3,1},{4,6},{5,7},{6,4},{7,5},{8,10},{9,11},{10,... | collective-permute-start | bytes 958472 | tf_op jit(solution)/shard_map/ppermute | solution.py:170
  18.1 15.5 %copy-start = (bf16[1,512,768]{2,1,0:T(8,128)(2,1)S(1)}, bf16[1,512,768]{2,1,0:T(8,128)(2,1)}, u32[]{:S(2)}) copy-start(bf16[1,512,768]{2,1,0:T(8,128)(2,1)} %param.8) | copy-start | bytes 2359300
  23.0 10.6 %all-to-all-start.1 = ((bf16[32,4,768]{2,1,0:T(4,128)(2,1)}), bf16[32,4,768]{2,1,0:T(4,128)(2,1)S(1)}, u32[]{:S(2)}, u32[]{:S(2)}) async-start(bf16[32,4,768]{2,1,0:T(4,128)(2,1)} %shard_map.84.refs_4_), calls=%async_computation.1 | async-start | bytes 393216 | tf_op jit(solution)/shard_map/all_to_all | solution.py:42
  25.6 1.9 %collective-permute-start = (bf16[208,768]{1,0:T(8,128)(2,1)}, bf16[208,768]{1,0:T(8,128)(2,1)S(1)}, u32[]{:S(2)}, u32[]{:S(2)}) collective-permute-start(bf16[208,768]{1,0:T(8,128)(2,1)} %get-tuple-element.15.refs_0_), channel_id=1, source_target_pairs={{0,1},{1,0},{2,3},{3,2},{4,5},{5,4},{6,7},{7,6},{8,9},{9,8},{10,11... | collective-permute-start | bytes 958472 | tf_op jit(solution)/shard_map/ppermute | solution.py:170
  25.8 2.1 %collective-permute-start.2 = (bf16[208,768]{1,0:T(8,128)(2,1)}, bf16[208,768]{1,0:T(8,128)(2,1)S(1)}, u32[]{:S(2)}, u32[]{:S(2)}) collective-permute-start(bf16[208,768]{1,0:T(8,128)(2,1)} %collective-permute-done.1.refs_2_), channel_id=1, source_target_pairs={{0,1},{1,0},{2,3},{3,2},{4,5},{5,4},{6,7},{7,6},{8,9},{9,8},{10,11... | collective-permute-start | bytes 958472 | tf_op jit(solution)/shard_map/ppermute | solution.py:170

commit v10 on v8

--- a/solution.py
+++ b/solution.py
@@ -125,6 +125,10 @@
     slot_grad = [got_ref[order.index(at)].astype(jnp.float32) for at in range(len(order))]
     slot_grad = jnp.concatenate(slot_grad, axis=0).astype(jnp.bfloat16)
     cross = dot_nt(sum_ref[...], slot_grad)
+    halves = math.gcd(tok_ref.shape[0] // chunk, 2)
+    half = tok_ref.shape[0] // halves
+    disp_cot = [dot_nt(tok_ref[pl.ds(at * half, half), :], slot_grad) for at in range(halves)]
+    disp_cot = jnp.concatenate(disp_cot, axis=0)
     row = lax.broadcasted_iota(jnp.int32, (slots, slots), 0)
     col = lax.broadcasted_iota(jnp.int32, (slots, slots), 1)
     slot_dots = jnp.sum(jnp.where(row == col, cross, 0.0), axis=0, keepdims=True)
@@ -133,8 +137,7 @@
     for step in range(tok_ref.shape[0] // chunk):
         part = pl.ds(step * chunk, chunk)
         dispatch = disp_ref[part, :]
-        disp_cot = dot_nt(tok_ref[part, :], slot_grad)
-        logit_grad = comb_ref[part, :] + dispatch * (disp_cot - slot_dots)
+        logit_grad = comb_ref[part, :] + dispatch * (disp_cot[part.start : part.start + chunk] - slot_dots)
         weights = jnp.concatenate([dispatch, logit_grad], axis=1).astype(jnp.bfloat16)
         stage[part, :] = dot_nn(weights, both_rows).astype(jnp.bfloat16)
         copy = pltpu.make_async_copy(stage.at[part, :], out_hbm.at[part, :], sems.at[step])

time: 35.4 us -> 35.2 us (level)
  no operation moved by 1% of the time
where the time goes in v10:
time: 35.2 us; the launch traced here: 34.9 us
  Pallas kernels  14.5 us (41%)
  starting transfers between devices  12.3 us (35%)
  waiting for transfers between devices  8.01 us (23%)
    all_to_all x2, starting transfers between devices, exchange(): lax.all_to_all(blocks, BOTH, split_axis=0, concat_axis=0, axis_index_grou...  9.9 us
    all_to_all x2, waiting for transfers between devices, exchange(): lax.all_to_all(blocks, BOTH, split_axis=0, concat_axis=0, axis_index_grou...  6.24 us
    pallas_call x1, Pallas kernels, on_device(): pl.pallas_call(functools.partial(expert_kernel, there, back, clip_count,...  4.69 us
    pallas_call x1, Pallas kernels, on_device(): pl.pallas_call(functools.partial(side_kernel, parts), out_shape=(jax.Shap...  4.28 us
    ppermute x3, starting transfers between devices, swap(): return lax.ppermute(value, 'seq', [(i, i ^ bit) for i in range(count)])  2.41 us
    pallas_call x1, Pallas kernels, on_device(): pl.pallas_call(functools.partial(cot_kernel, there), out_shape=jax.ShapeD...  2.21 us
    pallas_call x1, Pallas kernels, on_device(): pl.pallas_call(functools.partial(weight_kernel, seq_count), out_shape=(ja...  1.91 us
    ppermute x3, waiting for transfers between devices, swap(): return lax.ppermute(value, 'seq', [(i, i ^ bit) for i in range(count)])  1.77 us
  transfers between devices with their start and end apart: 5, of which 4 were waited for; matrix products, arithmetic and copies ran while one was open for 0% of the time, Pallas kernels for 31%

profile of v10, /device:TPU:0, one launch (start us, length us, event | category | flops | bytes accessed | tf_op | source)
XLA Modules:
  0.0 34.9 jit_solution(12128814859019782016)
XLA Ops:
  0.0 2.2 %shard_map.82 = bf16[32,4,768]{2,1,0:T(4,128)(2,1)} custom-call(bf16[512,128]{1,0:T(8,128)(2,1)} %bitcast.17, bf16[512,768]{1,0:T(8,128)(2,1)} %bitcast.15), custom_call_target="tpu_custom_call" | custom-call | tf_op jit(solution)/shard_map/pallas_call | solution.py:293
  2.2 7.3 %all-to-all-start = ((bf16[32,4,768]{2,1,0:T(4,128)(2,1)}), bf16[32,4,768]{2,1,0:T(4,128)(2,1)S(1)}, u32[]{:S(2)}, u32[]{:S(2)}) async-start(bf16[32,4,768]{2,1,0:T(4,128)(2,1)} %shard_map.82), calls=%async_computation | async-start | bytes 393216 | tf_op jit(solution)/shard_map/all_to_all | solution.py:42
  9.5 4.3 %shard_map.83 = (bf16[208,768]{1,0:T(8,128)(2,1)}, bf16[32,3072]{1,0:T(8,128)(2,1)S(1)}, bf16[1536,768]{1,0:T(8,128)(2,1)S(1)}) custom-call(bf16[512,128]{1,0:T(8,128)(2,1)} %bitcast.18, bf16[512,768]{1,0:T(8,128)(2,1)} %bitcast.9, bf16[32,768]{1,0:T(8,128)(2,1)} %bitcast.20, bf16[32,768]{1,0:T(8,128)(2,1)} %bitcast.21, bf16[8,4,768]{2,1,0:T(4,128)(2,1)} %feed_hbm.1, ...), custom_call_target="tpu_custom_call" | custom-call | tf_op jit(solution)/shard_map/pallas_call | solution.py:314
  13.8 1.8 %collective-permute-start.1 = (bf16[208,768]{1,0:T(8,128)(2,1)}, bf16[208,768]{1,0:T(8,128)(2,1)}, u32[]{:S(2)}, u32[]{:S(2)}) collective-permute-start(bf16[208,768]{1,0:T(8,128)(2,1)} %get-tuple-element.15.refs_0_), channel_id=1, source_target_pairs={{0,2},{1,3},{2,0},{3,1},{4,6},{5,7},{6,4},{7,5},{8,10},{9,11},{10,... | collective-permute-start | bytes 958472 | tf_op jit(solution)/shard_map/ppermute | solution.py:165
  15.7 2.5 %all-to-all-done.got_ref = bf16[32,4,768]{2,1,0:T(4,128)(2,1)S(1)} async-done(((bf16[32,4,768]{2,1,0:T(4,128)(2,1)}), bf16[32,4,768]{2,1,0:T(4,128)(2,1)S(1)}, u32[]{:S(2)}, u32[]{:S(2)}) %all-to-all-start) | async-done | bytes 196640 | tf_op jit(solution)/shard_map/all_to_all | solution.py:42
  18.1 0.0 copy-start
  18.1 4.7 %shard_map.84.refs_4_ = bf16[32,4,768]{2,1,0:T(4,128)(2,1)} custom-call(bf16[32,4,768]{2,1,0:T(4,128)(2,1)S(1)} %all-to-all-done.got_ref, bf16[1536,768]{1,0:T(8,128)(2,1)S(1)} %get-tuple-element.13.kept_ref, bf16[32,3072]{1,0:T(8,128)(2,1)S(1)} %get-tuple-element.14.slope_ref, bf16[768,3072]{1,0:T(8,128)(2,1)} %bitcast.12, bf16[3072,768]{1,0:T(8,128)(2,1)} %bitcast.14), custom_call_target="tpu_custom_call" | custom-call | flops 301989888 | bytes 9437184 | tf_op jit(solution)/shard_map/pallas_call | solution.py:343
  22.9 2.6 %all-to-all-start.1 = ((bf16[32,4,768]{2,1,0:T(4,128)(2,1)}), bf16[32,4,768]{2,1,0:T(4,128)(2,1)S(1)}, u32[]{:S(2)}, u32[]{:S(2)}) async-start(bf16[32,4,768]{2,1,0:T(4,128)(2,1)} %shard_map.84.refs_4_), calls=%async_computation.1 | async-start | bytes 393216 | tf_op jit(solution)/shard_map/all_to_all | solution.py:42
  25.5 0.2 collective-permute-start
  25.7 0.0 collective-permute-done.1.refs_2_
  25.7 0.3 collective-permute-start.2
  26.0 1.3 %collective-permute-done.refs_1_ = bf16[208,768]{1,0:T(8,128)(2,1)S(1)} collective-permute-done((bf16[208,768]{1,0:T(8,128)(2,1)}, bf16[208,768]{1,0:T(8,128)(2,1)S(1)}, u32[]{:S(2)}, u32[]{:S(2)}) %collective-permute-start) | collective-permute-done | bytes 319520 | tf_op jit(solution)/shard_map/ppermute | solution.py:165
  27.4 0.5 %collective-permute-done.2.refs_3_ = bf16[208,768]{1,0:T(8,128)(2,1)S(1)} collective-permute-done((bf16[208,768]{1,0:T(8,128)(2,1)}, bf16[208,768]{1,0:T(8,128)(2,1)S(1)}, u32[]{:S(2)}, u32[]{:S(2)}) %collective-permute-start.2) | collective-permute-done | bytes 319520 | tf_op jit(solution)/shard_map/ppermute | solution.py:165
  27.8 1.9 %shard_map.85 = (f32[512,128]{1,0:T(8,128)S(1)}, f32[512,128]{1,0:T(8,128)S(1)}, bf16[128,768]{1,0:T(8,128)(2,1)S(1)}, bf16[128,768]{1,0:T(8,128)(2,1)S(1)}) custom-call(s32[1]{0:T(128)} %bitcast.7.me_ref, bf16[512,128]{1,0:T(8,128)(2,1)} %bitcast.19, bf16[512,768]{1,0:T(8,128)(2,1)} %bitcast.16, bf16[208,768]{1,0:T(8,128)(2,1)} %get-tuple-element.15.refs_0_, ...), custom_call_target="tpu_custom_call" | custom-call | tf_op jit(solution)/shard_map/pallas_call | solution.py:373
  29.7 3.7 %all-to-all-done.1.got_ref = bf16[32,4,768]{2,1,0:T(4,128)(2,1)S(1)} async-done(((bf16[32,4,768]{2,1,0:T(4,128)(2,1)}), bf16[32,4,768]{2,1,0:T(4,128)(2,1)S(1)}, u32[]{:S(2)}, u32[]{:S(2)}) %all-to-all-start.1) | async-done | bytes 196640 | tf_op jit(solution)/shard_map/all_to_all | solution.py:42
  33.5 0.0 copy-done
  33.5 1.4 %shard_map.86 = bf16[512,768]{1,0:T(8,128)(2,1)} custom-call(bf16[512,768]{1,0:T(8,128)(2,1)S(1)} %bitcast.10, bf16[32,4,768]{2,1,0:T(4,128)(2,1)S(1)} %all-to-all-done.1.got_ref, bf16[128,768]{1,0:T(8,128)(2,1)S(1)} %get-tuple-element.17.sum_ref, f32[512,128]{1,0:T(8,128)S(1)} %get-tuple-element.18.disp_ref, f32[512,128]{1,0:T(8,128)S(1)} %get-tuple-element.19.comb_ref, ...), custom_call_target="tpu_custom_call" | custom-call | flops 301989888 | bytes 1572864 | tf_op jit(solution)/shard_map/pallas_call | solution.py:403
Async XLA Ops:
  2.2 15.9 %all-to-all-start = ((bf16[32,4,768]{2,1,0:T(4,128)(2,1)}), bf16[32,4,768]{2,1,0:T(4,128)(2,1)S(1)}, u32[]{:S(2)}, u32[]{:S(2)}) async-start(bf16[32,4,768]{2,1,0:T(4,128)(2,1)} %shard_map.82), calls=%async_computation | async-start | bytes 393216 | tf_op jit(solution)/shard_map/all_to_all | solution.py:42
  13.8 11.9 %collective-permute-start.1 = (bf16[208,768]{1,0:T(8,128)(2,1)}, bf16[208,768]{1,0:T(8,128)(2,1)}, u32[]{:S(2)}, u32[]{:S(2)}) collective-permute-start(bf16[208,768]{1,0:T(8,128)(2,1)} %get-tuple-element.15.refs_0_), channel_id=1, source_target_pairs={{0,2},{1,3},{2,0},{3,1},{4,6},{5,7},{6,4},{7,5},{8,10},{9,11},{10,... | collective-permute-start | bytes 958472 | tf_op jit(solution)/shard_map/ppermute | solution.py:165
  18.1 15.3 %copy-start = (bf16[1,512,768]{2,1,0:T(8,128)(2,1)S(1)}, bf16[1,512,768]{2,1,0:T(8,128)(2,1)}, u32[]{:S(2)}) copy-start(bf16[1,512,768]{2,1,0:T(8,128)(2,1)} %param.8) | copy-start | bytes 2359300
  22.9 10.6 %all-to-all-start.1 = ((bf16[32,4,768]{2,1,0:T(4,128)(2,1)}), bf16[32,4,768]{2,1,0:T(4,128)(2,1)S(1)}, u32[]{:S(2)}, u32[]{:S(2)}) async-start(bf16[32,4,768]{2,1,0:T(4,128)(2,1)} %shard_map.84.refs_4_), calls=%async_computation.1 | async-start | bytes 393216 | tf_op jit(solution)/shard_map/all_to_all | solution.py:42
  25.5 1.9 %collective-permute-start = (bf16[208,768]{1,0:T(8,128)(2,1)}, bf16[208,768]{1,0:T(8,128)(2,1)S(1)}, u32[]{:S(2)}, u32[]{:S(2)}) collective-permute-start(bf16[208,768]{1,0:T(8,128)(2,1)} %get-tuple-element.15.refs_0_), channel_id=1, source_target_pairs={{0,1},{1,0},{2,3},{3,2},{4,5},{5,4},{6,7},{7,6},{8,9},{9,8},{10,11... | collective-permute-start | bytes 958472 | tf_op jit(solution)/shard_map/ppermute | solution.py:165
  25.7 2.1 %collective-permute-start.2 = (bf16[208,768]{1,0:T(8,128)(2,1)}, bf16[208,768]{1,0:T(8,128)(2,1)S(1)}, u32[]{:S(2)}, u32[]{:S(2)}) collective-permute-start(bf16[208,768]{1,0:T(8,128)(2,1)} %collective-permute-done.1.refs_2_), channel_id=1, source_target_pairs={{0,1},{1,0},{2,3},{3,2},{4,5},{5,4},{6,7},{7,6},{8,9},{9,8},{10,11... | collective-permute-start | bytes 958472 | tf_op jit(solution)/shard_map/ppermute | solution.py:165

commit v11 on v10

--- a/solution.py
+++ b/solution.py
@@ -305,7 +305,7 @@
     )(still_logits, still_grad)
     received = exchange(blocks, there)
 
-    parts = math.gcd(hid // GROUP, 4)
+    parts = math.gcd(hid // GROUP, 3)
     seq_slots = slot_params.shape[1]
     pack_rows = slot_total + 2 * seq_slots + stat_rows(slot_total, width)
     pieces = math.gcd(hid // GROUP, 6)

time: 35.2 us -> 35.2 us (level)
  no operation moved by 1% of the time
where the time goes in v11:
time: 35.2 us; the launch traced here: 34.9 us
  Pallas kernels  14.5 us (41%)
  starting transfers between devices  12.3 us (35%)
  waiting for transfers between devices  8.03 us (23%)
    all_to_all x2, starting transfers between devices, exchange(): lax.all_to_all(blocks, BOTH, split_axis=0, concat_axis=0, axis_index_grou...  9.9 us
    all_to_all x2, waiting for transfers between devices, exchange(): lax.all_to_all(blocks, BOTH, split_axis=0, concat_axis=0, axis_index_grou...  6.26 us
    pallas_call x1, Pallas kernels, on_device(): pl.pallas_call(functools.partial(expert_kernel, there, back, clip_count,...  4.69 us
    pallas_call x1, Pallas kernels, on_device(): pl.pallas_call(functools.partial(side_kernel, parts), out_shape=(jax.Shap...  4.27 us
    ppermute x3, starting transfers between devices, swap(): return lax.ppermute(value, 'seq', [(i, i ^ bit) for i in range(count)])  2.41 us
    pallas_call x1, Pallas kernels, on_device(): pl.pallas_call(functools.partial(cot_kernel, there), out_shape=jax.ShapeD...  2.21 us
    pallas_call x1, Pallas kernels, on_device(): pl.pallas_call(functools.partial(weight_kernel, seq_count), out_shape=(ja...  1.91 us
    ppermute x3, waiting for transfers between devices, swap(): return lax.ppermute(value, 'seq', [(i, i ^ bit) for i in range(count)])  1.77 us
  transfers between devices with their start and end apart: 5, of which 4 were waited for; matrix products, arithmetic and copies ran while one was open for 0% of the time, Pallas kernels for 31%

profile of v11, /device:TPU:0, one launch (start us, length us, event | category | flops | bytes accessed | tf_op | source)
XLA Modules:
  0.0 34.9 jit_solution(6227702972433061921)
XLA Ops:
  0.0 2.2 %shard_map.82 = bf16[32,4,768]{2,1,0:T(4,128)(2,1)} custom-call(bf16[512,128]{1,0:T(8,128)(2,1)} %bitcast.17, bf16[512,768]{1,0:T(8,128)(2,1)} %bitcast.15), custom_call_target="tpu_custom_call" | custom-call | tf_op jit(solution)/shard_map/pallas_call | solution.py:293
  2.2 7.3 %all-to-all-start = ((bf16[32,4,768]{2,1,0:T(4,128)(2,1)}), bf16[32,4,768]{2,1,0:T(4,128)(2,1)S(1)}, u32[]{:S(2)}, u32[]{:S(2)}) async-start(bf16[32,4,768]{2,1,0:T(4,128)(2,1)} %shard_map.82), calls=%async_computation | async-start | bytes 393216 | tf_op jit(solution)/shard_map/all_to_all | solution.py:42
  9.5 4.3 %shard_map.83 = (bf16[208,768]{1,0:T(8,128)(2,1)}, bf16[32,3072]{1,0:T(8,128)(2,1)S(1)}, bf16[1536,768]{1,0:T(8,128)(2,1)S(1)}) custom-call(bf16[512,128]{1,0:T(8,128)(2,1)} %bitcast.18, bf16[512,768]{1,0:T(8,128)(2,1)} %bitcast.9, bf16[32,768]{1,0:T(8,128)(2,1)} %bitcast.20, bf16[32,768]{1,0:T(8,128)(2,1)} %bitcast.21, bf16[8,4,768]{2,1,0:T(4,128)(2,1)} %feed_hbm.1, ...), custom_call_target="tpu_custom_call" | custom-call | tf_op jit(solution)/shard_map/pallas_call | solution.py:314
  13.8 1.8 %collective-permute-start.1 = (bf16[208,768]{1,0:T(8,128)(2,1)}, bf16[208,768]{1,0:T(8,128)(2,1)}, u32[]{:S(2)}, u32[]{:S(2)}) collective-permute-start(bf16[208,768]{1,0:T(8,128)(2,1)} %get-tuple-element.15.refs_0_), channel_id=1, source_target_pairs={{0,2},{1,3},{2,0},{3,1},{4,6},{5,7},{6,4},{7,5},{8,10},{9,11},{10,... | collective-permute-start | bytes 958472 | tf_op jit(solution)/shard_map/ppermute | solution.py:165
  15.6 2.5 %all-to-all-done.got_ref = bf16[32,4,768]{2,1,0:T(4,128)(2,1)S(1)} async-done(((bf16[32,4,768]{2,1,0:T(4,128)(2,1)}), bf16[32,4,768]{2,1,0:T(4,128)(2,1)S(1)}, u32[]{:S(2)}, u32[]{:S(2)}) %all-to-all-start) | async-done | bytes 196640 | tf_op jit(solution)/shard_map/all_to_all | solution.py:42
  18.1 0.0 copy-start
  18.1 4.7 %shard_map.84.refs_4_ = bf16[32,4,768]{2,1,0:T(4,128)(2,1)} custom-call(bf16[32,4,768]{2,1,0:T(4,128)(2,1)S(1)} %all-to-all-done.got_ref, bf16[1536,768]{1,0:T(8,128)(2,1)S(1)} %get-tuple-element.13.kept_ref, bf16[32,3072]{1,0:T(8,128)(2,1)S(1)} %get-tuple-element.14.slope_ref, bf16[768,3072]{1,0:T(8,128)(2,1)} %bitcast.12, bf16[3072,768]{1,0:T(8,128)(2,1)} %bitcast.14), custom_call_target="tpu_custom_call" | custom-call | flops 301989888 | bytes 9437184 | tf_op jit(solution)/shard_map/pallas_call | solution.py:343
  22.9 2.6 %all-to-all-start.1 = ((bf16[32,4,768]{2,1,0:T(4,128)(2,1)}), bf16[32,4,768]{2,1,0:T(4,128)(2,1)S(1)}, u32[]{:S(2)}, u32[]{:S(2)}) async-start(bf16[32,4,768]{2,1,0:T(4,128)(2,1)} %shard_map.84.refs_4_), calls=%async_computation.1 | async-start | bytes 393216 | tf_op jit(solution)/shard_map/all_to_all | solution.py:42
  25.5 0.2 collective-permute-start
  25.7 0.0 collective-permute-done.1.refs_2_
  25.7 0.3 collective-permute-start.2
  26.0 1.3 %collective-permute-done.refs_1_ = bf16[208,768]{1,0:T(8,128)(2,1)S(1)} collective-permute-done((bf16[208,768]{1,0:T(8,128)(2,1)}, bf16[208,768]{1,0:T(8,128)(2,1)S(1)}, u32[]{:S(2)}, u32[]{:S(2)}) %collective-permute-start) | collective-permute-done | bytes 319520 | tf_op jit(solution)/shard_map/ppermute | solution.py:165
  27.4 0.5 %collective-permute-done.2.refs_3_ = bf16[208,768]{1,0:T(8,128)(2,1)S(1)} collective-permute-done((bf16[208,768]{1,0:T(8,128)(2,1)}, bf16[208,768]{1,0:T(8,128)(2,1)S(1)}, u32[]{:S(2)}, u32[]{:S(2)}) %collective-permute-start.2) | collective-permute-done | bytes 319520 | tf_op jit(solution)/shard_map/ppermute | solution.py:165
  27.8 1.9 %shard_map.85 = (f32[512,128]{1,0:T(8,128)S(1)}, f32[512,128]{1,0:T(8,128)S(1)}, bf16[128,768]{1,0:T(8,128)(2,1)S(1)}, bf16[128,768]{1,0:T(8,128)(2,1)S(1)}) custom-call(s32[1]{0:T(128)} %bitcast.7.me_ref, bf16[512,128]{1,0:T(8,128)(2,1)} %bitcast.19, bf16[512,768]{1,0:T(8,128)(2,1)} %bitcast.16, bf16[208,768]{1,0:T(8,128)(2,1)} %get-tuple-element.15.refs_0_, ...), custom_call_target="tpu_custom_call" | custom-call | tf_op jit(solution)/shard_map/pallas_call | solution.py:373
  29.7 3.7 %all-to-all-done.1.got_ref = bf16[32,4,768]{2,1,0:T(4,128)(2,1)S(1)} async-done(((bf16[32,4,768]{2,1,0:T(4,128)(2,1)}), bf16[32,4,768]{2,1,0:T(4,128)(2,1)S(1)}, u32[]{:S(2)}, u32[]{:S(2)}) %all-to-all-start.1) | async-done | bytes 196640 | tf_op jit(solution)/shard_map/all_to_all | solution.py:42
  33.5 0.0 copy-done
  33.5 1.4 %shard_map.86 = bf16[512,768]{1,0:T(8,128)(2,1)} custom-call(bf16[512,768]{1,0:T(8,128)(2,1)S(1)} %bitcast.10, bf16[32,4,768]{2,1,0:T(4,128)(2,1)S(1)} %all-to-all-done.1.got_ref, bf16[128,768]{1,0:T(8,128)(2,1)S(1)} %get-tuple-element.17.sum_ref, f32[512,128]{1,0:T(8,128)S(1)} %get-tuple-element.18.disp_ref, f32[512,128]{1,0:T(8,128)S(1)} %get-tuple-element.19.comb_ref, ...), custom_call_target="tpu_custom_call" | custom-call | flops 301989888 | bytes 1572864 | tf_op jit(solution)/shard_map/pallas_call | solution.py:403
Async XLA Ops:
  2.2 15.9 %all-to-all-start = ((bf16[32,4,768]{2,1,0:T(4,128)(2,1)}), bf16[32,4,768]{2,1,0:T(4,128)(2,1)S(1)}, u32[]{:S(2)}, u32[]{:S(2)}) async-start(bf16[32,4,768]{2,1,0:T(4,128)(2,1)} %shard_map.82), calls=%async_computation | async-start | bytes 393216 | tf_op jit(solution)/shard_map/all_to_all | solution.py:42
  13.8 11.9 %collective-permute-start.1 = (bf16[208,768]{1,0:T(8,128)(2,1)}, bf16[208,768]{1,0:T(8,128)(2,1)}, u32[]{:S(2)}, u32[]{:S(2)}) collective-permute-start(bf16[208,768]{1,0:T(8,128)(2,1)} %get-tuple-element.15.refs_0_), channel_id=1, source_target_pairs={{0,2},{1,3},{2,0},{3,1},{4,6},{5,7},{6,4},{7,5},{8,10},{9,11},{10,... | collective-permute-start | bytes 958472 | tf_op jit(solution)/shard_map/ppermute | solution.py:165
  18.1 15.3 %copy-start = (bf16[1,512,768]{2,1,0:T(8,128)(2,1)S(1)}, bf16[1,512,768]{2,1,0:T(8,128)(2,1)}, u32[]{:S(2)}) copy-start(bf16[1,512,768]{2,1,0:T(8,128)(2,1)} %param.8) | copy-start | bytes 2359300
  22.9 10.6 %all-to-all-start.1 = ((bf16[32,4,768]{2,1,0:T(4,128)(2,1)}), bf16[32,4,768]{2,1,0:T(4,128)(2,1)S(1)}, u32[]{:S(2)}, u32[]{:S(2)}) async-start(bf16[32,4,768]{2,1,0:T(4,128)(2,1)} %shard_map.84.refs_4_), calls=%async_computation.1 | async-start | bytes 393216 | tf_op jit(solution)/shard_map/all_to_all | solution.py:42
  25.5 1.9 %collective-permute-start = (bf16[208,768]{1,0:T(8,128)(2,1)}, bf16[208,768]{1,0:T(8,128)(2,1)S(1)}, u32[]{:S(2)}, u32[]{:S(2)}) collective-permute-start(bf16[208,768]{1,0:T(8,128)(2,1)} %get-tuple-element.15.refs_0_), channel_id=1, source_target_pairs={{0,1},{1,0},{2,3},{3,2},{4,5},{5,4},{6,7},{7,6},{8,9},{9,8},{10,11... | collective-permute-start | bytes 958472 | tf_op jit(solution)/shard_map/ppermute | solution.py:165
  25.7 2.1 %collective-permute-start.2 = (bf16[208,768]{1,0:T(8,128)(2,1)}, bf16[208,768]{1,0:T(8,128)(2,1)S(1)}, u32[]{:S(2)}, u32[]{:S(2)}) collective-permute-start(bf16[208,768]{1,0:T(8,128)(2,1)} %collective-permute-done.1.refs_2_), channel_id=1, source_target_pairs={{0,1},{1,0},{2,3},{3,2},{4,5},{5,4},{6,7},{7,6},{8,9},{9,8},{10,11... | collective-permute-start | bytes 958472 | tf_op jit(solution)/shard_map/ppermute | solution.py:165
